TPU v7x, 32 devices: a whole 2x2x4 slice. The times are simulated.
32 devices in a mesh: rows: 4 (over y, core), band: 8 (over z, x).
Axes of the slice: x: 2, y: 2, z: 4, core: 2. Of those that a mesh axis runs over, the one named last changes fastest.
Arguments:
- patches: bfloat16 [24, 256, 3072], P('rows', None, 'band'), may hold values from -6 to 6
- condition_table: bfloat16 [64, 384], replicated, may hold values from -6 to 6
- condition_index: int32 [24, 8], P('rows'), may hold values from 0 to 63
- image_lengths: int32 [24, 8], P('rows'), may hold values from 0 to 1024, as said below
- modulate_weight: bfloat16 [384, 2304], replicated, may hold values from -0.3125 to 0.3125
- modulate_bias: bfloat16 [2304], replicated, may hold values from -3 to 3
- triple_weight: bfloat16 [384, 1152], replicated, may hold values from -0.3125 to 0.3125
- query_bias: bfloat16 [384], replicated, may hold values from -3 to 3
- value_bias: bfloat16 [384], replicated, may hold values from -3 to 3
- mixer_weight: bfloat16 [384, 384], replicated, may hold values from -3.5 to 3.5
- mixer_bias: bfloat16 [384], replicated, may hold values from -3 to 3
- hidden_weight: bfloat16 [384, 1536], replicated, may hold values from -0.3125 to 0.3125
- hidden_bias: bfloat16 [1536], replicated, may hold values from -3 to 3
- output_weight: bfloat16 [1536, 384], replicated, may hold values from -0.15625 to 0.15625
- output_bias: bfloat16 [384], replicated, may hold values from -3 to 3
- cotangent: bfloat16 [24, 256, 3072], P('rows', None, 'band'), may hold values from -6 to 6
Outputs:
- block_out: bfloat16 [24, 256, 3072], P('rows', None, 'band')
- patch_grad: float32 [24, 256, 3072], P('rows', None, 'band')
- modulate_weight_grad: float32 [384, 2304], replicated
- modulate_bias_grad: float32 [2304], replicated
- triple_weight_grad: float32 [384, 1152], replicated
- query_bias_grad: float32 [384], replicated
- value_bias_grad: float32 [384], replicated
- mixer_weight_grad: float32 [384, 384], replicated
- mixer_bias_grad: float32 [384], replicated
- hidden_weight_grad: float32 [384, 1536], replicated
- hidden_bias_grad: float32 [1536], replicated
- output_weight_grad: float32 [1536, 384], replicated
- output_bias_grad: float32 [384], replicated
Inputs may be any that keep to these rules, and one draw needn't show every extreme that they name: `image_lengths`: in each row the nonzero lengths are 1024 or 256 and add up to 2048; they fill the first slots, the remaining slots of the 8 are zero.
All inputs are finite; a program needn't handle non-finite values.
Results may differ from a plain program's by a relative error of at most 0.014.
The roundings to bfloat16 on the way count: a program that leaves them out, or rounds other values in their place, can miss the bound.
Values may be sent and summed in bfloat16 or wider, within the bound.
No kernel may reach another device: no remote copies, remote signals or barrier semaphores. Data moves between devices by JAX's collectives and lax.ppermute only.
A program may use at most 128 MiB of HBM per device.

v0:
```python
from functools import partial

import jax
import jax.numpy as jnp
from jax import lax
from jax.sharding import PartitionSpec as P

HEADS = 6
HEAD_DIM = 64


EPSILON = 1e-06
HIGHEST = lax.Precision.HIGHEST


def layer_norm(values):
    centre = values - jnp.mean(values, axis=-1, keepdims=True)
    inverse = lax.rsqrt(jnp.mean(centre * centre, axis=-1, keepdims=True) + EPSILON)
    return (centre * inverse, inverse)


def norm_back(grad, normed, inverse):
    return inverse * (
        grad
        - jnp.mean(grad, axis=-1, keepdims=True)
        - normed * jnp.mean(grad * normed, axis=-1, keepdims=True)
    )


def contract_rows(left, right):
    return lax.dot_general(
        left, right, (((0,), (0,)), ((), ())), preferred_element_type=jnp.float32
    )


def times_transpose(left, right):
    return lax.dot_general(
        left, right, (((1,), (1,)), ((), ())), preferred_element_type=jnp.float32
    )


def body(
    patches,
    condition_table,
    condition_index,
    image_lengths,
    modulate_weight,
    modulate_bias,
    triple_weight,
    query_bias,
    value_bias,
    mixer_weight,
    mixer_bias,
    hidden_weight,
    hidden_bias,
    output_weight,
    output_bias,
    cotangent,
):
    band_index = lax.axis_index("band")
    band_count = lax.axis_size("band")
    row_count, band_length, width = patches.shape
    full_length = band_length * band_count
    slot_count = image_lengths.shape[1]
    scale = HEAD_DIM ** (-0.5)
    query_plus = query_bias.astype(jnp.float32)
    value_plus = value_bias.astype(jnp.float32)
    mixer_plus = mixer_bias.astype(jnp.float32)
    hidden_plus = hidden_bias.astype(jnp.float32)
    output_plus = output_bias.astype(jnp.float32)
    own_positions = jnp.arange(band_length, dtype=jnp.int32) * band_count + band_index
    key_order = jnp.arange(full_length, dtype=jnp.int32)
    key_positions = key_order % band_length * band_count + key_order // band_length
    image_ends = jnp.cumsum(image_lengths, axis=1)
    own_segment = jnp.sum(
        (own_positions[None, :, None] >= image_ends[:, None, :]).astype(jnp.int32), axis=2
    )
    key_segment = jnp.sum(
        (key_positions[None, :, None] >= image_ends[:, None, :]).astype(jnp.int32), axis=2
    )
    slot_ids = jnp.arange(slot_count, dtype=jnp.int32)
    own_onehot = (own_segment[:, :, None] == slot_ids).astype(jnp.float32)
    choose = (
        condition_index[:, :, None] == jnp.arange(condition_table.shape[0], dtype=jnp.int32)
    ).astype(jnp.bfloat16)
    condition = jnp.einsum(
        "rsn,nd->rsd", choose, condition_table, preferred_element_type=jnp.float32
    )
    activity = jax.nn.silu(condition).astype(jnp.bfloat16)
    modulation = jnp.einsum(
        "rsd,de->rse", activity, modulate_weight, preferred_element_type=jnp.float32
    ) + modulate_bias.astype(jnp.float32)
    patch_mods = jnp.einsum("rts,rse->rte", own_onehot, modulation, precision=HIGHEST)

    def probabilities(query, key_all, mask):
        query_heads = query.reshape(-1, HEADS, HEAD_DIM)
        key_heads = key_all.reshape(-1, HEADS, HEAD_DIM)
        scores = (
            jnp.einsum("qhd,khd->hqk", query_heads, key_heads, preferred_element_type=jnp.float32)
            * scale
        )
        scores = jnp.where(mask[None], scores, -1e30)
        maxima = jnp.max(scores, axis=2, keepdims=True)
        exps = jnp.exp(scores - maxima)
        sums = jnp.sum(exps, axis=2, keepdims=True)
        return (exps / sums, maxima + jnp.log(sums))

    def forward_row(row_patch, row_mods, own_seg, key_seg, fetch):
        source = row_patch.astype(jnp.float32)
        shift_one, scale_one, gate_one, shift_two, scale_two, gate_two = jnp.split(
            row_mods, 6, axis=1
        )
        normed_in, inverse_in = layer_norm(source)
        hidden_in = (normed_in * (1.0 + scale_one) + shift_one).astype(jnp.bfloat16)
        triple = jnp.dot(hidden_in, triple_weight, preferred_element_type=jnp.float32)
        query = (triple[:, :width] + query_plus).astype(jnp.bfloat16)
        keys = triple[:, width : 2 * width].astype(jnp.bfloat16)
        values = (triple[:, 2 * width :] + value_plus).astype(jnp.bfloat16)
        key_all, value_all = fetch(keys, values)
        mask = own_seg[:, None] == key_seg[None, :]
        probs, log_total = probabilities(query, key_all, mask)
        mixed = (
            jnp.einsum(
                "hqk,khd->qhd",
                probs.astype(jnp.bfloat16),
                value_all.reshape(-1, HEADS, HEAD_DIM),
                preferred_element_type=jnp.float32,
            )
            .reshape(-1, width)
            .astype(jnp.bfloat16)
        )
        branch = jnp.dot(mixed, mixer_weight, preferred_element_type=jnp.float32) + mixer_plus
        middle = source + gate_one * branch
        normed_mid, inverse_mid = layer_norm(middle)
        hidden_mid = (normed_mid * (1.0 + scale_two) + shift_two).astype(jnp.bfloat16)
        hidden = (
            jnp.dot(hidden_mid, hidden_weight, preferred_element_type=jnp.float32) + hidden_plus
        )
        active = jax.nn.gelu(hidden, approximate=True).astype(jnp.bfloat16)
        output = jnp.dot(active, output_weight, preferred_element_type=jnp.float32) + output_plus
        result = middle + gate_two * output
        return (
            normed_in,
            inverse_in,
            hidden_in,
            query,
            keys,
            values,
            key_all,
            value_all,
            probs,
            log_total,
            mixed,
            branch,
            normed_mid,
            inverse_mid,
            hidden_mid,
            hidden,
            active,
            output,
            result,
        )

    def gather_forward(keys, values):
        return (
            lax.all_gather(keys, "band", axis=0, tiled=True),
            lax.all_gather(values, "band", axis=0, tiled=True),
        )

    def forward_step(carry, row_items):
        row_patch, row_mods, own_seg, key_seg = row_items
        state = forward_row(row_patch, row_mods, own_seg, key_seg, gather_forward)
        return (carry, (state[18].astype(jnp.bfloat16),))

    forward_out = lax.scan(
        forward_step, jnp.zeros((), jnp.float32), (patches, patch_mods, own_segment, key_segment)
    )[1]
    block_out = forward_out[0]

    def gather_again(keys, values):
        return (
            lax.all_gather(keys, "band", axis=0, tiled=True),
            lax.all_gather(values, "band", axis=0, tiled=True),
        )

    def backward_step(totals, row_items):
        row_patch, row_mods, own_seg, key_seg, row_cot, own_hot = row_items
        (
            normed_in,
            inverse_in,
            hidden_in,
            query,
            keys,
            values,
            key_all,
            value_all,
            probs,
            log_total,
            mixed,
            branch,
            normed_mid,
            inverse_mid,
            hidden_mid,
            hidden,
            active,
            output,
            result,
        ) = forward_row(row_patch, row_mods, own_seg, key_seg, gather_again)
        shift_one, scale_one, gate_one, shift_two, scale_two, gate_two = jnp.split(
            row_mods, 6, axis=1
        )
        grad_out = row_cot.astype(jnp.float32)
        output_grad = (gate_two * grad_out).astype(jnp.bfloat16)
        gate_two_grad = grad_out * output
        output_w_grad = contract_rows(active, output_grad)
        output_b_grad = jnp.sum(output_grad.astype(jnp.float32), axis=0)
        active_grad = times_transpose(output_grad, output_weight)
        gelu_pull = jax.vjp(partial(jax.nn.gelu, approximate=True), hidden)[1]
        hidden_grad = gelu_pull(active_grad)[0].astype(jnp.bfloat16)
        hidden_w_grad = contract_rows(hidden_mid, hidden_grad)
        hidden_b_grad = jnp.sum(hidden_grad.astype(jnp.float32), axis=0)
        mid_grad = times_transpose(hidden_grad, hidden_weight)
        scale_two_grad = mid_grad * normed_mid
        middle_grad = grad_out + norm_back(mid_grad * (1.0 + scale_two), normed_mid, inverse_mid)
        gate_one_grad = middle_grad * branch
        branch_grad = (gate_one * middle_grad).astype(jnp.bfloat16)
        mixer_w_grad = contract_rows(mixed, branch_grad)
        mixer_b_grad = jnp.sum(branch_grad.astype(jnp.float32), axis=0)
        mixed_grad = times_transpose(branch_grad, mixer_weight).astype(jnp.bfloat16)
        grad_heads = mixed_grad.reshape(-1, HEADS, HEAD_DIM)
        query_heads = query.reshape(-1, HEADS, HEAD_DIM)
        key_heads_all = key_all.reshape(-1, HEADS, HEAD_DIM)
        value_heads_all = value_all.reshape(-1, HEADS, HEAD_DIM)
        prob_grad = jnp.einsum(
            "qhd,khd->hqk", grad_heads, value_heads_all, preferred_element_type=jnp.float32
        )
        deltas = jnp.sum(probs * prob_grad, axis=2, keepdims=True)
        score_grad = (probs * (prob_grad - deltas)).astype(jnp.bfloat16)
        query_grad = (
            (
                jnp.einsum(
                    "hqk,khd->qhd", score_grad, key_heads_all, preferred_element_type=jnp.float32
                )
                * scale
            )
            .reshape(-1, width)
            .astype(jnp.bfloat16)
        )
        key_term = (
            jnp.einsum("hqk,qhd->khd", score_grad, query_heads, preferred_element_type=jnp.float32)
            * scale
        ).reshape(-1, width)
        value_term = jnp.einsum(
            "hqk,qhd->khd",
            probs.astype(jnp.bfloat16),
            grad_heads,
            preferred_element_type=jnp.float32,
        ).reshape(-1, width)
        key_sum, value_sum = (
            lax.psum_scatter(
                key_term.astype(jnp.bfloat16), "band", scatter_dimension=0, tiled=True
            ).astype(jnp.float32),
            lax.psum_scatter(
                value_term.astype(jnp.bfloat16), "band", scatter_dimension=0, tiled=True
            ).astype(jnp.float32),
        )
        key_grad = key_sum.astype(jnp.bfloat16)
        value_grad = value_sum.astype(jnp.bfloat16)
        triple_grad = jnp.concatenate([query_grad, key_grad, value_grad], axis=1)
        triple_w_grad = contract_rows(hidden_in, triple_grad)
        query_b_grad = jnp.sum(query_grad.astype(jnp.float32), axis=0)
        value_b_grad = jnp.sum(value_grad.astype(jnp.float32), axis=0)
        in_grad = times_transpose(triple_grad, triple_weight)
        scale_one_grad = in_grad * normed_in
        patch_grad_row = middle_grad + norm_back(in_grad * (1.0 + scale_one), normed_in, inverse_in)
        mod_grad_rows = jnp.concatenate(
            [in_grad, scale_one_grad, gate_one_grad, mid_grad, scale_two_grad, gate_two_grad],
            axis=1,
        )
        slot_grad = jnp.einsum("ts,te->se", own_hot, mod_grad_rows, precision=HIGHEST)
        increments = (
            triple_w_grad,
            query_b_grad,
            value_b_grad,
            mixer_w_grad,
            mixer_b_grad,
            hidden_w_grad,
            hidden_b_grad,
            output_w_grad,
            output_b_grad,
        )
        totals = tuple((summed + addend for summed, addend in zip(totals, increments)))
        return (totals, (patch_grad_row, slot_grad))

    starting = (
        jnp.zeros(triple_weight.shape, jnp.float32),
        jnp.zeros(query_bias.shape, jnp.float32),
        jnp.zeros(value_bias.shape, jnp.float32),
        jnp.zeros(mixer_weight.shape, jnp.float32),
        jnp.zeros(mixer_bias.shape, jnp.float32),
        jnp.zeros(hidden_weight.shape, jnp.float32),
        jnp.zeros(hidden_bias.shape, jnp.float32),
        jnp.zeros(output_weight.shape, jnp.float32),
        jnp.zeros(output_bias.shape, jnp.float32),
    )
    back_items = (patches, patch_mods, own_segment, key_segment, cotangent, own_onehot)
    totals, (patch_grad, slot_grads) = lax.scan(backward_step, starting, back_items)
    modulate_w_grad = jnp.einsum(
        "rsd,rse->de", activity.astype(jnp.float32), slot_grads, precision=HIGHEST
    )
    modulate_b_grad = jnp.sum(slot_grads, axis=(0, 1))
    summed = lax.psum(
        (
            modulate_w_grad,
            modulate_b_grad,
            totals[0],
            totals[1],
            totals[2],
            totals[3],
            totals[4],
            totals[5],
            totals[6],
            totals[7],
            totals[8],
        ),
        ("rows", "band"),
    )
    return (
        block_out,
        patch_grad,
        summed[0],
        summed[1],
        summed[2],
        summed[3],
        summed[4],
        summed[5],
        summed[6],
        summed[7],
        summed[8],
        summed[9],
        summed[10],
    )


def solution(mesh):
    return jax.shard_map(
        body,
        mesh=mesh,
        in_specs=(
            P("rows", None, "band"),
            P(),
            P("rows", None),
            P("rows", None),
            P(),
            P(),
            P(),
            P(),
            P(),
            P(),
            P(),
            P(),
            P(),
            P(),
            P(),
            P("rows", None, "band"),
        ),
        out_specs=(
            P("rows", None, "band"),
            P("rows", None, "band"),
            P(),
            P(),
            P(),
            P(),
            P(),
            P(),
            P(),
            P(),
            P(),
            P(),
            P(),
        ),
        check_vma=False,
    )
```

profile of v0, /device:TPU:0, one launch (start us, length us, event | category | flops | bytes accessed | tf_op | source)
XLA Modules:
  0.0 2597.1 jit_solution(8583007620600934508)
XLA Ops:
  19.7 9.7 fusion.128
  29.5 1652.1 %while.44 = (s32[]{:T(128)}, f32[384,1152]{1,0:T(8,128)}, f32[384]{0:T(512)}, f32[384]{0:T(512)}, f32[384,384]{1,0:T(8,128)}, /*index=5*/f32[384]{0:T(512)}, f32...) while((s32[]{:T(128)}, f32[384,1152]{1,0:T(8,128)}, ...), condition=%wide.region_30.31_spmd.clone, body=%wide.region_11.30_spmd.clone.sunk | while | flops 5272670208 | bytes 313570656 | solution.py:307
  39.4 44.0 %all-gather.11.cloned.1.call-done = bf16[2048,384]{1,0:T(8,128)(2,1)} async-done(((bf16[256,384]{1,0:T(8,128)(2,1)}), bf16[2048,384]{1,0:T(8,128)(2,1)}) %all-gather.11.cloned.1.call-update) | async-done | bytes 1572880 | tf_op jit(solution)/shard_map/while/body/eval_jaxpr/all_gather | solution.py:182
  92.3 36.3 %all-gather.9.cloned.1.call-done = bf16[2048,384]{1,0:T(8,128)(2,1)} async-done(((bf16[256,384]{1,0:T(8,128)(2,1)}), bf16[2048,384]{1,0:T(8,128)(2,1)}) %all-gather.9.cloned.1.call-update) | async-done | bytes 1572880 | tf_op jit(solution)/shard_map/while/body/eval_jaxpr/all_gather | solution.py:183
  131.3 7.3 fusion.317
  189.3 36.0 %reduce-scatter.3.cloned.1.call-done = bf16[256,384]{0,1:T(8,128)(2,1)} async-done(((bf16[2048,384]{0,1:T(8,128)(2,1)}), bf16[256,384]{0,1:T(8,128)(2,1)}) %reduce-scatter.3.cloned.1.call-update) | async-done | bytes 196624 | tf_op jit(solution)/shard_map/while/body/eval_jaxpr/reduce_scatter | solution.py:263
  225.2 68.3 %reduce-scatter.5.cloned.1.call-done = bf16[256,384]{0,1:T(8,128)(2,1)} async-done(((bf16[2048,384]{0,1:T(8,128)(2,1)}), bf16[256,384]{0,1:T(8,128)(2,1)}) %reduce-scatter.5.cloned.1.call-update) | async-done | bytes 196624 | tf_op jit(solution)/shard_map/while/body/eval_jaxpr/reduce_scatter | solution.py:260
  316.4 40.2 %all-gather.11.cloned.1.call-done = bf16[2048,384]{1,0:T(8,128)(2,1)} async-done(((bf16[256,384]{1,0:T(8,128)(2,1)}), bf16[2048,384]{1,0:T(8,128)(2,1)}) %all-gather.11.cloned.1.call-update) | async-done | bytes 1572880 | tf_op jit(solution)/shard_map/while/body/eval_jaxpr/all_gather | solution.py:182
  365.6 36.2 %all-gather.9.cloned.1.call-done = bf16[2048,384]{1,0:T(8,128)(2,1)} async-done(((bf16[256,384]{1,0:T(8,128)(2,1)}), bf16[2048,384]{1,0:T(8,128)(2,1)}) %all-gather.9.cloned.1.call-update) | async-done | bytes 1572880 | tf_op jit(solution)/shard_map/while/body/eval_jaxpr/all_gather | solution.py:183
  466.2 32.2 %reduce-scatter.3.cloned.1.call-done = bf16[256,384]{0,1:T(8,128)(2,1)} async-done(((bf16[2048,384]{0,1:T(8,128)(2,1)}), bf16[256,384]{0,1:T(8,128)(2,1)}) %reduce-scatter.3.cloned.1.call-update) | async-done | bytes 196624 | tf_op jit(solution)/shard_map/while/body/eval_jaxpr/reduce_scatter | solution.py:263
  498.4 68.5 %reduce-scatter.5.cloned.1.call-done = bf16[256,384]{0,1:T(8,128)(2,1)} async-done(((bf16[2048,384]{0,1:T(8,128)(2,1)}), bf16[256,384]{0,1:T(8,128)(2,1)}) %reduce-scatter.5.cloned.1.call-update) | async-done | bytes 196624 | tf_op jit(solution)/shard_map/while/body/eval_jaxpr/reduce_scatter | solution.py:260
  589.8 40.3 %all-gather.11.cloned.1.call-done = bf16[2048,384]{1,0:T(8,128)(2,1)} async-done(((bf16[256,384]{1,0:T(8,128)(2,1)}), bf16[2048,384]{1,0:T(8,128)(2,1)}) %all-gather.11.cloned.1.call-update) | async-done | bytes 1572880 | tf_op jit(solution)/shard_map/while/body/eval_jaxpr/all_gather | solution.py:182
  638.9 36.2 %all-gather.9.cloned.1.call-done = bf16[2048,384]{1,0:T(8,128)(2,1)} async-done(((bf16[256,384]{1,0:T(8,128)(2,1)}), bf16[2048,384]{1,0:T(8,128)(2,1)}) %all-gather.9.cloned.1.call-update) | async-done | bytes 1572880 | tf_op jit(solution)/shard_map/while/body/eval_jaxpr/all_gather | solution.py:183
  739.5 32.1 %reduce-scatter.3.cloned.1.call-done = bf16[256,384]{0,1:T(8,128)(2,1)} async-done(((bf16[2048,384]{0,1:T(8,128)(2,1)}), bf16[256,384]{0,1:T(8,128)(2,1)}) %reduce-scatter.3.cloned.1.call-update) | async-done | bytes 196624 | tf_op jit(solution)/shard_map/while/body/eval_jaxpr/reduce_scatter | solution.py:263
  771.7 68.4 %reduce-scatter.5.cloned.1.call-done = bf16[256,384]{0,1:T(8,128)(2,1)} async-done(((bf16[2048,384]{0,1:T(8,128)(2,1)}), bf16[256,384]{0,1:T(8,128)(2,1)}) %reduce-scatter.5.cloned.1.call-update) | async-done | bytes 196624 | tf_op jit(solution)/shard_map/while/body/eval_jaxpr/reduce_scatter | solution.py:260
  862.9 40.2 %all-gather.11.cloned.1.call-done = bf16[2048,384]{1,0:T(8,128)(2,1)} async-done(((bf16[256,384]{1,0:T(8,128)(2,1)}), bf16[2048,384]{1,0:T(8,128)(2,1)}) %all-gather.11.cloned.1.call-update) | async-done | bytes 1572880 | tf_op jit(solution)/shard_map/while/body/eval_jaxpr/all_gather | solution.py:182
  912.0 36.2 %all-gather.9.cloned.1.call-done = bf16[2048,384]{1,0:T(8,128)(2,1)} async-done(((bf16[256,384]{1,0:T(8,128)(2,1)}), bf16[2048,384]{1,0:T(8,128)(2,1)}) %all-gather.9.cloned.1.call-update) | async-done | bytes 1572880 | tf_op jit(solution)/shard_map/while/body/eval_jaxpr/all_gather | solution.py:183
  1012.6 32.2 %reduce-scatter.3.cloned.1.call-done = bf16[256,384]{0,1:T(8,128)(2,1)} async-done(((bf16[2048,384]{0,1:T(8,128)(2,1)}), bf16[256,384]{0,1:T(8,128)(2,1)}) %reduce-scatter.3.cloned.1.call-update) | async-done | bytes 196624 | tf_op jit(solution)/shard_map/while/body/eval_jaxpr/reduce_scatter | solution.py:263
  1044.8 68.4 %reduce-scatter.5.cloned.1.call-done = bf16[256,384]{0,1:T(8,128)(2,1)} async-done(((bf16[2048,384]{0,1:T(8,128)(2,1)}), bf16[256,384]{0,1:T(8,128)(2,1)}) %reduce-scatter.5.cloned.1.call-update) | async-done | bytes 196624 | tf_op jit(solution)/shard_map/while/body/eval_jaxpr/reduce_scatter | solution.py:260
  1136.0 40.2 %all-gather.11.cloned.1.call-done = bf16[2048,384]{1,0:T(8,128)(2,1)} async-done(((bf16[256,384]{1,0:T(8,128)(2,1)}), bf16[2048,384]{1,0:T(8,128)(2,1)}) %all-gather.11.cloned.1.call-update) | async-done | bytes 1572880 | tf_op jit(solution)/shard_map/while/body/eval_jaxpr/all_gather | solution.py:182
  1185.2 36.2 %all-gather.9.cloned.1.call-done = bf16[2048,384]{1,0:T(8,128)(2,1)} async-done(((bf16[256,384]{1,0:T(8,128)(2,1)}), bf16[2048,384]{1,0:T(8,128)(2,1)}) %all-gather.9.cloned.1.call-update) | async-done | bytes 1572880 | tf_op jit(solution)/shard_map/while/body/eval_jaxpr/all_gather | solution.py:183
  1285.8 32.2 %reduce-scatter.3.cloned.1.call-done = bf16[256,384]{0,1:T(8,128)(2,1)} async-done(((bf16[2048,384]{0,1:T(8,128)(2,1)}), bf16[256,384]{0,1:T(8,128)(2,1)}) %reduce-scatter.3.cloned.1.call-update) | async-done | bytes 196624 | tf_op jit(solution)/shard_map/while/body/eval_jaxpr/reduce_scatter | solution.py:263
  1318.0 68.2 %reduce-scatter.5.cloned.1.call-done = bf16[256,384]{0,1:T(8,128)(2,1)} async-done(((bf16[2048,384]{0,1:T(8,128)(2,1)}), bf16[256,384]{0,1:T(8,128)(2,1)}) %reduce-scatter.5.cloned.1.call-update) | async-done | bytes 196624 | tf_op jit(solution)/shard_map/while/body/eval_jaxpr/reduce_scatter | solution.py:260
  1409.1 40.3 %all-gather.11.cloned.1.call-done = bf16[2048,384]{1,0:T(8,128)(2,1)} async-done(((bf16[256,384]{1,0:T(8,128)(2,1)}), bf16[2048,384]{1,0:T(8,128)(2,1)}) %all-gather.11.cloned.1.call-update) | async-done | bytes 1572880 | tf_op jit(solution)/shard_map/while/body/eval_jaxpr/all_gather | solution.py:182
  1458.2 36.3 %all-gather.9.cloned.1.call-done = bf16[2048,384]{1,0:T(8,128)(2,1)} async-done(((bf16[256,384]{1,0:T(8,128)(2,1)}), bf16[2048,384]{1,0:T(8,128)(2,1)}) %all-gather.9.cloned.1.call-update) | async-done | bytes 1572880 | tf_op jit(solution)/shard_map/while/body/eval_jaxpr/all_gather | solution.py:183
  1559.0 32.2 %reduce-scatter.3.cloned.1.call-done = bf16[256,384]{0,1:T(8,128)(2,1)} async-done(((bf16[2048,384]{0,1:T(8,128)(2,1)}), bf16[256,384]{0,1:T(8,128)(2,1)}) %reduce-scatter.3.cloned.1.call-update) | async-done | bytes 196624 | tf_op jit(solution)/shard_map/while/body/eval_jaxpr/reduce_scatter | solution.py:263
  1591.2 68.4 %reduce-scatter.5.cloned.1.call-done = bf16[256,384]{0,1:T(8,128)(2,1)} async-done(((bf16[2048,384]{0,1:T(8,128)(2,1)}), bf16[256,384]{0,1:T(8,128)(2,1)}) %reduce-scatter.5.cloned.1.call-update) | async-done | bytes 196624 | tf_op jit(solution)/shard_map/while/body/eval_jaxpr/reduce_scatter | solution.py:260
  1686.0 667.5 %while.43 = (s32[]{:T(128)}, bf16[6,256,384]{2,1,0:T(8,128)(2,1)}, bf16[6,256,384]{2,1,0:T(8,128)(2,1)}, f32[6,256,2304]{2,1,0:T(8,128)}, bf16[384,1152]{1,0:T(8...) while((s32[]{:T(128)}, bf16[6,256,384]{2,1,0:T(8,128)(2,1)}, ...), condition=%wide.region_10.11_spmd, body=%wide.region_3.10_spmd.sunk | while | flops 1738148352 | bytes 72687400 | solution.py:175
  1696.6 40.4 %all-gather.7.cloned.1.call-done = bf16[2048,384]{1,0:T(8,128)(2,1)} async-done(((bf16[256,384]{1,0:T(8,128)(2,1)}), bf16[2048,384]{1,0:T(8,128)(2,1)}) %all-gather.7.cloned.1.call-update) | async-done | bytes 1572880 | tf_op jit(solution)/shard_map/while/body/eval_jaxpr/all_gather | solution.py:166
  1739.6 10.1 fusion.274
  1749.7 32.3 %all-gather.5.cloned.1.call-done = bf16[2048,384]{1,0:T(8,128)(2,1)} async-done(((bf16[256,384]{1,0:T(8,128)(2,1)}), bf16[2048,384]{1,0:T(8,128)(2,1)}) %all-gather.5.cloned.1.call-update) | async-done | bytes 1572880 | tf_op jit(solution)/shard_map/while/body/eval_jaxpr/all_gather | solution.py:167
  1807.9 40.3 %all-gather.7.cloned.1.call-done = bf16[2048,384]{1,0:T(8,128)(2,1)} async-done(((bf16[256,384]{1,0:T(8,128)(2,1)}), bf16[2048,384]{1,0:T(8,128)(2,1)}) %all-gather.7.cloned.1.call-update) | async-done | bytes 1572880 | tf_op jit(solution)/shard_map/while/body/eval_jaxpr/all_gather | solution.py:166
  1850.8 10.1 fusion.274
  1860.9 32.5 %all-gather.5.cloned.1.call-done = bf16[2048,384]{1,0:T(8,128)(2,1)} async-done(((bf16[256,384]{1,0:T(8,128)(2,1)}), bf16[2048,384]{1,0:T(8,128)(2,1)}) %all-gather.5.cloned.1.call-update) | async-done | bytes 1572880 | tf_op jit(solution)/shard_map/while/body/eval_jaxpr/all_gather | solution.py:167
  1919.2 40.3 %all-gather.7.cloned.1.call-done = bf16[2048,384]{1,0:T(8,128)(2,1)} async-done(((bf16[256,384]{1,0:T(8,128)(2,1)}), bf16[2048,384]{1,0:T(8,128)(2,1)}) %all-gather.7.cloned.1.call-update) | async-done | bytes 1572880 | tf_op jit(solution)/shard_map/while/body/eval_jaxpr/all_gather | solution.py:166
  1962.1 10.1 fusion.274
  1972.2 32.3 %all-gather.5.cloned.1.call-done = bf16[2048,384]{1,0:T(8,128)(2,1)} async-done(((bf16[256,384]{1,0:T(8,128)(2,1)}), bf16[2048,384]{1,0:T(8,128)(2,1)}) %all-gather.5.cloned.1.call-update) | async-done | bytes 1572880 | tf_op jit(solution)/shard_map/while/body/eval_jaxpr/all_gather | solution.py:167
  2030.3 40.3 %all-gather.7.cloned.1.call-done = bf16[2048,384]{1,0:T(8,128)(2,1)} async-done(((bf16[256,384]{1,0:T(8,128)(2,1)}), bf16[2048,384]{1,0:T(8,128)(2,1)}) %all-gather.7.cloned.1.call-update) | async-done | bytes 1572880 | tf_op jit(solution)/shard_map/while/body/eval_jaxpr/all_gather | solution.py:166
  2073.2 10.1 fusion.274
  2083.3 32.5 %all-gather.5.cloned.1.call-done = bf16[2048,384]{1,0:T(8,128)(2,1)} async-done(((bf16[256,384]{1,0:T(8,128)(2,1)}), bf16[2048,384]{1,0:T(8,128)(2,1)}) %all-gather.5.cloned.1.call-update) | async-done | bytes 1572880 | tf_op jit(solution)/shard_map/while/body/eval_jaxpr/all_gather | solution.py:167
  2141.6 40.3 %all-gather.7.cloned.1.call-done = bf16[2048,384]{1,0:T(8,128)(2,1)} async-done(((bf16[256,384]{1,0:T(8,128)(2,1)}), bf16[2048,384]{1,0:T(8,128)(2,1)}) %all-gather.7.cloned.1.call-update) | async-done | bytes 1572880 | tf_op jit(solution)/shard_map/while/body/eval_jaxpr/all_gather | solution.py:166
  2184.5 10.1 fusion.274
  2194.6 32.5 %all-gather.5.cloned.1.call-done = bf16[2048,384]{1,0:T(8,128)(2,1)} async-done(((bf16[256,384]{1,0:T(8,128)(2,1)}), bf16[2048,384]{1,0:T(8,128)(2,1)}) %all-gather.5.cloned.1.call-update) | async-done | bytes 1572880 | tf_op jit(solution)/shard_map/while/body/eval_jaxpr/all_gather | solution.py:167
  2252.9 40.3 %all-gather.7.cloned.1.call-done = bf16[2048,384]{1,0:T(8,128)(2,1)} async-done(((bf16[256,384]{1,0:T(8,128)(2,1)}), bf16[2048,384]{1,0:T(8,128)(2,1)}) %all-gather.7.cloned.1.call-update) | async-done | bytes 1572880 | tf_op jit(solution)/shard_map/while/body/eval_jaxpr/all_gather | solution.py:166
  2295.8 10.1 fusion.274
  2306.0 32.3 %all-gather.5.cloned.1.call-done = bf16[2048,384]{1,0:T(8,128)(2,1)} async-done(((bf16[256,384]{1,0:T(8,128)(2,1)}), bf16[2048,384]{1,0:T(8,128)(2,1)}) %all-gather.5.cloned.1.call-update) | async-done | bytes 1572880 | tf_op jit(solution)/shard_map/while/body/eval_jaxpr/all_gather | solution.py:167
  2354.7 41.1 %all-reduce = (f32[2304]{0:T(1024)}, f32[384]{0:T(512)}, f32[384]{0:T(512)}, f32[384]{0:T(512)}, f32[1536]{0:T(1024)}, /*index=5*/f32[384]{0:T(512)}) all-reduce(f32[2304]{0:T(1024)S(1)} %reduce_sum.253, f32[384]{0:T(512)S(1)} %copy-done.58, f32[384]{0:T(512)S(1)} %copy-done.55, ...), channel_id=1, replica_groups=mesh['rows'=4,'band'=8] {'rows','band'}, use_global_device_ids=true, to_apply=%region_33.34 | all-reduce | flops 5376 | bytes 43008 | tf_op jit(solution)/shard_map/psum | solution.py:312
  2395.7 183.3 %all-reduce.4.cloned.1.call-done = (f32[384,2304]{1,0:T(8,128)}, f32[384,1152]{1,0:T(8,128)}, f32[384,384]{1,0:T(8,128)}, f32[384,1536]{1,0:T(8,128)}, f32[1536,384]{1,0:T(8,128)}) async-done(((f32[384,2304]{1,0:T(8,128)}, f32[384,1152]{1,0:T(8,128)}, f32[384,384]{1,0:T(8,128)}, f32[384,1536]{1,0:T(8,128)}, f32[1536,384]{1,0:T(8,128)}), (f32[384,2304]{1,0:T(8,128)}, f32[384,1152]{1,0:T(8,128)}, ...) | async-done | bytes 10616848 | tf_op jit(solution)/shard_map/psum | solution.py:312
  (1138 shorter events, 760.2 us)
Async XLA Ops:
  29.8 53.7 %all-gather.11.cloned.1.call-start = ((), (), s32[]{:S(2)}) async-start(), calls=%async_computation.6 | async-start | bytes 1769472 | tf_op jit(solution)/shard_map/while/body/eval_jaxpr/all_gather | solution.py:182
  36.4 92.2 %all-gather.9.cloned.1.call-start = ((), (), s32[]{:S(2)}) async-start(), calls=%async_computation.5 | async-start | bytes 1769472 | tf_op jit(solution)/shard_map/while/body/eval_jaxpr/all_gather | solution.py:183
  37.2 188.0 %reduce-scatter.3.cloned.1.call-start = ((), (), s32[]{:S(2)}) async-start(), calls=%async_computation.7 | async-start | bytes 1769472 | tf_op jit(solution)/shard_map/while/body/eval_jaxpr/reduce_scatter | solution.py:263
  160.6 132.9 %reduce-scatter.5.cloned.1.call-start = ((), (), s32[]{:S(2)}) async-start(), calls=%async_computation.8 | async-start | bytes 1769472 | tf_op jit(solution)/shard_map/while/body/eval_jaxpr/reduce_scatter | solution.py:260
  186.9 106.7 %copy-start.7 = (bf16[384,1152]{1,0:T(8,128)(2,1)S(1)}, bf16[384,1152]{1,0:T(8,128)(2,1)}, u32[]{:S(2)}) copy-start(bf16[384,1152]{1,0:T(8,128)(2,1)} %get-tuple-element.1184) | copy-start | bytes 2654212 | tf_op jit(solution)/shard_map/while
  186.9 106.7 %copy-start.26 = (bf16[6,64,256]{2,1,0:T(8,128)(2,1)S(1)}, bf16[6,64,256]{2,1,0:T(8,128)(2,1)}, u32[]{:S(2)}) copy-start(bf16[6,64,256]{2,1,0:T(8,128)(2,1)} %get-tuple-element.971) | copy-start | bytes 589828 | tf_op jit(solution)/shard_map/while
  306.8 49.9 %all-gather.11.cloned.1.call-start = ((), (), s32[]{:S(2)}) async-start(), calls=%async_computation.6 | async-start | bytes 1769472 | tf_op jit(solution)/shard_map/while/body/eval_jaxpr/all_gather | solution.py:182
  313.4 88.3 %all-gather.9.cloned.1.call-start = ((), (), s32[]{:S(2)}) async-start(), calls=%async_computation.5 | async-start | bytes 1769472 | tf_op jit(solution)/shard_map/while/body/eval_jaxpr/all_gather | solution.py:183
  314.2 184.2 %reduce-scatter.3.cloned.1.call-start = ((), (), s32[]{:S(2)}) async-start(), calls=%async_computation.7 | async-start | bytes 1769472 | tf_op jit(solution)/shard_map/while/body/eval_jaxpr/reduce_scatter | solution.py:263
  433.7 133.2 %reduce-scatter.5.cloned.1.call-start = ((), (), s32[]{:S(2)}) async-start(), calls=%async_computation.8 | async-start | bytes 1769472 | tf_op jit(solution)/shard_map/while/body/eval_jaxpr/reduce_scatter | solution.py:260
  462.0 104.9 %copy-start.7 = (bf16[384,1152]{1,0:T(8,128)(2,1)S(1)}, bf16[384,1152]{1,0:T(8,128)(2,1)}, u32[]{:S(2)}) copy-start(bf16[384,1152]{1,0:T(8,128)(2,1)} %get-tuple-element.1184) | copy-start | bytes 2654212 | tf_op jit(solution)/shard_map/while
  462.0 104.9 %copy-start.26 = (bf16[6,64,256]{2,1,0:T(8,128)(2,1)S(1)}, bf16[6,64,256]{2,1,0:T(8,128)(2,1)}, u32[]{:S(2)}) copy-start(bf16[6,64,256]{2,1,0:T(8,128)(2,1)} %get-tuple-element.971) | copy-start | bytes 589828 | tf_op jit(solution)/shard_map/while
  580.1 49.9 %all-gather.11.cloned.1.call-start = ((), (), s32[]{:S(2)}) async-start(), calls=%async_computation.6 | async-start | bytes 1769472 | tf_op jit(solution)/shard_map/while/body/eval_jaxpr/all_gather | solution.py:182
  586.8 88.3 %all-gather.9.cloned.1.call-start = ((), (), s32[]{:S(2)}) async-start(), calls=%async_computation.5 | async-start | bytes 1769472 | tf_op jit(solution)/shard_map/while/body/eval_jaxpr/all_gather | solution.py:183
  587.6 184.1 %reduce-scatter.3.cloned.1.call-start = ((), (), s32[]{:S(2)}) async-start(), calls=%async_computation.7 | async-start | bytes 1769472 | tf_op jit(solution)/shard_map/while/body/eval_jaxpr/reduce_scatter | solution.py:263
  707.1 132.9 %reduce-scatter.5.cloned.1.call-start = ((), (), s32[]{:S(2)}) async-start(), calls=%async_computation.8 | async-start | bytes 1769472 | tf_op jit(solution)/shard_map/while/body/eval_jaxpr/reduce_scatter | solution.py:260
  735.4 104.7 %copy-start.7 = (bf16[384,1152]{1,0:T(8,128)(2,1)S(1)}, bf16[384,1152]{1,0:T(8,128)(2,1)}, u32[]{:S(2)}) copy-start(bf16[384,1152]{1,0:T(8,128)(2,1)} %get-tuple-element.1184) | copy-start | bytes 2654212 | tf_op jit(solution)/shard_map/while
  735.4 104.7 %copy-start.26 = (bf16[6,64,256]{2,1,0:T(8,128)(2,1)S(1)}, bf16[6,64,256]{2,1,0:T(8,128)(2,1)}, u32[]{:S(2)}) copy-start(bf16[6,64,256]{2,1,0:T(8,128)(2,1)} %get-tuple-element.971) | copy-start | bytes 589828 | tf_op jit(solution)/shard_map/while
  853.2 49.9 %all-gather.11.cloned.1.call-start = ((), (), s32[]{:S(2)}) async-start(), calls=%async_computation.6 | async-start | bytes 1769472 | tf_op jit(solution)/shard_map/while/body/eval_jaxpr/all_gather | solution.py:182
  859.9 88.3 %all-gather.9.cloned.1.call-start = ((), (), s32[]{:S(2)}) async-start(), calls=%async_computation.5 | async-start | bytes 1769472 | tf_op jit(solution)/shard_map/while/body/eval_jaxpr/all_gather | solution.py:183
  860.7 184.1 %reduce-scatter.3.cloned.1.call-start = ((), (), s32[]{:S(2)}) async-start(), calls=%async_computation.7 | async-start | bytes 1769472 | tf_op jit(solution)/shard_map/while/body/eval_jaxpr/reduce_scatter | solution.py:263
  980.2 133.0 %reduce-scatter.5.cloned.1.call-start = ((), (), s32[]{:S(2)}) async-start(), calls=%async_computation.8 | async-start | bytes 1769472 | tf_op jit(solution)/shard_map/while/body/eval_jaxpr/reduce_scatter | solution.py:260
  1008.4 104.7 %copy-start.7 = (bf16[384,1152]{1,0:T(8,128)(2,1)S(1)}, bf16[384,1152]{1,0:T(8,128)(2,1)}, u32[]{:S(2)}) copy-start(bf16[384,1152]{1,0:T(8,128)(2,1)} %get-tuple-element.1184) | copy-start | bytes 2654212 | tf_op jit(solution)/shard_map/while
  1008.5 104.7 %copy-start.26 = (bf16[6,64,256]{2,1,0:T(8,128)(2,1)S(1)}, bf16[6,64,256]{2,1,0:T(8,128)(2,1)}, u32[]{:S(2)}) copy-start(bf16[6,64,256]{2,1,0:T(8,128)(2,1)} %get-tuple-element.971) | copy-start | bytes 589828 | tf_op jit(solution)/shard_map/while
  1126.4 49.9 %all-gather.11.cloned.1.call-start = ((), (), s32[]{:S(2)}) async-start(), calls=%async_computation.6 | async-start | bytes 1769472 | tf_op jit(solution)/shard_map/while/body/eval_jaxpr/all_gather | solution.py:182
  1133.0 88.3 %all-gather.9.cloned.1.call-start = ((), (), s32[]{:S(2)}) async-start(), calls=%async_computation.5 | async-start | bytes 1769472 | tf_op jit(solution)/shard_map/while/body/eval_jaxpr/all_gather | solution.py:183
  1133.9 184.2 %reduce-scatter.3.cloned.1.call-start = ((), (), s32[]{:S(2)}) async-start(), calls=%async_computation.7 | async-start | bytes 1769472 | tf_op jit(solution)/shard_map/while/body/eval_jaxpr/reduce_scatter | solution.py:263
  1253.3 132.9 %reduce-scatter.5.cloned.1.call-start = ((), (), s32[]{:S(2)}) async-start(), calls=%async_computation.8 | async-start | bytes 1769472 | tf_op jit(solution)/shard_map/while/body/eval_jaxpr/reduce_scatter | solution.py:260
  1281.6 104.6 %copy-start.7 = (bf16[384,1152]{1,0:T(8,128)(2,1)S(1)}, bf16[384,1152]{1,0:T(8,128)(2,1)}, u32[]{:S(2)}) copy-start(bf16[384,1152]{1,0:T(8,128)(2,1)} %get-tuple-element.1184) | copy-start | bytes 2654212 | tf_op jit(solution)/shard_map/while
  1399.4 49.9 %all-gather.11.cloned.1.call-start = ((), (), s32[]{:S(2)}) async-start(), calls=%async_computation.6 | async-start | bytes 1769472 | tf_op jit(solution)/shard_map/while/body/eval_jaxpr/all_gather | solution.py:182
  1406.1 88.5 %all-gather.9.cloned.1.call-start = ((), (), s32[]{:S(2)}) async-start(), calls=%async_computation.5 | async-start | bytes 1769472 | tf_op jit(solution)/shard_map/while/body/eval_jaxpr/all_gather | solution.py:183
  1406.9 184.3 %reduce-scatter.3.cloned.1.call-start = ((), (), s32[]{:S(2)}) async-start(), calls=%async_computation.7 | async-start | bytes 1769472 | tf_op jit(solution)/shard_map/while/body/eval_jaxpr/reduce_scatter | solution.py:263
  1526.5 133.1 %reduce-scatter.5.cloned.1.call-start = ((), (), s32[]{:S(2)}) async-start(), calls=%async_computation.8 | async-start | bytes 1769472 | tf_op jit(solution)/shard_map/while/body/eval_jaxpr/reduce_scatter | solution.py:260
  1554.8 104.8 %copy-start.7 = (bf16[384,1152]{1,0:T(8,128)(2,1)S(1)}, bf16[384,1152]{1,0:T(8,128)(2,1)}, u32[]{:S(2)}) copy-start(bf16[384,1152]{1,0:T(8,128)(2,1)} %get-tuple-element.1184) | copy-start | bytes 2654212 | tf_op jit(solution)/shard_map/while
  1554.8 104.8 %copy-start.26 = (bf16[6,64,256]{2,1,0:T(8,128)(2,1)S(1)}, bf16[6,64,256]{2,1,0:T(8,128)(2,1)}, u32[]{:S(2)}) copy-start(bf16[6,64,256]{2,1,0:T(8,128)(2,1)} %get-tuple-element.971) | copy-start | bytes 589828 | tf_op jit(solution)/shard_map/while
  1686.0 51.0 %all-gather.7.cloned.1.call-start = ((), (), s32[]{:S(2)}) async-start(), calls=%async_computation.4 | async-start | bytes 1769472 | tf_op jit(solution)/shard_map/while/body/eval_jaxpr/all_gather | solution.py:166
  1693.7 88.3 %all-gather.5.cloned.1.call-start = ((), (), s32[]{:S(2)}) async-start(), calls=%async_computation.3 | async-start | bytes 1769472 | tf_op jit(solution)/shard_map/while/body/eval_jaxpr/all_gather | solution.py:167
  1797.3 50.8 %all-gather.7.cloned.1.call-start = ((), (), s32[]{:S(2)}) async-start(), calls=%async_computation.4 | async-start | bytes 1769472 | tf_op jit(solution)/shard_map/while/body/eval_jaxpr/all_gather | solution.py:166
  1805.0 88.4 %all-gather.5.cloned.1.call-start = ((), (), s32[]{:S(2)}) async-start(), calls=%async_computation.3 | async-start | bytes 1769472 | tf_op jit(solution)/shard_map/while/body/eval_jaxpr/all_gather | solution.py:167
  1908.6 50.8 %all-gather.7.cloned.1.call-start = ((), (), s32[]{:S(2)}) async-start(), calls=%async_computation.4 | async-start | bytes 1769472 | tf_op jit(solution)/shard_map/while/body/eval_jaxpr/all_gather | solution.py:166
  1916.3 88.2 %all-gather.5.cloned.1.call-start = ((), (), s32[]{:S(2)}) async-start(), calls=%async_computation.3 | async-start | bytes 1769472 | tf_op jit(solution)/shard_map/while/body/eval_jaxpr/all_gather | solution.py:167
  2019.8 50.8 %all-gather.7.cloned.1.call-start = ((), (), s32[]{:S(2)}) async-start(), calls=%async_computation.4 | async-start | bytes 1769472 | tf_op jit(solution)/shard_map/while/body/eval_jaxpr/all_gather | solution.py:166
  2027.4 88.4 %all-gather.5.cloned.1.call-start = ((), (), s32[]{:S(2)}) async-start(), calls=%async_computation.3 | async-start | bytes 1769472 | tf_op jit(solution)/shard_map/while/body/eval_jaxpr/all_gather | solution.py:167
  2131.1 50.8 %all-gather.7.cloned.1.call-start = ((), (), s32[]{:S(2)}) async-start(), calls=%async_computation.4 | async-start | bytes 1769472 | tf_op jit(solution)/shard_map/while/body/eval_jaxpr/all_gather | solution.py:166
  2138.7 88.4 %all-gather.5.cloned.1.call-start = ((), (), s32[]{:S(2)}) async-start(), calls=%async_computation.3 | async-start | bytes 1769472 | tf_op jit(solution)/shard_map/while/body/eval_jaxpr/all_gather | solution.py:167
  2242.4 50.8 %all-gather.7.cloned.1.call-start = ((), (), s32[]{:S(2)}) async-start(), calls=%async_computation.4 | async-start | bytes 1769472 | tf_op jit(solution)/shard_map/while/body/eval_jaxpr/all_gather | solution.py:166
  2250.1 88.2 %all-gather.5.cloned.1.call-start = ((), (), s32[]{:S(2)}) async-start(), calls=%async_computation.3 | async-start | bytes 1769472 | tf_op jit(solution)/shard_map/while/body/eval_jaxpr/all_gather | solution.py:167
  2353.6 225.5 %all-reduce.4.cloned.1.call-start = ((), (), s32[]{:S(2)}) async-start(), calls=%async_computation.2 | async-start | bytes 21233664 | tf_op jit(solution)/shard_map/psum | solution.py:312
  (283 other events, 1536.3 us)
Sparse Core Ops, SparseCore 0:
  36.5 46.8 all-gather.10
  85.6 42.9 all-gather.8
  160.8 64.4 reduce-scatter.2
  228.9 64.5 reduce-scatter.4
  313.5 43.0 all-gather.10
  358.7 42.9 all-gather.8
  433.8 64.5 reduce-scatter.2
  502.2 64.6 reduce-scatter.4
  586.9 43.1 all-gather.10
  632.1 42.9 all-gather.8
  707.2 64.4 reduce-scatter.2
  775.4 64.6 reduce-scatter.4
  860.0 43.0 all-gather.10
  905.2 42.9 all-gather.8
  980.3 64.4 reduce-scatter.2
  1048.5 64.6 reduce-scatter.4
  1133.2 43.0 all-gather.10
  1178.3 42.9 all-gather.8
  1253.5 64.5 reduce-scatter.2
  1321.7 64.4 reduce-scatter.4
  1406.2 43.0 all-gather.10
  1451.5 42.9 all-gather.8
  1526.7 64.5 reduce-scatter.2
  1594.9 64.6 reduce-scatter.4
  1693.8 43.1 all-gather.6
  1739.0 42.9 all-gather.4
  1805.1 42.9 all-gather.6
  1850.3 42.9 all-gather.4
  1916.4 42.9 all-gather.6
  1961.5 42.9 all-gather.4
  2027.5 42.9 all-gather.6
  2072.8 43.0 all-gather.4
  2138.9 42.9 all-gather.6
  2184.1 43.0 all-gather.4
  2250.2 42.9 all-gather.6
  2295.2 42.9 all-gather.4
Sparse Core Ops, SparseCore 1:
  2361.6 217.4 all-reduce.3
where the time goes:
time: 2610 us; the launch traced here: 2600 us
  waiting for transfers between devices  1690 us (65%)
  matrix products  529 us (20%)
  local copies, waits for them, and re-layouts  171 us (7%)
  other arithmetic  135 us (5%)
  blocking collectives  41.1 us (2%)
    reduce_scatter x6, waiting for transfers between devices, backward_step(): lax.psum_scatter(key_term.astype(jnp.bfloat16), 'band', scatter_dimension...  410 us
    all_gather x6, waiting for transfers between devices, gather_again(): lax.all_gather(keys, 'band', axis=0, tiled=True)  245 us
    all_gather x6, waiting for transfers between devices, gather_forward(): lax.all_gather(keys, 'band', axis=0, tiled=True)  242 us
    all_gather x6, waiting for transfers between devices, gather_again(): lax.all_gather(values, 'band', axis=0, tiled=True)  217 us
    reduce_scatter x6, waiting for transfers between devices, backward_step(): lax.psum_scatter(value_term.astype(jnp.bfloat16), 'band', scatter_dimensi...  197 us
    all_gather x6, waiting for transfers between devices, gather_forward(): lax.all_gather(values, 'band', axis=0, tiled=True)  194 us
    psum x1, waiting for transfers between devices, body(): lax.psum((modulate_w_grad, modulate_b_grad, totals[0], totals[1], totals[...  183 us
    sub x12, matrix products, probabilities(): exps = jnp.exp(scores - maxima)  104 us
  transfers between devices with their start and end apart: 37, of which 37 were waited for; matrix products, arithmetic and copies ran while one was open for 14% of the time, Pallas kernels for 0%

commit v1 on v0

v1 whole, which is shorter than its diff:
```python
from functools import partial

import jax
import jax.numpy as jnp
from jax import lax
from jax.experimental import pallas as pl
from jax.experimental.pallas import tpu as pltpu
from jax.sharding import PartitionSpec as P

HEADS = 6
HEAD_DIM = 64
PAIRS = HEADS // 2
LANES = 128
BLOCK = 256
HALF = 4
EPSILON = 1e-06
ONES = 16
F32 = jnp.float32
BF16 = jnp.bfloat16
MIB = 1 << 20


def dot(left, right):
    return jnp.dot(left, right, preferred_element_type=F32)


def dot_nt(left, right):
    return lax.dot_general(left, right, (((1,), (1,)), ((), ())), preferred_element_type=F32)


def params(limit=56, **more):
    return pltpu.CompilerParams(vmem_limit_bytes=limit * MIB, **more)


def full(shape):
    return pl.BlockSpec(shape, lambda *_: (0,) * len(shape))


SMEM = pl.BlockSpec(memory_space=pltpu.SMEM)


def row_layout(lens_ref, row, slots, big):
    count = jnp.int32(0)
    before = jnp.int32(0)
    for j in range(slots):
        is_big = (lens_ref[row, j] == big).astype(jnp.int32)
        before = before + jnp.where(count + is_big == 0, 1, 0)
        count = count + is_big
    return count, jnp.where(count == 1, before, 0)


def chunk_of(start, half, k):
    return jnp.where(half == 0, start + k, jnp.where(k < start, k, k + HALF))


class Plan:
    def __init__(self, rows, bands):
        self.rows, self.bands = rows, bands
        self.halves = 2 * rows
        self.whole = self.halves // bands
        assert self.whole <= 1
        self.rest = self.halves - self.whole * bands
        self.group = 1
        while self.rest and self.rest * self.group * 2 <= bands and self.group < HALF:
            self.group *= 2
        self.idle = self.rest * self.group != bands
        self.own = HALF // self.group

    def units(self):
        found = []
        if self.whole:
            found.append(("whole", HALF))
        if self.rest:
            found.append(("shared", self.own))
        return found

    def half_row(self, name, device):
        if name == "whole":
            return device
        return self.whole * self.bands + device // self.group

    def first(self, name, device):
        return 0 if name == "whole" else (device % self.group) * self.own


def pack_kernel(plan, chunk, slots, big, me_ref, lens_ref, x_ref, *outs):
    me = me_ref[0]
    at = 0
    for name, count in plan.units():
        for s in range(plan.bands):
            dest = me ^ s
            half_row = jnp.minimum(plan.half_row(name, dest), plan.halves - 1)
            row, half = half_row // 2, half_row % 2
            start = row_layout(lens_ref, row, slots, big)[1]
            for k in range(count):
                source = chunk_of(start, half, plan.first(name, dest) + k)
                outs[at][k] = x_ref[row, pl.ds(pl.multiple_of(source * chunk, chunk), chunk), :]
            at += 1


def pack(plan, chunk, big, me, lens, x):
    width = x.shape[2]
    shapes = [
        jax.ShapeDtypeStruct((count, chunk, width), x.dtype)
        for _, count in plan.units()
        for _ in range(plan.bands)
    ]
    return pl.pallas_call(
        partial(pack_kernel, plan, chunk, lens.shape[1], big),
        in_specs=[SMEM, SMEM, full(x.shape)],
        out_specs=[full(s.shape) for s in shapes],
        out_shape=shapes,
        grid=(1,),
        compiler_params=params(32),
        name="pack",
    )(me, lens, x)


def unpack_kernel(plan, chunk, slots, big, me_ref, lens_ref, *refs):
    out_ref = refs[-1]
    me = me_ref[0]
    at = 0
    for name, count in plan.units():
        for s in range(plan.bands):
            owner = me ^ s
            half_row = plan.half_row(name, owner)

            def place(piece=refs[at], name=name, count=count, owner=owner, half_row=half_row):
                row, half = half_row // 2, half_row % 2
                start = row_layout(lens_ref, row, slots, big)[1]
                for k in range(count):
                    source = chunk_of(start, half, plan.first(name, owner) + k)
                    rows = pl.ds(pl.multiple_of(source * chunk, chunk), chunk)
                    out_ref[row, rows, :] = piece[k].astype(out_ref.dtype)

            if name == "shared" and plan.idle:
                pl.when(half_row < plan.halves)(place)
            else:
                place()
            at += 1


def unpack(plan, chunk, big, me, lens, pieces, dtype):
    width = pieces[0].shape[2]
    shape = (plan.rows, chunk * 2 * HALF, width)
    return pl.pallas_call(
        partial(unpack_kernel, plan, chunk, lens.shape[1], big),
        in_specs=[SMEM, SMEM] + [full(p.shape) for p in pieces],
        out_specs=full(shape),
        out_shape=jax.ShapeDtypeStruct(shape, dtype),
        grid=(1,),
        compiler_params=params(32),
        name="unpack",
    )(me, lens, *pieces)


def layer_norm(values):
    centre = values - jnp.mean(values, axis=-1, keepdims=True)
    inverse = lax.rsqrt(jnp.mean(centre * centre, axis=-1, keepdims=True) + EPSILON)
    return centre * inverse, inverse


def norm_back(grad, normed, inverse):
    return inverse * (
        grad
        - jnp.mean(grad, axis=-1, keepdims=True)
        - normed * jnp.mean(grad * normed, axis=-1, keepdims=True)
    )


def column_sum(values):
    return jnp.sum(values, axis=0, keepdims=True)


def attend_kernel(n, nq, nk, chunk, width, flag_ref, *refs):
    pieces, refs = refs[:n], refs[n:]
    count = nk // nq - 1
    others, refs = refs[:count], refs[count:]
    mods_ref, weight_ref, query_bias_ref, value_bias_ref = refs[:4]
    x_out, hin_out, q_out, k_out, v_out, e_out, ot_out, inv_out, mixed_out = refs[4:13]
    k_scr, qt_scr, vt_scr = refs[13:]
    p = pl.program_id(0)

    @pl.when(p == 0)
    def _():
        qt_scr[...] = jnp.zeros_like(qt_scr)
        for h in range(HEADS):
            vt_scr[h, HEAD_DIM:, :] = jnp.ones((ONES, nk * BLOCK), BF16)
        for b in range(nk):
            rows = pl.ds(b * BLOCK, BLOCK)
            if b < nq:
                for s in range(n):
                    x_out[pl.ds(b * BLOCK + s * chunk, chunk), :] = pieces[s][b]
            else:
                t, inner = b // nq - 1, b % nq
                x_out[rows, :] = others[t][pl.ds(inner * BLOCK, BLOCK), :]
            source = x_out[rows, :].astype(F32)
            normed = layer_norm(source)[0]
            shift = mods_ref[b : b + 1, 0:width]
            scale = mods_ref[b : b + 1, width : 2 * width]
            hin = (normed * (1.0 + scale) + shift).astype(BF16)
            hin_out[rows, :] = hin
            triple = dot(hin, weight_ref[...])
            keys = triple[:, width : 2 * width].astype(BF16)
            values = (triple[:, 2 * width :] + value_bias_ref[...]).astype(BF16)
            values_t = values.T
            for j in range(PAIRS):
                lanes = slice(j * LANES, (j + 1) * LANES)
                k_scr[j, rows, :] = keys[:, lanes]
                k_out[j, rows, :] = keys[:, lanes]
                v_out[j, rows, :] = values[:, lanes]
            for h in range(HEADS):
                vt_scr[h, :HEAD_DIM, rows] = values_t[h * HEAD_DIM : (h + 1) * HEAD_DIM]
            if b < nq:
                query = (triple[:, :width] + query_bias_ref[...]) * (HEAD_DIM**-0.5)
                query = query.astype(BF16)
                for j in range(PAIRS):
                    q_out[j, rows, :] = query[:, j * LANES : (j + 1) * LANES]
                query_t = query.T
                for h in range(HEADS):
                    to = (h % 2) * HEAD_DIM
                    qt_scr[h, to : to + HEAD_DIM, rows] = query_t[
                        h * HEAD_DIM : (h + 1) * HEAD_DIM
                    ]

    def tile(qt, low, size):
        columns = pl.ds(pl.multiple_of(qt * BLOCK, BLOCK), BLOCK)
        krows = pl.ds(low, size)
        found = []
        for hh in range(2):
            h = 2 * p + hh
            scores = dot(k_scr[p, krows, :], qt_scr[h, :, columns])
            exps = jnp.exp(scores - jnp.max(scores, axis=0, keepdims=True)).astype(BF16)
            e_out[hh, krows, columns] = exps
            summed = dot(vt_scr[h, :, krows], exps)
            inverse = 1.0 / summed[HEAD_DIM : HEAD_DIM + 1]
            found.append(summed[:HEAD_DIM] * inverse)
            inv_out[0, hh : hh + 1, columns] = inverse
        both = jnp.concatenate(found, axis=0)
        ot_out[0, :, columns] = both
        mixed_out[columns, :] = both.T.astype(BF16)

    @pl.when(flag_ref[0] == 1)
    def _():
        @pl.loop(0, nq)
        def _(qt):
            tile(qt, 0, nk * BLOCK)

    @pl.when(flag_ref[0] == 0)
    def _():
        @pl.loop(0, nq)
        def _(qt):
            tile(qt, pl.multiple_of(qt * BLOCK, BLOCK), BLOCK)


def attend(n, nq, nk, chunk, flag, pieces, others, mods, weight, query_bias, value_bias):
    width = weight.shape[0]
    qs, ks = nq * BLOCK, nk * BLOCK
    shape = jax.ShapeDtypeStruct
    outs = [
        (shape((ks, width), BF16), None),
        (shape((ks, width), BF16), None),
        (shape((PAIRS, qs, LANES), BF16), None),
        (shape((PAIRS, ks, LANES), BF16), None),
        (shape((PAIRS, ks, LANES), BF16), None),
        (shape((HEADS, ks, qs), BF16), pl.BlockSpec((2, ks, qs), lambda p: (p, 0, 0))),
        (shape((PAIRS, LANES, qs), F32), pl.BlockSpec((1, LANES, qs), lambda p: (p, 0, 0))),
        (shape((PAIRS, 8, qs), F32), pl.BlockSpec((1, 8, qs), lambda p: (p, 0, 0))),
        (shape((qs, width), BF16), pl.BlockSpec((qs, LANES), lambda p: (0, p))),
    ]
    arrays = [*pieces, *others, mods, weight, query_bias, value_bias]
    flops = 2 * ks * width * 3 * width + 4 * HEADS * qs * ks * HEAD_DIM * 4
    return pl.pallas_call(
        partial(attend_kernel, n, nq, nk, chunk, width),
        grid=(PAIRS,),
        in_specs=[SMEM] + [full(a.shape) for a in arrays],
        out_specs=[spec or full(s.shape) for s, spec in outs],
        out_shape=[s for s, _ in outs],
        scratch_shapes=[
            pltpu.VMEM((PAIRS, ks, LANES), BF16),
            pltpu.VMEM((HEADS, LANES, qs), BF16),
            pltpu.VMEM((HEADS, HEAD_DIM + ONES, ks), BF16),
        ],
        compiler_params=params(),
        cost_estimate=pl.CostEstimate(
            flops=flops, bytes_accessed=2 * HEADS * qs * ks, transcendentals=HEADS * qs * ks
        ),
        name="attend",
    )(flag, *arrays)


def attend_back_kernel(nq, nk, width, flag_ref, *refs):
    e_ref, q_ref, k_ref, v_ref, ot_ref, inv_ref, grad_ref, hin_ref, weight_ref = refs[:9]
    count = nk // nq - 1
    own_out, others_out = refs[9], refs[10 : 10 + count]
    tw_out, tb_out, dk_acc, dv_acc, kt_scr, tg_scr = refs[10 + count :]
    p = pl.program_id(0)
    dk_acc[...] = jnp.zeros_like(dk_acc)
    dv_acc[...] = jnp.zeros_like(dv_acc)
    kt_scr[...] = k_ref[0].T
    lane = lax.broadcasted_iota(jnp.int32, (BLOCK, LANES), 1)

    if nk > nq:

        @pl.when(p == 0)
        def _():
            tg_scr[0, nq * BLOCK :, :] = jnp.zeros(((nk - nq) * BLOCK, LANES), BF16)
            tg_scr[1, nq * BLOCK :, :] = jnp.zeros(((nk - nq) * BLOCK, LANES), BF16)
            tg_scr[2, nq * BLOCK :, :] = jnp.zeros(((nk - nq) * BLOCK, LANES), BF16)

    def tile(qt, low, size):
        columns = pl.ds(pl.multiple_of(qt * BLOCK, BLOCK), BLOCK)
        krows = pl.ds(low, size)
        grad_t = grad_ref[columns, :].astype(F32).T
        query = q_ref[0, columns, :]
        zeros = jnp.zeros((HEAD_DIM, BLOCK), BF16)
        found = []
        for hh in range(2):
            part = slice(hh * HEAD_DIM, (hh + 1) * HEAD_DIM)
            scaled = (grad_t[part] * inv_ref[0, hh : hh + 1, columns]).astype(BF16)
            delta = column_sum(scaled.astype(F32) * ot_ref[0, part, columns])
            masked = jnp.concatenate([scaled, zeros] if hh == 0 else [zeros, scaled], axis=0)
            exps = e_ref[hh, krows, columns]
            prob_grad = dot(v_ref[0, krows, :], masked)
            score_grad = (exps.astype(F32) * (prob_grad - delta)).astype(BF16)
            dv_acc[krows, :] += dot_nt(exps, masked)
            own = (lane < HEAD_DIM) if hh == 0 else (lane >= HEAD_DIM)
            dk_acc[krows, :] += dot(score_grad, jnp.where(own, query, jnp.zeros_like(query)))
            found.append(dot(kt_scr[part, krows], score_grad))
        both = jnp.concatenate(found, axis=0) * (HEAD_DIM**-0.5)
        tg_scr[p, columns, :] = both.T.astype(BF16)

    @pl.when(flag_ref[0] == 1)
    def _():
        @pl.loop(0, nq)
        def _(qt):
            tile(qt, 0, nk * BLOCK)

    @pl.when(flag_ref[0] == 0)
    def _():
        @pl.loop(0, nq)
        def _(qt):
            tile(qt, pl.multiple_of(qt * BLOCK, BLOCK), BLOCK)

    tg_scr[PAIRS + p] = dk_acc[...].astype(BF16)
    tg_scr[2 * PAIRS + p] = dv_acc[...].astype(BF16)

    @pl.when(p == PAIRS - 1)
    def _():
        grads = jnp.concatenate([tg_scr[j] for j in range(3 * PAIRS)], axis=1)
        back = dot_nt(grads, weight_ref[...])
        own_out[...] = back[: nq * BLOCK]
        for t in range(count):
            lo = (t + 1) * nq * BLOCK
            others_out[t][...] = back[lo : lo + nq * BLOCK].astype(BF16)
        tw_out[...] = dot(hin_ref[...].T, grads)
        tb_out[...] = jnp.broadcast_to(column_sum(grads.astype(F32)), tb_out.shape)


def attend_back(nq, nk, flag, kept, grad, weight):
    hin, q, k, v, e, ot, inv = kept
    width = weight.shape[0]
    qs, ks = nq * BLOCK, nk * BLOCK
    shape = jax.ShapeDtypeStruct
    outs = [shape((qs, width), F32)]
    outs += [shape((qs, width), BF16)] * (nk // nq - 1)
    outs += [shape((width, 3 * width), F32), shape((8, 3 * width), F32)]
    by_pair = lambda *tail: pl.BlockSpec((1,) + tail, lambda p: (p, 0, 0))
    flops = 4 * ks * width * 3 * width + 8 * HEADS * qs * ks * HEAD_DIM * 4
    return pl.pallas_call(
        partial(attend_back_kernel, nq, nk, width),
        grid=(PAIRS,),
        in_specs=[
            SMEM,
            pl.BlockSpec((2, ks, qs), lambda p: (p, 0, 0)),
            by_pair(qs, LANES),
            by_pair(ks, LANES),
            by_pair(ks, LANES),
            by_pair(LANES, qs),
            by_pair(8, qs),
            pl.BlockSpec((qs, LANES), lambda p: (0, p)),
            full(hin.shape),
            full(weight.shape),
        ],
        out_specs=[full(s.shape) for s in outs],
        out_shape=outs,
        scratch_shapes=[
            pltpu.VMEM((ks, LANES), F32),
            pltpu.VMEM((ks, LANES), F32),
            pltpu.VMEM((LANES, ks), BF16),
            pltpu.VMEM((3 * PAIRS, ks, LANES), BF16),
        ],
        compiler_params=params(),
        cost_estimate=pl.CostEstimate(
            flops=flops, bytes_accessed=2 * HEADS * qs * ks, transcendentals=0
        ),
        name="attend_back",
    )(flag, e, q, k, v, ot, inv, grad, hin, weight)


SMALL = 16


def feed_kernel(units, n, chunk, width, valid_ref, *refs):
    total = sum(count for _, count in units)
    u = len(units)
    xs, mixes, refs = refs[:u], refs[u : 2 * u], refs[2 * u :]
    cots, refs = [refs[i * n : (i + 1) * n] for i in range(u)], refs[u * n :]
    mods_ref, mixer_w, mixer_b, hidden_w, hidden_b, output_w, output_b = refs[:7]
    refs = refs[7:]
    outs, refs = [refs[i * n : (i + 1) * n] for i in range(u)], refs[u * n :]
    middle_out, mixed_grad_out, grads_out, slots_out = refs[:4]
    x_scr, mix_scr, cot_scr, ow_acc, hw_acc, mw_acc, ob_acc, hb_acc, mb_acc = refs[4:]
    i = pl.program_id(0)

    @pl.when(i == 0)
    def _():
        for acc in (ow_acc, hw_acc, mw_acc, ob_acc, hb_acc, mb_acc):
            acc[...] = jnp.zeros_like(acc)
        slots_out[...] = jnp.zeros_like(slots_out)

    def in_unit(j):
        low = sum(count for _, count in units[:j])
        return jnp.logical_and(i >= low, i < low + units[j][1])

    for j in range(u):

        @pl.when(in_unit(j))
        def _(j=j):
            x_scr[...] = xs[j][...]
            mix_scr[...] = mixes[j][...]
            for s in range(n):
                cot_scr[pl.ds(s * chunk, chunk), :] = cots[j][s][0]

    mods = mods_ref[pl.ds(i, 1), :]
    gate_one, shift_two, scale_two, gate_two = (
        mods[:, m * width : (m + 1) * width] for m in (2, 3, 4, 5)
    )
    mixed = mix_scr[...]
    branch = dot(mixed, mixer_w[...]) + mixer_b[...]
    middle = x_scr[...].astype(F32) + gate_one * branch
    normed, inverse = layer_norm(middle)
    normed_mid = (normed * (1.0 + scale_two) + shift_two).astype(BF16)
    hidden = dot(normed_mid, hidden_w[...]) + hidden_b[...]
    square = hidden * hidden
    bend = 0.7978845608028654 * 0.044715
    curve = jnp.tanh(hidden * (0.7978845608028654 + bend * square))
    half = 0.5 + 0.5 * curve
    active = (hidden * half).astype(BF16)
    slope = half + (0.5 * hidden) * (1.0 - curve * curve) * (0.7978845608028654 + 3.0 * bend * square)
    output = dot(active, output_w[...]) + output_b[...]
    cot = cot_scr[...].astype(F32)
    if valid_ref is not None:
        cot = cot * valid_ref[0]
    result = (middle + gate_two * output).astype(BF16)
    for j in range(u):

        @pl.when(in_unit(j))
        def _(j=j):
            for s in range(n):
                outs[j][s][0] = result[s * chunk : (s + 1) * chunk]

    output_grad = (gate_two * cot).astype(BF16)
    gate_two_grad = column_sum(cot * output)
    ow_acc[...] += dot(output_grad.T, active)
    ob_acc[...] += column_sum(output_grad.astype(F32))
    active_grad = dot_nt(output_grad, output_w[...])
    hidden_grad_wide = active_grad * slope
    hidden_grad = hidden_grad_wide.astype(BF16)
    hw_acc[...] += dot(normed_mid.T, hidden_grad)
    hb_acc[...] += column_sum(hidden_grad.astype(F32))
    mid_grad = dot_nt(hidden_grad, hidden_w[...])
    scale_two_grad = column_sum(mid_grad * normed)
    shift_two_grad = column_sum(mid_grad)
    middle_grad = cot + norm_back(mid_grad * (1.0 + scale_two), normed, inverse)
    middle_out[...] = middle_grad
    gate_one_grad = column_sum(middle_grad * branch)
    branch_grad = (gate_one * middle_grad).astype(BF16)
    mw_acc[...] += dot(mixed.T, branch_grad)
    mb_acc[...] += column_sum(branch_grad.astype(F32))
    mixed_grad_out[...] = dot_nt(branch_grad, mixer_w[...]).astype(BF16)
    slots_out[pl.ds(i, 1), :] = jnp.concatenate(
        [gate_one_grad, shift_two_grad, scale_two_grad, gate_two_grad], axis=1
    )

    @pl.when(i == total - 1)
    def _():
        ff = ow_acc.shape[1]
        grads_out[:ff, :] = ow_acc[...].T.astype(BF16)
        for j in range(ff // width):
            lo = ff + j * width
            grads_out[lo : lo + width, :] = hw_acc[:, j * width : (j + 1) * width].astype(BF16)
        grads_out[2 * ff : 2 * ff + width, :] = mw_acc[...].astype(BF16)
        rows = [ob_acc[...]]
        rows += [hb_acc[:, j * width : (j + 1) * width] for j in range(ff // width)]
        rows += [mb_acc[...], jnp.zeros((SMALL - 2 - ff // width, width), F32)]
        base = 2 * ff + width
        grads_out[base : base + SMALL, :] = jnp.concatenate(rows, axis=0).astype(BF16)
        rest = grads_out.shape[0] - base - SMALL
        grads_out[base + SMALL :, :] = jnp.zeros((rest, width), BF16)


def feed(units, n, chunk, valid, xs, mixes, cots, mods, weights, grad_rows):
    width, ff = weights[2].shape
    total = sum(count for _, count in units)
    shape = jax.ShapeDtypeStruct
    lows = [sum(count for _, count in units[:j]) for j in range(len(units))]

    def clip(j):
        return lambda i: jnp.clip(i - lows[j], 0, units[j][1] - 1)

    def rows_of(j):
        at = clip(j)
        return pl.BlockSpec((BLOCK, width), lambda i: (at(i), 0))

    def chunks_of(j):
        at = clip(j)
        return pl.BlockSpec((1, chunk, width), lambda i: (at(i), 0, 0))

    unit_ids = range(len(units))
    in_specs = [rows_of(j) for j in unit_ids] * 2
    in_specs += [chunks_of(j) for j in unit_ids for _ in range(n)]
    in_specs += [full(mods.shape)] + [full(w.shape) for w in weights]
    outs, out_specs = [], []
    for j in unit_ids:
        for _ in range(n):
            outs.append(shape((units[j][1], chunk, width), BF16))
            out_specs.append(chunks_of(j))
    outs += [shape((total * BLOCK, width), F32), shape((total * BLOCK, width), BF16)]
    out_specs += [pl.BlockSpec((BLOCK, width), lambda i: (i, 0))] * 2
    outs += [shape((grad_rows, width), BF16), shape((8, 4 * width), F32)]
    out_specs += [full((grad_rows, width)), full((8, 4 * width))]
    kernel = partial(feed_kernel, units, n, chunk, width)
    arrays = [*xs, *mixes, *[c for unit in cots for c in unit], mods, *weights]
    if valid is None:
        kernel = partial(kernel, None)
    else:
        in_specs, arrays = [SMEM] + in_specs, [valid] + arrays
    flops = total * BLOCK * 2 * (6 * width * ff + 3 * width * width)
    found = pl.pallas_call(
        kernel,
        grid=(total,),
        in_specs=in_specs,
        out_specs=out_specs,
        out_shape=outs,
        scratch_shapes=[
            pltpu.VMEM((BLOCK, width), BF16),
            pltpu.VMEM((BLOCK, width), BF16),
            pltpu.VMEM((BLOCK, width), BF16),
            pltpu.VMEM((width, ff), F32),
            pltpu.VMEM((width, ff), F32),
            pltpu.VMEM((width, width), F32),
            pltpu.VMEM((1, width), F32),
            pltpu.VMEM((1, ff), F32),
            pltpu.VMEM((1, width), F32),
        ],
        compiler_params=params(),
        cost_estimate=pl.CostEstimate(flops=flops, bytes_accessed=16 * MIB, transcendentals=0),
        name="feed",
    )(*arrays)
    pieces = [found[j * n : (j + 1) * n] for j in unit_ids]
    return pieces, found[len(units) * n :]


def finish_kernel(units, n, chunk, width, counts, *refs):
    u = len(units)
    xs, owns, refs = refs[:u], refs[u : 2 * u], refs[2 * u :]
    others = []
    for count in counts:
        others.append(refs[:count])
        refs = refs[count:]
    middle_ref, mods_ref, refs = refs[0], refs[1], refs[2:]
    outs, refs = [refs[i * n : (i + 1) * n] for i in range(u)], refs[u * n :]
    slots_out, x_scr, g_scr = refs
    i = pl.program_id(0)

    @pl.when(i == 0)
    def _():
        slots_out[...] = jnp.zeros_like(slots_out)

    def in_unit(j):
        low = sum(count for _, count in units[:j])
        return jnp.logical_and(i >= low, i < low + units[j][1])

    for j in range(u):

        @pl.when(in_unit(j))
        def _(j=j):
            x_scr[...] = xs[j][...]
            grad = owns[j][...]
            for other in others[j]:
                grad = grad + other[...].astype(F32)
            g_scr[...] = grad

    scale_one = mods_ref[pl.ds(i, 1), width : 2 * width]
    normed, inverse = layer_norm(x_scr[...].astype(F32))
    grad = g_scr[...]
    slots_out[pl.ds(i, 1), :] = jnp.concatenate(
        [column_sum(grad), column_sum(grad * normed)], axis=1
    )
    result = middle_ref[...] + norm_back(grad * (1.0 + scale_one), normed, inverse)
    result = result.astype(BF16)
    for j in range(u):

        @pl.when(in_unit(j))
        def _(j=j):
            for s in range(n):
                outs[j][s][0] = result[s * chunk : (s + 1) * chunk]


def finish(units, n, chunk, xs, owns, others, middle, mods):
    width = middle.shape[1]
    total = sum(count for _, count in units)
    shape = jax.ShapeDtypeStruct
    lows = [sum(count for _, count in units[:j]) for j in range(len(units))]

    def clip(j):
        return lambda i: jnp.clip(i - lows[j], 0, units[j][1] - 1)

    def rows_of(j):
        at = clip(j)
        return pl.BlockSpec((BLOCK, width), lambda i: (at(i), 0))

    def chunks_of(j):
        at = clip(j)
        return pl.BlockSpec((1, chunk, width), lambda i: (at(i), 0, 0))

    unit_ids = range(len(units))
    in_specs = [rows_of(j) for j in unit_ids] * 2
    in_specs += [rows_of(j) for j in unit_ids for _ in others[j]]
    in_specs += [pl.BlockSpec((BLOCK, width), lambda i: (i, 0)), full(mods.shape)]
    outs = [shape((units[j][1], chunk, width), BF16) for j in unit_ids for _ in range(n)]
    out_specs = [chunks_of(j) for j in unit_ids for _ in range(n)]
    found = pl.pallas_call(
        partial(finish_kernel, units, n, chunk, width, [len(o) for o in others]),
        grid=(total,),
        in_specs=in_specs,
        out_specs=out_specs + [full((8, 2 * width))],
        out_shape=outs + [shape((8, 2 * width), F32)],
        scratch_shapes=[pltpu.VMEM((BLOCK, width), BF16), pltpu.VMEM((BLOCK, width), F32)],
        compiler_params=params(),
        cost_estimate=pl.CostEstimate(
            flops=total * BLOCK * width * 40, bytes_accessed=total * BLOCK * width * 12, transcendentals=0
        ),
        name="finish",
    )(*xs, *owns, *[o for unit in others for o in unit], middle, mods)
    return [found[j * n : (j + 1) * n] for j in unit_ids], found[-1]


def xor_permute(value, mask, size):
    return lax.ppermute(value, ("rows", "band"), [(i, i ^ mask) for i in range(size)])


def stages_of(rows, bands):
    band_bits = bands.bit_length() - 1
    bits = (rows * bands).bit_length() - 1
    core = band_bits
    rest = [b for b in range(bits) if b != core and b >= core] + [0]
    rest += [b for b in range(1, core)]
    return [[core]] + [rest[i : i + 2] for i in range(0, len(rest), 2)]


def digit_of(me, stage):
    return sum(((me >> b) & 1) << i for i, b in enumerate(stage))


def mask_of(t, stage):
    return sum(((t >> i) & 1) << b for i, b in enumerate(stage))


def reduce_scatter(value, me, stages, size):
    for stage in stages:
        parts = 1 << len(stage)
        rows = value.shape[0] // parts
        digit = digit_of(me, stage)
        received = [
            xor_permute(
                lax.dynamic_slice_in_dim(value, (digit ^ t) * rows, rows, 0), mask_of(t, stage), size
            )
            for t in range(1, parts)
        ]
        mine = lax.dynamic_slice_in_dim(value, digit * rows, rows, 0).astype(F32)
        for part in received:
            mine = mine + part.astype(F32)
        value = mine.astype(BF16)
    return value


def gather_all(value, me, stages, size):
    for stage in reversed(stages):
        parts = 1 << len(stage)
        rows = value.shape[0]
        digit = digit_of(me, stage)
        whole = jnp.zeros((rows * parts,) + value.shape[1:], value.dtype)
        for t in range(parts):
            part = value if t == 0 else xor_permute(value, mask_of(t, stage), size)
            whole = lax.dynamic_update_slice_in_dim(whole, part, (digit ^ t) * rows, 0)
        value = whole
    return value


def body(
    patches,
    condition_table,
    condition_index,
    image_lengths,
    modulate_weight,
    modulate_bias,
    triple_weight,
    query_bias,
    value_bias,
    mixer_weight,
    mixer_bias,
    hidden_weight,
    hidden_bias,
    output_weight,
    output_bias,
    cotangent,
):
    band = lax.axis_index("band")
    n = lax.axis_size("band")
    size = n * lax.axis_size("rows")
    everyone = lax.axis_index(("rows", "band"))
    rows, band_length, width = patches.shape
    ff = hidden_weight.shape[1]
    length = band_length * n
    big = length // 2
    chunk = band_length // (2 * HALF)
    assert length == 2 * HALF * BLOCK
    plan = Plan(rows, n)
    units = plan.units()
    me = band.astype(jnp.int32).reshape(1)
    stages = stages_of(size // n, n)

    def deal(pieces):
        return [
            piece if i % n == 0 else xor_permute(piece, i % n, size) for i, piece in enumerate(pieces)
        ]

    def by_unit(pieces):
        return [pieces[j * n : (j + 1) * n] for j in range(len(units))]

    x_pieces = by_unit(deal(pack(plan, chunk, big, me, image_lengths, patches)))

    is_big = (image_lengths == big).astype(jnp.int32)
    big_count = jnp.sum(is_big, axis=1)
    lead = jnp.sum((jnp.cumsum(is_big, axis=1) == 0).astype(jnp.int32), axis=1)
    start = jnp.where(big_count == 1, lead, 0)
    flags, half_rows, places = [], [], []
    for name, count in units:
        half_row = jnp.minimum(plan.half_row(name, band), plan.halves - 1)
        for t in range(HALF // count):
            first = 0 if name == "whole" else ((band % plan.group) ^ t) * count
            half_rows += [half_row] * count
            places += [first + k for k in range(count)]
        of_row, half = big_count[half_row // 2], half_row % 2
        flags.append(((of_row == 2) | ((of_row == 1) & (half == 0))).astype(jnp.int32).reshape(1))
    half_rows, places = jnp.stack(half_rows), jnp.stack([jnp.asarray(p, jnp.int32) for p in places])
    row_ids, half_ids = half_rows // 2, half_rows % 2
    bigs, starts = big_count[row_ids], start[row_ids]
    single = jnp.where(half_ids == 0, starts, jnp.where(places < starts, places, places + 1))
    slot = jnp.where(bigs == 2, half_ids, jnp.where(bigs == 0, HALF * half_ids + places, single))
    index = condition_index[row_ids, slot]
    choose = (index[:, None] == jnp.arange(condition_table.shape[0], dtype=jnp.int32)).astype(BF16)
    activity = jax.nn.silu(dot(choose, condition_table)).astype(BF16)
    mods = dot(activity, modulate_weight) + modulate_bias.astype(F32)

    wide = lambda v: v.astype(F32).reshape(1, -1)
    attended, xs, mixes = [], [], []
    for j, (name, count) in enumerate(units):
        lo = j * HALF
        others = []
        if count < HALF:
            own = jnp.stack(x_pieces[j], axis=1).reshape(count * BLOCK, width)
            others = [xor_permute(own, t, size) for t in range(1, HALF // count)]
        found = attend(
            n,
            count,
            HALF,
            chunk,
            flags[j],
            x_pieces[j],
            others,
            mods[lo : lo + HALF],
            triple_weight,
            wide(query_bias),
            wide(value_bias),
        )
        xs.append(found[0])
        attended.append(found[1:8])
        mixes.append(found[8])

    if len(units) == 2:
        own_rows = [*range(HALF), *range(HALF, HALF + units[1][1])]
    else:
        own_rows = [*range(units[0][1])]
    total = len(own_rows)
    own_mods = jnp.pad(mods[:total], ((0, 8 - total), (0, 0)))
    valid = None
    if plan.idle:
        valid = (plan.half_row("shared", band) < plan.halves).astype(F32).reshape(1)

    tied = lax.optimization_barrier((cotangent, x_pieces[-1][-1]))
    c_pieces = by_unit(deal(pack(plan, chunk, big, me, image_lengths, tied[0])))

    grad_rows = 2 * ff + width + 128
    weights = [
        mixer_weight,
        wide(mixer_bias),
        hidden_weight,
        wide(hidden_bias),
        output_weight,
        wide(output_bias),
    ]
    out_pieces, (middle_grad, mixed_grad, feed_grads, feed_slots) = feed(
        units, n, chunk, valid, xs, mixes, c_pieces, own_mods, weights, grad_rows
    )
    out_back = [p for unit in out_pieces for p in deal(unit)]
    block_out = unpack(plan, chunk, big, me, image_lengths, out_back, BF16)
    feed_part = reduce_scatter(feed_grads, everyone, stages, size)

    owns, others, triple_grads, triple_sums = [], [], [], []
    lows = [0, HALF] if len(units) == 2 else [0]
    results = {}
    for j in reversed(range(len(units))):
        count = units[j][1]
        grad = mixed_grad[lows[j] * BLOCK : (lows[j] + count) * BLOCK]
        results[j] = attend_back(count, HALF, flags[j], attended[j], grad, triple_weight)
    for j in range(len(units)):
        found = results[j]
        owns.append(found[0])
        others.append([xor_permute(o, t + 1, size) for t, o in enumerate(found[1:-2])])
        triple_grads.append(found[-2])
        triple_sums.append(found[-1])
    triple_grad = sum(triple_grads)
    triple_sum = sum(triple_sums)[:1]
    triple_rows = jnp.concatenate(
        [triple_grad[:, m * width : (m + 1) * width] for m in range(3)]
        + [triple_sum[:, :width], triple_sum[:, 2 * width :], jnp.zeros((126, width), F32)],
        axis=0,
    ).astype(BF16)
    extra = -triple_rows.shape[0] % size
    if extra:
        triple_rows = jnp.pad(triple_rows, ((0, extra), (0, 0)))
    triple_part = reduce_scatter(triple_rows, everyone, stages, size)

    grad_pieces, finish_slots = finish(units, n, chunk, xs, owns, others, middle_grad, own_mods)
    grad_back = [p for unit in grad_pieces for p in deal(unit)]
    patch_grad = unpack(plan, chunk, big, me, image_lengths, grad_back, F32)

    slots = jnp.concatenate([finish_slots[:total], feed_slots[:total]], axis=1).astype(BF16)
    slots = gather_all(jnp.concatenate([slots, activity[:total]], axis=1), everyone, stages, size)
    slot_grads, activities = slots[:, : 6 * width], slots[:, 6 * width :]
    modulate_w_grad = lax.dot_general(
        activities, slot_grads, (((0,), (0,)), ((), ())), preferred_element_type=F32
    )
    modulate_b_grad = jnp.sum(slot_grads.astype(F32), axis=0)

    feed_all = gather_all(feed_part, everyone, stages, size).astype(F32)
    triple_all = gather_all(triple_part, everyone, stages, size).astype(F32)
    base = 2 * ff + width
    hidden_w_grad = jnp.concatenate(
        [feed_all[ff + j * width : ff + (j + 1) * width] for j in range(ff // width)], axis=1
    )
    triple_w_grad = jnp.concatenate(
        [triple_all[m * width : (m + 1) * width] for m in range(3)], axis=1
    )
    return (
        block_out,
        patch_grad,
        modulate_w_grad,
        modulate_b_grad,
        triple_w_grad,
        triple_all[3 * width],
        triple_all[3 * width + 1],
        feed_all[2 * ff : base],
        feed_all[base + 1 + ff // width],
        hidden_w_grad,
        feed_all[base + 1 : base + 1 + ff // width].reshape(-1),
        feed_all[:ff],
        feed_all[base],
    )


def solution(mesh):
    return jax.shard_map(
        body,
        mesh=mesh,
        in_specs=(
            P("rows", None, "band"),
            P(),
            P("rows", None),
            P("rows", None),
            P(),
            P(),
            P(),
            P(),
            P(),
            P(),
            P(),
            P(),
            P(),
            P(),
            P(),
            P("rows", None, "band"),
        ),
        out_specs=(
            P("rows", None, "band"),
            P("rows", None, "band"),
            P(),
            P(),
            P(),
            P(),
            P(),
            P(),
            P(),
            P(),
            P(),
            P(),
            P(),
        ),
        check_vma=False,
    )
```

time: 2610 us -> 382 us (0.15)
  waiting for transfers between devices: 1690 us -> 57.7 us
  matrix products: 529 us -> 5.28 us
  starting transfers between devices: 1.36 us -> 142 us
  local copies, waits for them, and re-layouts: 171 us -> 34.1 us
  other arithmetic: 135 us -> 11.6 us
  Pallas kernels: 0 us -> 120 us
  blocking collectives: 41.1 us -> 0 us
    all_gather x24 -> x0, waiting for transfers between devices: 899 us -> none  [the longest x6 245 us: gather_again(): lax.all_gather(keys, 'band', axis=0, tiled=True)]
    reduce_scatter x12 -> x0, waiting for transfers between devices: 607 us -> none  [the longest x6 410 us: backward_step(): lax.psum_scatter(key_term.astype(jnp.bfloat16), 'band', scatter_dimension...]
    dot_general x136 -> x3, matrix products: 425 us -> 5.28 us  [the longest x2 2.81 us: dot(): return jnp.dot(left, right, preferred_element_type=F32)]
    psum x1 -> x0, waiting for transfers between devices: 183 us -> none  [body(): lax.psum((modulate_w_grad, modulate_b_grad, totals[0], totals[1], totals[...]
    ppermute x0 -> x93, starting transfers between devices: none -> 142 us  [xor_permute(): lax.ppermute(value, ('rows', 'band'), [(i, i ^ mask) for i in range(size)])]
    pallas_call x0 -> x10, Pallas kernels: none -> 120 us  [the longest x2 38.1 us: attend(): pl.pallas_call(partial(attend_kernel, n, nq, nk, chunk, width), grid=(PAI...]
    sub x12 -> x0, matrix products: 104 us -> none  [probabilities(): exps = jnp.exp(scores - maxima)]
    ppermute x0 -> x93, waiting for transfers between devices: none -> 57.7 us  [xor_permute(): lax.ppermute(value, ('rows', 'band'), [(i, i ^ mask) for i in range(size)])]
  transfers between devices with their start and end apart: 37 -> 93, of which waited for: 37 -> 30; matrix products, arithmetic and copies ran while one was open for 14% -> 9% of each run, Pallas kernels for 0% -> 23%
where the time goes in v1:
time: 382 us; the launch traced here: 376 us
  starting transfers between devices  142 us (37%)
  Pallas kernels  120 us (31%)
  waiting for transfers between devices  57.7 us (15%)
  local copies, waits for them, and re-layouts  34.1 us (9%)
  other arithmetic  11.6 us (3%)
  matrix products  5.28 us (1%)
  between operations  5.1 us (1%)
    ppermute x93, starting transfers between devices, xor_permute(): lax.ppermute(value, ('rows', 'band'), [(i, i ^ mask) for i in range(size)])  142 us
    ppermute x93, waiting for transfers between devices, xor_permute(): lax.ppermute(value, ('rows', 'band'), [(i, i ^ mask) for i in range(size)])  57.7 us
    pallas_call x2, Pallas kernels, attend(): pl.pallas_call(partial(attend_kernel, n, nq, nk, chunk, width), grid=(PAI...  38.1 us
    pallas_call x2, Pallas kernels, attend_back(): pl.pallas_call(partial(attend_back_kernel, nq, nk, width), grid=(PAIRS,),...  35.3 us
    pallas_call x1, Pallas kernels, feed(): pl.pallas_call(kernel, grid=(total,), in_specs=in_specs, out_specs=out_sp...  31.7 us
    unnamed x137, local copies, waits for them, and re-layouts  8.42 us
  transfers between devices with their start and end apart: 93, of which 30 were waited for; matrix products, arithmetic and copies ran while one was open for 9% of the time, Pallas kernels for 23%

profile of v1, /device:TPU:0, one launch (start us, length us, event | category | flops | bytes accessed | tf_op | source)
XLA Modules:
  0.0 376.5 jit_solution(10184888951147119103)
XLA Ops:
  7.8 2.9 collective-permute-start
  34.9 3.1 collective-permute-start.10
  39.3 2.6 collective-permute-start.11
  41.9 3.7 collective-permute-start.12
  46.0 2.8 collective-permute-start.13
  49.0 3.9 %collective-permute-done.13.refs_7_ = bf16[2,32,384]{2,1,0:T(8,128)(2,1)S(1)} collective-permute-done((bf16[2,32,384]{2,1,0:T(8,128)(2,1)S(1)}, bf16[2,32,384]{2,1,0:T(8,128)(2,1)S(1)}, u32[]{:S(2)}, u32[]{:S(2)}) %collective-permute-start.13) | collective-permute-done | bytes 49184 | tf_op jit(solution)/shard_map/ppermute | solution.py:651
  53.2 2.5 collective-permute-start.5
  55.7 2.1 collective-permute-start.6
  61.7 2.6 collective-permute-done.4.refs_5_
  64.5 2.8 collective-permute-start.25
  67.3 2.7 collective-permute-start.26
  72.5 2.8 collective-permute-start.27
  77.2 27.5 %attend.2 = (bf16[1024,384]{1,0:T(8,128)(2,1)}, bf16[1024,384]{1,0:T(8,128)(2,1)}, bf16[3,1024,128]{2,1,0:T(8,128)(2,1)}, bf16[3,1024,128]{2,1,0:T(8,128)(2,1)},...) custom-call(s32[1]{0:T(128)} %bitcast.3.flag_ref, ...), custom_call_target="tpu_custom_call" | custom-call | flops 7348420608 | bytes 12582912 | tf_op jit(solution)/shard_map/attend/pallas_call | solution.py:273
  105.2 5.2 %collective-permute-start.20 = (bf16[4,32,384]{2,1,0:T(8,128)(2,1)S(1)}, bf16[4,32,384]{2,1,0:T(8,128)(2,1)S(1)}, u32[]{:S(2)}, u32[]{:S(2)}) collective-permute-start(bf16[4,32,384]{2,1,0:T(8,128)(2,1)S(1)} %get-tuple-element.135), channel_id=1, source_target_pairs={{0,6},{1,7},{2,4},{3,5},{4,2},{5,3},{6,0},{7,1},{8,14},{9,15},{10,... | collective-permute-start | bytes 294920 | tf_op jit(solution)/shard_map/ppermute | solution.py:651
  110.3 2.4 collective-permute-start.21
  112.7 10.6 %attend.3 = (bf16[1024,384]{1,0:T(8,128)(2,1)}, bf16[1024,384]{1,0:T(8,128)(2,1)}, bf16[3,512,128]{2,1,0:T(8,128)(2,1)}, bf16[3,1024,128]{2,1,0:T(8,128)(2,1)}, ...) custom-call(s32[1]{0:T(128)} %bitcast.17.flag_ref, ...), custom_call_target="tpu_custom_call" | custom-call | flops 4127195136 | bytes 6291456 | tf_op jit(solution)/shard_map/attend/pallas_call | solution.py:273
  124.1 31.7 %feed.1 = (bf16[4,32,384]{2,1,0:T(8,128)(2,1)}, bf16[4,32,384]{2,1,0:T(8,128)(2,1)}, bf16[4,32,384]{2,1,0:T(8,128)(2,1)}, bf16[4,32,384]{2,1,0:T(8,128)(2,1)}, b...) custom-call(bf16[1024,384]{1,0:T(8,128)(2,1)} %get-tuple-element.116, ...), custom_call_target="tpu_custom_call" | custom-call | flops 12230590464 | bytes 16777216 | tf_op jit(solution)/shard_map/feed/pallas_call | solution.py:540
  155.9 2.1 slice.98.refs_6_
  163.3 5.7 %collective-permute-start.39 = (bf16[2,32,384]{2,1,0:T(8,128)(2,1)}, bf16[2,32,384]{2,1,0:T(8,128)(2,1)S(1)}, u32[]{:S(2)}, u32[]{:S(2)}) collective-permute-start(bf16[2,32,384]{2,1,0:T(8,128)(2,1)} %get-tuple-element.157), channel_id=1, source_target_pairs={{0,4},{1,5},{2,6},{3,7},{4,0},{5,1},{6,2},{7,3},{8,12},{9,13},{10,... | collective-permute-start | bytes 147464 | tf_op jit(solution)/shard_map/ppermute | solution.py:651
  168.9 11.7 %attend_back.3 = (f32[512,384]{1,0:T(8,128)}, bf16[512,384]{1,0:T(8,128)(2,1)}, f32[384,1152]{1,0:T(8,128)}, f32[8,1152]{1,0:T(8,128)}) custom-call(s32[1]{0:T(128)} %bitcast.17.flag_ref, bf16[6,1024,512]{2,1,0:T(8,128)(2,1)} %get-tuple-element.170.refs_0_, bf16[3,512,128]{2,1,0:T(8,128)(2,1)} %get-tuple-element.171.refs_1_, ...), custom_call_target="tpu_custom_call" | custom-call | flops 8254390272 | bytes 6291456 | tf_op jit(solution)/shard_map/attend_back/pallas_call | solution.py:370
  181.5 23.6 %attend_back.2 = (f32[1024,384]{1,0:T(8,128)}, f32[384,1152]{1,0:T(8,128)}, f32[8,1152]{1,0:T(8,128)}) custom-call(s32[1]{0:T(128)} %bitcast.3.flag_ref, bf16[6,1024,1024]{2,1,0:T(8,128)(2,1)} %get-tuple-element.161.refs_0_, bf16[3,1024,128]{2,1,0:T(8,128)(2,1)} %get-tuple-element.162.refs_1_, bf16[3,1024,128]{2,1,0:T(8,128)(2,1)} %get-tuple-element.163.refs_2_, ...), custom_call_target="tpu_custom_call" | custom-call | flops 14696841216 | bytes 12582912 | tf_op jit(solution)/shard_map/attend_back/pallas_call | solution.py:370
  208.9 7.0 %finish.1 = (bf16[4,32,384]{2,1,0:T(8,128)(2,1)}, bf16[4,32,384]{2,1,0:T(8,128)(2,1)}, bf16[4,32,384]{2,1,0:T(8,128)(2,1)}, bf16[4,32,384]{2,1,0:T(8,128)(2,1)},...) custom-call(bf16[1024,384]{1,0:T(8,128)(2,1)} %get-tuple-element.116, ...), custom_call_target="tpu_custom_call" | custom-call | flops 23592960 | bytes 7077888 | tf_op jit(solution)/shard_map/finish/pallas_call | solution.py:634
  216.6 4.7 %collective-permute-start.29 = (bf16[4,32,384]{2,1,0:T(8,128)(2,1)S(1)}, bf16[4,32,384]{2,1,0:T(8,128)(2,1)S(1)}, u32[]{:S(2)}, u32[]{:S(2)}) collective-permute-start(bf16[4,32,384]{2,1,0:T(8,128)(2,1)S(1)} %copy-done.39), channel_id=1, source_target_pairs={{0,1},{1,0},{2,3},{3,2},{4,5},{5,4},{6,7},{7,6},{8,9},{9,8},{10,11... | collective-permute-start | bytes 294920 | tf_op jit(solution)/shard_map/ppermute | solution.py:651
  222.9 5.2 %collective-permute-start.42 = (bf16[2,32,384]{2,1,0:T(8,128)(2,1)S(1)}, bf16[2,32,384]{2,1,0:T(8,128)(2,1)S(1)}, u32[]{:S(2)}, u32[]{:S(2)}) collective-permute-start(bf16[2,32,384]{2,1,0:T(8,128)(2,1)S(1)} %copy-done.58), channel_id=1, source_target_pairs={{0,7},{1,6},{2,5},{3,4},{4,3},{5,2},{6,1},{7,0},{8,15},{9,14},{10,... | collective-permute-start | bytes 147464 | tf_op jit(solution)/shard_map/ppermute | solution.py:651
  230.7 2.4 collective-permute-start.33
  234.3 2.3 collective-permute-start.35
  243.1 3.9 %collective-permute-start.52 = (bf16[2,32,384]{2,1,0:T(8,128)(2,1)}, bf16[2,32,384]{2,1,0:T(8,128)(2,1)S(1)}, u32[]{:S(2)}, u32[]{:S(2)}) collective-permute-start(bf16[2,32,384]{2,1,0:T(8,128)(2,1)} %get-tuple-element.190), channel_id=1, source_target_pairs={{0,2},{1,3},{2,0},{3,1},{4,6},{5,7},{6,4},{7,5},{8,10},{9,11},{10,... | collective-permute-start | bytes 147464 | tf_op jit(solution)/shard_map/ppermute | solution.py:651
  248.3 2.3 unpack.2
  252.1 2.5 collective-permute-start.54
  256.5 2.3 collective-permute-start.56
  265.0 3.9 %collective-permute-start.61 = (bf16[24,2688]{1,0:T(8,128)(2,1)S(1)}, bf16[24,2688]{1,0:T(8,128)(2,1)S(1)}, u32[]{:S(2)}, u32[]{:S(2)}) collective-permute-start(bf16[24,2688]{1,0:T(8,128)(2,1)S(1)} %dynamic_update_slice.93), channel_id=1, source_target_pairs={{0,16},{1,17},{2,18},{3,19},{4,20},{5,21},{6,22},{7,23},{8,24},{9,... | collective-permute-start | bytes 387080 | tf_op jit(solution)/shard_map/ppermute | solution.py:651
  270.2 3.7 collective-permute-start.48
  275.3 2.6 collective-permute-start.50
  277.9 3.1 collective-permute-done.47.refs_4_
  280.9 3.7 collective-permute-done.48.refs_5_
  285.6 3.6 collective-permute-start.63
  289.2 2.6 unpack.3
  292.9 2.4 collective-permute-start.66
  309.9 2.2 collective-permute-done.73
  322.9 5.1 %collective-permute-done.82 = bf16[448,384]{1,0:T(8,128)(2,1)S(1)} collective-permute-done((bf16[448,384]{1,0:T(8,128)(2,1)S(1)}, bf16[448,384]{1,0:T(8,128)(2,1)S(1)}, u32[]{:S(2)}, u32[]{:S(2)}) %collective-permute-start.82) | collective-permute-done | bytes 344096 | tf_op jit(solution)/shard_map/ppermute | solution.py:651
  328.0 2.8 collective-permute-done.81
  333.6 2.6 collective-permute-start.83
  342.8 2.1 collective-permute-start.88
  345.4 2.8 collective-permute-done.87
  353.8 5.6 %collective-permute-done.89 = bf16[448,384]{1,0:T(8,128)(2,1)S(1)} collective-permute-done((bf16[448,384]{1,0:T(8,128)(2,1)S(1)}, bf16[448,384]{1,0:T(8,128)(2,1)S(1)}, u32[]{:S(2)}, u32[]{:S(2)}) %collective-permute-start.89) | collective-permute-done | bytes 344096 | tf_op jit(solution)/shard_map/ppermute | solution.py:651
  359.5 3.6 collective-permute-done.91
  363.2 2.5 fusion
  373.1 2.9 pad_maximum_fusion
  (383 shorter events, 126.3 us)
Async XLA Ops:
  7.8 45.3 %collective-permute-start = (bf16[4,32,384]{2,1,0:T(8,128)(2,1)}, bf16[4,32,384]{2,1,0:T(8,128)(2,1)}, u32[]{:S(2)}, u32[]{:S(2)}) collective-permute-start(bf16[4,32,384]{2,1,0:T(8,128)(2,1)} %get-tuple-element.109), channel_id=1, source_target_pairs={{0,1},{1,0},{2,3},{3,2},{4,5},{5,4},{6,7},{7,6},{8,9},{9,8},{10,11... | collective-permute-start | bytes 294920 | tf_op jit(solution)/shard_map/ppermute | solution.py:651
  10.8 44.9 %collective-permute-start.1 = (bf16[4,32,384]{2,1,0:T(8,128)(2,1)}, bf16[4,32,384]{2,1,0:T(8,128)(2,1)}, u32[]{:S(2)}, u32[]{:S(2)}) collective-permute-start(bf16[4,32,384]{2,1,0:T(8,128)(2,1)} %get-tuple-element.110), channel_id=1, source_target_pairs={{0,2},{1,3},{2,0},{3,1},{4,6},{5,7},{6,4},{7,5},{8,10},{9,11},{10,... | collective-permute-start | bytes 294920 | tf_op jit(solution)/shard_map/ppermute | solution.py:651
  12.3 46.8 %collective-permute-start.2 = (bf16[4,32,384]{2,1,0:T(8,128)(2,1)S(1)}, bf16[4,32,384]{2,1,0:T(8,128)(2,1)}, u32[]{:S(2)}, u32[]{:S(2)}) collective-permute-start(bf16[4,32,384]{2,1,0:T(8,128)(2,1)S(1)} %get-tuple-element.111), channel_id=1, source_target_pairs={{0,3},{1,2},{2,1},{3,0},{4,7},{5,6},{6,5},{7,4},{8,11},{9,10},{10,... | collective-permute-start | bytes 294920 | tf_op jit(solution)/shard_map/ppermute | solution.py:651
  12.3 21.7 %collective-permute-start.7 = (bf16[2,32,384]{2,1,0:T(8,128)(2,1)}, bf16[2,32,384]{2,1,0:T(8,128)(2,1)}, u32[]{:S(2)}, u32[]{:S(2)}) collective-permute-start(bf16[2,32,384]{2,1,0:T(8,128)(2,1)} %get-tuple-element.118), channel_id=1, source_target_pairs={{0,1},{1,0},{2,3},{3,2},{4,5},{5,4},{6,7},{7,6},{8,9},{9,8},{10,11... | collective-permute-start | bytes 147464 | tf_op jit(solution)/shard_map/ppermute | solution.py:651
  14.3 20.6 %collective-permute-start.8 = (bf16[2,32,384]{2,1,0:T(8,128)(2,1)}, bf16[2,32,384]{2,1,0:T(8,128)(2,1)}, u32[]{:S(2)}, u32[]{:S(2)}) collective-permute-start(bf16[2,32,384]{2,1,0:T(8,128)(2,1)} %get-tuple-element.119), channel_id=1, source_target_pairs={{0,2},{1,3},{2,0},{3,1},{4,6},{5,7},{6,4},{7,5},{8,10},{9,11},{10,... | collective-permute-start | bytes 147464 | tf_op jit(solution)/shard_map/ppermute | solution.py:651
  48.9 11.8 %collective-permute-start.3 = (bf16[4,32,384]{2,1,0:T(8,128)(2,1)S(1)}, bf16[4,32,384]{2,1,0:T(8,128)(2,1)S(1)}, u32[]{:S(2)}, u32[]{:S(2)}) collective-permute-start(bf16[4,32,384]{2,1,0:T(8,128)(2,1)S(1)} %get-tuple-element.112), channel_id=1, source_target_pairs={{0,4},{1,5},{2,6},{3,7},{4,0},{5,1},{6,2},{7,3},{8,12},{9,13},{10,... | collective-permute-start | bytes 294920 | tf_op jit(solution)/shard_map/ppermute | solution.py:651
  52.9 11.5 %collective-permute-start.4 = (bf16[4,32,384]{2,1,0:T(8,128)(2,1)S(1)}, bf16[4,32,384]{2,1,0:T(8,128)(2,1)S(1)}, u32[]{:S(2)}, u32[]{:S(2)}) collective-permute-start(bf16[4,32,384]{2,1,0:T(8,128)(2,1)S(1)} %get-tuple-element.113), channel_id=1, source_target_pairs={{0,5},{1,4},{2,7},{3,6},{4,1},{5,0},{6,3},{7,2},{8,13},{9,12},{10,... | collective-permute-start | bytes 294920 | tf_op jit(solution)/shard_map/ppermute | solution.py:651
  53.2 11.3 %collective-permute-start.5 = (bf16[4,32,384]{2,1,0:T(8,128)(2,1)S(1)}, bf16[4,32,384]{2,1,0:T(8,128)(2,1)S(1)}, u32[]{:S(2)}, u32[]{:S(2)}) collective-permute-start(bf16[4,32,384]{2,1,0:T(8,128)(2,1)S(1)} %get-tuple-element.114), channel_id=1, source_target_pairs={{0,6},{1,7},{2,4},{3,5},{4,2},{5,3},{6,0},{7,1},{8,14},{9,15},{10,... | collective-permute-start | bytes 294920 | tf_op jit(solution)/shard_map/ppermute | solution.py:651
  55.7 11.6 %collective-permute-start.6 = (bf16[4,32,384]{2,1,0:T(8,128)(2,1)S(1)}, bf16[4,32,384]{2,1,0:T(8,128)(2,1)S(1)}, u32[]{:S(2)}, u32[]{:S(2)}) collective-permute-start(bf16[4,32,384]{2,1,0:T(8,128)(2,1)S(1)} %get-tuple-element.115), channel_id=1, source_target_pairs={{0,7},{1,6},{2,5},{3,4},{4,3},{5,2},{6,1},{7,0},{8,15},{9,14},{10,... | collective-permute-start | bytes 294920 | tf_op jit(solution)/shard_map/ppermute | solution.py:651
  60.6 11.1 %collective-permute-start.23 = (bf16[2,32,384]{2,1,0:T(8,128)(2,1)S(1)}, bf16[2,32,384]{2,1,0:T(8,128)(2,1)S(1)}, u32[]{:S(2)}, u32[]{:S(2)}) collective-permute-start(bf16[2,32,384]{2,1,0:T(8,128)(2,1)S(1)} %get-tuple-element.139), channel_id=1, source_target_pairs={{0,2},{1,3},{2,0},{3,1},{4,6},{5,7},{6,4},{7,5},{8,10},{9,11},{10,... | collective-permute-start | bytes 147464 | tf_op jit(solution)/shard_map/ppermute | solution.py:651
  70.0 40.3 %collective-permute-start.14 = (bf16[512,384]{1,0:T(8,128)(2,1)S(1)}, bf16[512,384]{1,0:T(8,128)(2,1)S(1)}, u32[]{:S(2)}, u32[]{:S(2)}) collective-permute-start(bf16[512,384]{1,0:T(8,128)(2,1)S(1)} %bitcast.52), channel_id=1, source_target_pairs={{0,1},{1,0},{2,3},{3,2},{4,5},{5,4},{6,7},{7,6},{8,9},{9,8},{10,11... | collective-permute-start | bytes 1179656 | tf_op jit(solution)/shard_map/ppermute | solution.py:651
  71.8 33.4 %collective-permute-start.15 = (bf16[4,32,384]{2,1,0:T(8,128)(2,1)S(1)}, bf16[4,32,384]{2,1,0:T(8,128)(2,1)S(1)}, u32[]{:S(2)}, u32[]{:S(2)}) collective-permute-start(bf16[4,32,384]{2,1,0:T(8,128)(2,1)S(1)} %get-tuple-element.130), channel_id=1, source_target_pairs={{0,1},{1,0},{2,3},{3,2},{4,5},{5,4},{6,7},{7,6},{8,9},{9,8},{10,11... | collective-permute-start | bytes 294920 | tf_op jit(solution)/shard_map/ppermute | solution.py:651
  72.1 33.0 %collective-permute-start.16 = (bf16[4,32,384]{2,1,0:T(8,128)(2,1)S(1)}, bf16[4,32,384]{2,1,0:T(8,128)(2,1)S(1)}, u32[]{:S(2)}, u32[]{:S(2)}) collective-permute-start(bf16[4,32,384]{2,1,0:T(8,128)(2,1)S(1)} %get-tuple-element.131), channel_id=1, source_target_pairs={{0,2},{1,3},{2,0},{3,1},{4,6},{5,7},{6,4},{7,5},{8,10},{9,11},{10,... | collective-permute-start | bytes 294920 | tf_op jit(solution)/shard_map/ppermute | solution.py:651
  72.5 32.4 %collective-permute-start.27 = (bf16[2,32,384]{2,1,0:T(8,128)(2,1)S(1)}, bf16[2,32,384]{2,1,0:T(8,128)(2,1)S(1)}, u32[]{:S(2)}, u32[]{:S(2)}) collective-permute-start(bf16[2,32,384]{2,1,0:T(8,128)(2,1)S(1)} %get-tuple-element.143), channel_id=1, source_target_pairs={{0,6},{1,7},{2,4},{3,5},{4,2},{5,3},{6,0},{7,1},{8,14},{9,15},{10,... | collective-permute-start | bytes 147464 | tf_op jit(solution)/shard_map/ppermute | solution.py:651
  75.3 29.6 %collective-permute-start.28 = (bf16[2,32,384]{2,1,0:T(8,128)(2,1)S(1)}, bf16[2,32,384]{2,1,0:T(8,128)(2,1)S(1)}, u32[]{:S(2)}, u32[]{:S(2)}) collective-permute-start(bf16[2,32,384]{2,1,0:T(8,128)(2,1)S(1)} %get-tuple-element.144), channel_id=1, source_target_pairs={{0,7},{1,6},{2,5},{3,4},{4,3},{5,2},{6,1},{7,0},{8,15},{9,14},{10,... | collective-permute-start | bytes 147464 | tf_op jit(solution)/shard_map/ppermute | solution.py:651
  104.9 18.5 %collective-permute-start.17 = (bf16[4,32,384]{2,1,0:T(8,128)(2,1)S(1)}, bf16[4,32,384]{2,1,0:T(8,128)(2,1)S(1)}, u32[]{:S(2)}, u32[]{:S(2)}) collective-permute-start(bf16[4,32,384]{2,1,0:T(8,128)(2,1)S(1)} %get-tuple-element.132), channel_id=1, source_target_pairs={{0,3},{1,2},{2,1},{3,0},{4,7},{5,6},{6,5},{7,4},{8,11},{9,10},{10,... | collective-permute-start | bytes 294920 | tf_op jit(solution)/shard_map/ppermute | solution.py:651
  105.0 18.4 %collective-permute-start.18 = (bf16[4,32,384]{2,1,0:T(8,128)(2,1)S(1)}, bf16[4,32,384]{2,1,0:T(8,128)(2,1)S(1)}, u32[]{:S(2)}, u32[]{:S(2)}) collective-permute-start(bf16[4,32,384]{2,1,0:T(8,128)(2,1)S(1)} %get-tuple-element.133), channel_id=1, source_target_pairs={{0,4},{1,5},{2,6},{3,7},{4,0},{5,1},{6,2},{7,3},{8,12},{9,13},{10,... | collective-permute-start | bytes 294920 | tf_op jit(solution)/shard_map/ppermute | solution.py:651
  105.1 18.3 %collective-permute-start.19 = (bf16[4,32,384]{2,1,0:T(8,128)(2,1)S(1)}, bf16[4,32,384]{2,1,0:T(8,128)(2,1)S(1)}, u32[]{:S(2)}, u32[]{:S(2)}) collective-permute-start(bf16[4,32,384]{2,1,0:T(8,128)(2,1)S(1)} %get-tuple-element.134), channel_id=1, source_target_pairs={{0,5},{1,4},{2,7},{3,6},{4,1},{5,0},{6,3},{7,2},{8,13},{9,12},{10,... | collective-permute-start | bytes 294920 | tf_op jit(solution)/shard_map/ppermute | solution.py:651
  105.2 18.2 %collective-permute-start.20 = (bf16[4,32,384]{2,1,0:T(8,128)(2,1)S(1)}, bf16[4,32,384]{2,1,0:T(8,128)(2,1)S(1)}, u32[]{:S(2)}, u32[]{:S(2)}) collective-permute-start(bf16[4,32,384]{2,1,0:T(8,128)(2,1)S(1)} %get-tuple-element.135), channel_id=1, source_target_pairs={{0,6},{1,7},{2,4},{3,5},{4,2},{5,3},{6,0},{7,1},{8,14},{9,15},{10,... | collective-permute-start | bytes 294920 | tf_op jit(solution)/shard_map/ppermute | solution.py:651
  110.3 13.1 %collective-permute-start.21 = (bf16[4,32,384]{2,1,0:T(8,128)(2,1)S(1)}, bf16[4,32,384]{2,1,0:T(8,128)(2,1)S(1)}, u32[]{:S(2)}, u32[]{:S(2)}) collective-permute-start(bf16[4,32,384]{2,1,0:T(8,128)(2,1)S(1)} %get-tuple-element.136), channel_id=1, source_target_pairs={{0,7},{1,6},{2,5},{3,4},{4,3},{5,2},{6,1},{7,0},{8,15},{9,14},{10,... | collective-permute-start | bytes 294920 | tf_op jit(solution)/shard_map/ppermute | solution.py:651
  159.8 56.8 %collective-permute-start.36 = (bf16[2,32,384]{2,1,0:T(8,128)(2,1)}, bf16[2,32,384]{2,1,0:T(8,128)(2,1)S(1)}, u32[]{:S(2)}, u32[]{:S(2)}) collective-permute-start(bf16[2,32,384]{2,1,0:T(8,128)(2,1)} %get-tuple-element.154), channel_id=1, source_target_pairs={{0,1},{1,0},{2,3},{3,2},{4,5},{5,4},{6,7},{7,6},{8,9},{9,8},{10,11... | collective-permute-start | bytes 147464 | tf_op jit(solution)/shard_map/ppermute | solution.py:651
  159.8 61.6 %collective-permute-start.37 = (bf16[2,32,384]{2,1,0:T(8,128)(2,1)}, bf16[2,32,384]{2,1,0:T(8,128)(2,1)S(1)}, u32[]{:S(2)}, u32[]{:S(2)}) collective-permute-start(bf16[2,32,384]{2,1,0:T(8,128)(2,1)} %get-tuple-element.155), channel_id=1, source_target_pairs={{0,2},{1,3},{2,0},{3,1},{4,6},{5,7},{6,4},{7,5},{8,10},{9,11},{10,... | collective-permute-start | bytes 147464 | tf_op jit(solution)/shard_map/ppermute | solution.py:651
  161.4 60.0 %collective-permute-start.38 = (bf16[2,32,384]{2,1,0:T(8,128)(2,1)}, bf16[2,32,384]{2,1,0:T(8,128)(2,1)S(1)}, u32[]{:S(2)}, u32[]{:S(2)}) collective-permute-start(bf16[2,32,384]{2,1,0:T(8,128)(2,1)} %get-tuple-element.156), channel_id=1, source_target_pairs={{0,3},{1,2},{2,1},{3,0},{4,7},{5,6},{6,5},{7,4},{8,11},{9,10},{10,... | collective-permute-start | bytes 147464 | tf_op jit(solution)/shard_map/ppermute | solution.py:651
  163.3 59.7 %collective-permute-start.39 = (bf16[2,32,384]{2,1,0:T(8,128)(2,1)}, bf16[2,32,384]{2,1,0:T(8,128)(2,1)S(1)}, u32[]{:S(2)}, u32[]{:S(2)}) collective-permute-start(bf16[2,32,384]{2,1,0:T(8,128)(2,1)} %get-tuple-element.157), channel_id=1, source_target_pairs={{0,4},{1,5},{2,6},{3,7},{4,0},{5,1},{6,2},{7,3},{8,12},{9,13},{10,... | collective-permute-start | bytes 147464 | tf_op jit(solution)/shard_map/ppermute | solution.py:651
  180.6 27.1 %collective-permute-start.43 = (bf16[512,384]{1,0:T(8,128)(2,1)}, bf16[512,384]{1,0:T(8,128)(2,1)S(1)}, u32[]{:S(2)}, u32[]{:S(2)}) collective-permute-start(bf16[512,384]{1,0:T(8,128)(2,1)} %get-tuple-element.178), channel_id=1, source_target_pairs={{0,1},{1,0},{2,3},{3,2},{4,5},{5,4},{6,7},{7,6},{8,9},{9,8},{10,11... | collective-permute-start | bytes 1179656 | tf_op jit(solution)/shard_map/ppermute | solution.py:651
  207.7 15.2 %collective-permute-start.40 = (bf16[2,32,384]{2,1,0:T(8,128)(2,1)}, bf16[2,32,384]{2,1,0:T(8,128)(2,1)S(1)}, u32[]{:S(2)}, u32[]{:S(2)}) collective-permute-start(bf16[2,32,384]{2,1,0:T(8,128)(2,1)} %get-tuple-element.158), channel_id=1, source_target_pairs={{0,5},{1,4},{2,7},{3,6},{4,1},{5,0},{6,3},{7,2},{8,13},{9,12},{10,... | collective-permute-start | bytes 147464 | tf_op jit(solution)/shard_map/ppermute | solution.py:651
  216.6 16.5 %collective-permute-start.29 = (bf16[4,32,384]{2,1,0:T(8,128)(2,1)S(1)}, bf16[4,32,384]{2,1,0:T(8,128)(2,1)S(1)}, u32[]{:S(2)}, u32[]{:S(2)}) collective-permute-start(bf16[4,32,384]{2,1,0:T(8,128)(2,1)S(1)} %copy-done.39), channel_id=1, source_target_pairs={{0,1},{1,0},{2,3},{3,2},{4,5},{5,4},{6,7},{7,6},{8,9},{9,8},{10,11... | collective-permute-start | bytes 294920 | tf_op jit(solution)/shard_map/ppermute | solution.py:651
  221.4 12.9 %collective-permute-start.30 = (bf16[4,32,384]{2,1,0:T(8,128)(2,1)S(1)}, bf16[4,32,384]{2,1,0:T(8,128)(2,1)S(1)}, u32[]{:S(2)}, u32[]{:S(2)}) collective-permute-start(bf16[4,32,384]{2,1,0:T(8,128)(2,1)S(1)} %copy-done.38), channel_id=1, source_target_pairs={{0,2},{1,3},{2,0},{3,1},{4,6},{5,7},{6,4},{7,5},{8,10},{9,11},{10,... | collective-permute-start | bytes 294920 | tf_op jit(solution)/shard_map/ppermute | solution.py:651
  221.4 15.2 %collective-permute-start.31 = (bf16[4,32,384]{2,1,0:T(8,128)(2,1)S(1)}, bf16[4,32,384]{2,1,0:T(8,128)(2,1)S(1)}, u32[]{:S(2)}, u32[]{:S(2)}) collective-permute-start(bf16[4,32,384]{2,1,0:T(8,128)(2,1)S(1)} %copy-done.37), channel_id=1, source_target_pairs={{0,3},{1,2},{2,1},{3,0},{4,7},{5,6},{6,5},{7,4},{8,11},{9,10},{10,... | collective-permute-start | bytes 294920 | tf_op jit(solution)/shard_map/ppermute | solution.py:651
  237.2 27.8 %collective-permute-start.65 = (bf16[640,384]{1,0:T(8,128)(2,1)S(1)}, bf16[640,384]{1,0:T(8,128)(2,1)}, u32[]{:S(2)}, u32[]{:S(2)}) collective-permute-start(bf16[640,384]{1,0:T(8,128)(2,1)S(1)} %constant_dynamic-slice_fusion.13), channel_id=1, source_target_pairs={{0,8},{1,9},{2,10},{3,11},{4,12},{5,13},{6,14},{7,15},{8,0},{9,1},... | collective-permute-start | bytes 1474568 | tf_op jit(solution)/shard_map/ppermute | solution.py:651
  239.2 12.4 %collective-permute-start.59 = (bf16[6,2688]{1,0:T(8,128)(2,1)S(1)}, bf16[6,2688]{1,0:T(8,128)(2,1)S(1)}, u32[]{:S(2)}, u32[]{:S(2)}) collective-permute-start(bf16[6,2688]{1,0:T(8,128)(2,1)S(1)} %pad_maximum_fusion.2), channel_id=1, source_target_pairs={{0,4},{1,5},{2,6},{3,7},{4,0},{5,1},{6,2},{7,3},{8,12},{9,13},{10,... | collective-permute-start | bytes 96776 | tf_op jit(solution)/shard_map/ppermute | solution.py:651
  239.7 12.4 %collective-permute-start.60 = (bf16[6,2688]{1,0:T(8,128)(2,1)S(1)}, bf16[6,2688]{1,0:T(8,128)(2,1)S(1)}, u32[]{:S(2)}, u32[]{:S(2)}) collective-permute-start(bf16[6,2688]{1,0:T(8,128)(2,1)S(1)} %pad_maximum_fusion.2), channel_id=1, source_target_pairs={{0,6},{1,7},{2,4},{3,5},{4,2},{5,3},{6,0},{7,1},{8,14},{9,15},{10,... | collective-permute-start | bytes 96776 | tf_op jit(solution)/shard_map/ppermute | solution.py:651
  241.8 13.0 %collective-permute-start.51 = (bf16[2,32,384]{2,1,0:T(8,128)(2,1)}, bf16[2,32,384]{2,1,0:T(8,128)(2,1)S(1)}, u32[]{:S(2)}, u32[]{:S(2)}) collective-permute-start(bf16[2,32,384]{2,1,0:T(8,128)(2,1)} %get-tuple-element.189), channel_id=1, source_target_pairs={{0,1},{1,0},{2,3},{3,2},{4,5},{5,4},{6,7},{7,6},{8,9},{9,8},{10,11... | collective-permute-start | bytes 147464 | tf_op jit(solution)/shard_map/ppermute | solution.py:651
  243.1 13.4 %collective-permute-start.52 = (bf16[2,32,384]{2,1,0:T(8,128)(2,1)}, bf16[2,32,384]{2,1,0:T(8,128)(2,1)S(1)}, u32[]{:S(2)}, u32[]{:S(2)}) collective-permute-start(bf16[2,32,384]{2,1,0:T(8,128)(2,1)} %get-tuple-element.190), channel_id=1, source_target_pairs={{0,2},{1,3},{2,0},{3,1},{4,6},{5,7},{6,4},{7,5},{8,10},{9,11},{10,... | collective-permute-start | bytes 147464 | tf_op jit(solution)/shard_map/ppermute | solution.py:651
  258.9 11.2 %collective-permute-start.44 = (bf16[4,32,384]{2,1,0:T(8,128)(2,1)}, bf16[4,32,384]{2,1,0:T(8,128)(2,1)S(1)}, u32[]{:S(2)}, u32[]{:S(2)}) collective-permute-start(bf16[4,32,384]{2,1,0:T(8,128)(2,1)} %get-tuple-element.181), channel_id=1, source_target_pairs={{0,1},{1,0},{2,3},{3,2},{4,5},{5,4},{6,7},{7,6},{8,9},{9,8},{10,11... | collective-permute-start | bytes 294920 | tf_op jit(solution)/shard_map/ppermute | solution.py:651
  259.6 14.2 %collective-permute-start.45 = (bf16[4,32,384]{2,1,0:T(8,128)(2,1)}, bf16[4,32,384]{2,1,0:T(8,128)(2,1)S(1)}, u32[]{:S(2)}, u32[]{:S(2)}) collective-permute-start(bf16[4,32,384]{2,1,0:T(8,128)(2,1)} %get-tuple-element.182), channel_id=1, source_target_pairs={{0,2},{1,3},{2,0},{3,1},{4,6},{5,7},{6,4},{7,5},{8,10},{9,11},{10,... | collective-permute-start | bytes 294920 | tf_op jit(solution)/shard_map/ppermute | solution.py:651
  261.7 13.5 %collective-permute-start.46 = (bf16[4,32,384]{2,1,0:T(8,128)(2,1)}, bf16[4,32,384]{2,1,0:T(8,128)(2,1)S(1)}, u32[]{:S(2)}, u32[]{:S(2)}) collective-permute-start(bf16[4,32,384]{2,1,0:T(8,128)(2,1)} %get-tuple-element.183), channel_id=1, source_target_pairs={{0,3},{1,2},{2,1},{3,0},{4,7},{5,6},{6,5},{7,4},{8,11},{9,10},{10,... | collective-permute-start | bytes 294920 | tf_op jit(solution)/shard_map/ppermute | solution.py:651
  265.0 26.9 %collective-permute-start.61 = (bf16[24,2688]{1,0:T(8,128)(2,1)S(1)}, bf16[24,2688]{1,0:T(8,128)(2,1)S(1)}, u32[]{:S(2)}, u32[]{:S(2)}) collective-permute-start(bf16[24,2688]{1,0:T(8,128)(2,1)S(1)} %dynamic_update_slice.93), channel_id=1, source_target_pairs={{0,16},{1,17},{2,18},{3,19},{4,20},{5,21},{6,22},{7,23},{8,24},{9,... | collective-permute-start | bytes 387080 | tf_op jit(solution)/shard_map/ppermute | solution.py:651
  270.2 14.4 %collective-permute-start.48 = (bf16[4,32,384]{2,1,0:T(8,128)(2,1)}, bf16[4,32,384]{2,1,0:T(8,128)(2,1)S(1)}, u32[]{:S(2)}, u32[]{:S(2)}) collective-permute-start(bf16[4,32,384]{2,1,0:T(8,128)(2,1)} %get-tuple-element.185), channel_id=1, source_target_pairs={{0,5},{1,4},{2,7},{3,6},{4,1},{5,0},{6,3},{7,2},{8,13},{9,12},{10,... | collective-permute-start | bytes 294920 | tf_op jit(solution)/shard_map/ppermute | solution.py:651
  273.9 11.7 %collective-permute-start.49 = (bf16[4,32,384]{2,1,0:T(8,128)(2,1)}, bf16[4,32,384]{2,1,0:T(8,128)(2,1)S(1)}, u32[]{:S(2)}, u32[]{:S(2)}) collective-permute-start(bf16[4,32,384]{2,1,0:T(8,128)(2,1)} %get-tuple-element.186), channel_id=1, source_target_pairs={{0,6},{1,7},{2,4},{3,5},{4,2},{5,3},{6,0},{7,1},{8,14},{9,15},{10,... | collective-permute-start | bytes 294920 | tf_op jit(solution)/shard_map/ppermute | solution.py:651
  275.3 13.9 %collective-permute-start.50 = (bf16[4,32,384]{2,1,0:T(8,128)(2,1)S(1)}, bf16[4,32,384]{2,1,0:T(8,128)(2,1)S(1)}, u32[]{:S(2)}, u32[]{:S(2)}) collective-permute-start(bf16[4,32,384]{2,1,0:T(8,128)(2,1)S(1)} %copy-done.32), channel_id=1, source_target_pairs={{0,7},{1,6},{2,5},{3,4},{4,3},{5,2},{6,1},{7,0},{8,15},{9,14},{10,... | collective-permute-start | bytes 294920 | tf_op jit(solution)/shard_map/ppermute | solution.py:651
  280.9 35.9 %collective-permute-start.79 = (bf16[1792,384]{1,0:T(8,128)(2,1)}, bf16[1792,384]{1,0:T(8,128)(2,1)S(1)}, u32[]{:S(2)}, u32[]{:S(2)}) collective-permute-start(bf16[1792,384]{1,0:T(8,128)(2,1)} %constant_dynamic-slice_fusion.6), channel_id=1, source_target_pairs={{0,8},{1,9},{2,10},{3,11},{4,12},{5,13},{6,14},{7,15},{8,0},{9,1},... | collective-permute-start | bytes 4128776 | tf_op jit(solution)/shard_map/ppermute | solution.py:651
  285.6 17.2 %collective-permute-start.63 = (bf16[24,2688]{1,0:T(8,128)(2,1)S(1)}, bf16[24,2688]{1,0:T(8,128)(2,1)S(1)}, u32[]{:S(2)}, u32[]{:S(2)}) collective-permute-start(bf16[24,2688]{1,0:T(8,128)(2,1)S(1)} %dynamic_update_slice.93), channel_id=1, source_target_pairs={{0,17},{1,16},{2,19},{3,18},{4,21},{5,20},{6,23},{7,22},{8,25},{9,... | collective-permute-start | bytes 387080 | tf_op jit(solution)/shard_map/ppermute | solution.py:651
  318.1 12.7 %collective-permute-start.81 = (bf16[448,384]{1,0:T(8,128)(2,1)S(1)}, bf16[448,384]{1,0:T(8,128)(2,1)S(1)}, u32[]{:S(2)}, u32[]{:S(2)}) collective-permute-start(bf16[448,384]{1,0:T(8,128)(2,1)S(1)} %get-tuple-element.218), channel_id=1, source_target_pairs={{0,1},{1,0},{2,3},{3,2},{4,5},{5,4},{6,7},{7,6},{8,9},{9,8},{10,11... | collective-permute-start | bytes 1032200 | tf_op jit(solution)/shard_map/ppermute | solution.py:651
  319.2 12.3 %collective-permute-start.80 = (bf16[448,384]{1,0:T(8,128)(2,1)S(1)}, bf16[448,384]{1,0:T(8,128)(2,1)S(1)}, u32[]{:S(2)}, u32[]{:S(2)}) collective-permute-start(bf16[448,384]{1,0:T(8,128)(2,1)S(1)} %get-tuple-element.216), channel_id=1, source_target_pairs={{0,16},{1,17},{2,18},{3,19},{4,20},{5,21},{6,22},{7,23},{8,24},{9,... | collective-permute-start | bytes 1032200 | tf_op jit(solution)/shard_map/ppermute | solution.py:651
  321.0 28.9 %collective-permute-start.64 = (bf16[96,2688]{1,0:T(8,128)(2,1)S(1)}, bf16[96,2688]{1,0:T(8,128)(2,1)S(1)}, u32[]{:S(2)}, u32[]{:S(2)}) collective-permute-start(bf16[96,2688]{1,0:T(8,128)(2,1)S(1)} %constant_dynamic-update-slice_fusion.22), channel_id=1, source_target_pairs={{0,8},{1,9},{2,10},{3,11},{4,12},{5,13},{6,14},{7,15},{8,0},{9,1},... | collective-permute-start | bytes 1548296 | tf_op jit(solution)/shard_map/ppermute | solution.py:651
  322.0 14.2 %collective-permute-start.77 = (bf16[160,384]{1,0:T(8,128)(2,1)S(1)}, bf16[160,384]{1,0:T(8,128)(2,1)S(1)}, u32[]{:S(2)}, u32[]{:S(2)}) collective-permute-start(bf16[160,384]{1,0:T(8,128)(2,1)S(1)} %constant_dynamic-update-slice_fusion.16), channel_id=1, source_target_pairs={{0,17},{1,16},{2,19},{3,18},{4,21},{5,20},{6,23},{7,22},{8,25},{9,... | collective-permute-start | bytes 368648 | tf_op jit(solution)/shard_map/ppermute | solution.py:651
  336.2 29.4 %collective-permute-start.78 = (bf16[640,384]{1,0:T(8,128)(2,1)S(1)}, bf16[640,384]{1,0:T(8,128)(2,1)S(1)}, u32[]{:S(2)}, u32[]{:S(2)}) collective-permute-start(bf16[640,384]{1,0:T(8,128)(2,1)S(1)} %constant_dynamic-update-slice_fusion.12), channel_id=1, source_target_pairs={{0,8},{1,9},{2,10},{3,11},{4,12},{5,13},{6,14},{7,15},{8,0},{9,1},... | collective-permute-start | bytes 1474568 | tf_op jit(solution)/shard_map/ppermute | solution.py:651
  (110 other events, 1542.6 us)

commit v2 on v1

v2 whole, which is shorter than its diff:
```python
from functools import partial

import jax
import jax.numpy as jnp
from jax import lax
from jax.experimental import pallas as pl
from jax.experimental.pallas import tpu as pltpu
from jax.sharding import PartitionSpec as P

HEADS = 6
HEAD_DIM = 64
PAIRS = HEADS // 2
LANES = 128
BLOCK = 256
HALF = 4
EPSILON = 1e-06
ONES = 16
TIE = 8
F32 = jnp.float32
BF16 = jnp.bfloat16
MIB = 1 << 20


def dot(left, right):
    return jnp.dot(left, right, preferred_element_type=F32)


def dot_nt(left, right):
    return lax.dot_general(left, right, (((1,), (1,)), ((), ())), preferred_element_type=F32)


def params(limit=56, **more):
    return pltpu.CompilerParams(vmem_limit_bytes=limit * MIB, **more)


def cost(micros):
    return pl.CostEstimate(flops=0, bytes_accessed=int(micros * 3e6), transcendentals=0)


def full(shape):
    return pl.BlockSpec(shape, lambda *_: (0,) * len(shape))


SMEM = pl.BlockSpec(memory_space=pltpu.SMEM)


def row_layout(lens_ref, row, slots, big):
    count = jnp.int32(0)
    before = jnp.int32(0)
    for j in range(slots):
        is_big = (lens_ref[row, j] == big).astype(jnp.int32)
        before = before + jnp.where(count + is_big == 0, 1, 0)
        count = count + is_big
    return count, jnp.where(count == 1, before, 0)


def chunk_of(start, half, k):
    return jnp.where(half == 0, start + k, jnp.where(k < start, k, k + HALF))


class Plan:
    def __init__(self, rows, bands):
        self.rows, self.bands = rows, bands
        self.halves = 2 * rows
        self.whole = self.halves // bands
        assert self.whole <= 1
        self.rest = self.halves - self.whole * bands
        self.group = 1
        while self.rest and self.rest * self.group * 2 <= bands and self.group < HALF:
            self.group *= 2
        self.idle = self.rest * self.group != bands
        self.own = HALF // self.group

    @property
    def total(self):
        return sum(count for _, count in self.units())

    def units(self):
        found = []
        if self.whole:
            found.append(("whole", HALF))
        if self.rest:
            found.append(("shared", self.own))
        return found

    def half_row(self, name, device):
        if name == "whole":
            return device
        return self.whole * self.bands + device // self.group

    def first(self, name, device):
        return 0 if name == "whole" else (device % self.group) * self.own


def pack_kernel(plan, chunk, slots, big, apart, me_ref, lens_ref, x_ref, *outs):
    for s in range(plan.bands):
        dest = me_ref[0] ^ s if apart else s
        at = 0
        for name, count in plan.units():
            half_row = jnp.minimum(plan.half_row(name, dest), plan.halves - 1)
            row, half = half_row // 2, half_row % 2
            start = row_layout(lens_ref, row, slots, big)[1]
            for k in range(count):
                source = chunk_of(start, half, plan.first(name, dest) + k)
                rows = pl.ds(pl.multiple_of(source * chunk, chunk), chunk)
                if apart:
                    outs[s][at] = x_ref[row, rows, :]
                else:
                    outs[0][dest, at] = x_ref[row, rows, :]
                at += 1


def pack(plan, chunk, big, me, lens, x, apart):
    shape = (plan.total, chunk, x.shape[2])
    shapes = [shape] * plan.bands if apart else [(plan.bands,) + shape]
    found = pl.pallas_call(
        partial(pack_kernel, plan, chunk, lens.shape[1], big, apart),
        in_specs=[SMEM, SMEM, full(x.shape)],
        out_specs=[full(s) for s in shapes],
        out_shape=[jax.ShapeDtypeStruct(s, x.dtype) for s in shapes],
        grid=(1,),
        compiler_params=params(32),
        cost_estimate=cost(0.1),
        name="pack",
    )(me, lens, x)
    return found if apart else found[0]


def unpack_kernel(plan, chunk, slots, big, lens_ref, piece_ref, out_ref):
    for owner in range(plan.bands):
        at = 0
        for name, count in plan.units():
            half_row = plan.half_row(name, owner)
            if half_row < plan.halves:
                row, half = half_row // 2, half_row % 2
                start = row_layout(lens_ref, row, slots, big)[1]
                for k in range(count):
                    source = chunk_of(start, half, plan.first(name, owner) + k)
                    rows = pl.ds(pl.multiple_of(source * chunk, chunk), chunk)
                    out_ref[row, rows, :] = piece_ref[owner, at + k].astype(out_ref.dtype)
            at += count


def unpack(plan, chunk, big, lens, pieces, dtype):
    shape = (plan.rows, chunk * 2 * HALF, pieces.shape[3])
    return pl.pallas_call(
        partial(unpack_kernel, plan, chunk, lens.shape[1], big),
        in_specs=[SMEM, full(pieces.shape)],
        out_specs=full(shape),
        out_shape=jax.ShapeDtypeStruct(shape, dtype),
        grid=(1,),
        compiler_params=params(32),
        cost_estimate=cost(0.1),
        name="unpack",
    )(lens, pieces)


def collect_kernel(n, low, count, chunk, me_ref, *refs):
    for b in range(count):
        for s in range(n):
            at = pl.multiple_of(b * BLOCK + (me_ref[0] ^ s) * chunk, chunk)
            refs[n][pl.ds(at, chunk), :] = refs[s][low + b]


def collect(n, low, count, chunk, me, pieces):
    width = pieces[0].shape[2]
    return pl.pallas_call(
        partial(collect_kernel, n, low, count, chunk),
        in_specs=[SMEM] + [full(p.shape) for p in pieces],
        out_specs=full((count * BLOCK, width)),
        out_shape=jax.ShapeDtypeStruct((count * BLOCK, width), BF16),
        grid=(1,),
        compiler_params=params(16),
        cost_estimate=cost(0.1),
        name="collect",
    )(me, *pieces)


def prepare_kernel(plan, slots, big, me_ref, lens_ref, index_ref, table_ref, weight_ref, bias_ref, *refs):
    mods_out, activity_out, flags_out, table_scr, activity_scr = refs
    table_scr[...] = table_ref[...].astype(F32)
    activity_scr[...] = jnp.zeros_like(activity_scr)
    at = 0
    for j, (name, count) in enumerate(plan.units()):
        half_row = jnp.minimum(plan.half_row(name, me_ref[0]), plan.halves - 1)
        row, half = half_row // 2, half_row % 2
        bigs, start = row_layout(lens_ref, row, slots, big)
        is_big = jnp.logical_or(bigs == 2, jnp.logical_and(bigs == 1, half == 0))
        flags_out[j] = is_big.astype(jnp.int32)
        for t in range(HALF // count):
            first = 0 if count == HALF else ((me_ref[0] % plan.group) ^ t) * count
            for k in range(count):
                place = first + k
                single = jnp.where(half == 0, start, jnp.where(place < start, place, place + 1))
                slot = jnp.where(bigs == 2, half, jnp.where(bigs == 0, HALF * half + place, single))
                chosen = table_scr[pl.ds(index_ref[row, slot], 1), :]
                activity_scr[at : at + 1, :] = chosen * (1.0 / (1.0 + jnp.exp(-chosen)))
                at += 1
    activity = activity_scr[...].astype(BF16)
    activity_out[...] = activity.astype(F32)
    mods_out[...] = dot(activity, weight_ref[...]) + as_row(bias_ref)


def prepare(plan, big, me, lens, index, table, weight, bias):
    width = table.shape[1]
    shape = jax.ShapeDtypeStruct
    arrays = [table, weight, bias]
    return pl.pallas_call(
        partial(prepare_kernel, plan, lens.shape[1], big),
        in_specs=[SMEM] * 3 + [full(a.shape) for a in arrays],
        out_specs=[full((8, weight.shape[1])), full((8, width)), SMEM],
        out_shape=[
            shape((8, weight.shape[1]), F32),
            shape((8, width), F32),
            shape((2,), jnp.int32),
        ],
        grid=(1,),
        scratch_shapes=[pltpu.VMEM(table.shape, F32), pltpu.VMEM((8, width), F32)],
        compiler_params=params(32),
        cost_estimate=cost(0.1),
        name="prepare",
    )(me, lens, index, *arrays)


def layer_norm(values):
    centre = values - jnp.mean(values, axis=-1, keepdims=True)
    inverse = lax.rsqrt(jnp.mean(centre * centre, axis=-1, keepdims=True) + EPSILON)
    return centre * inverse, inverse


def norm_back(grad, normed, inverse):
    return inverse * (
        grad
        - jnp.mean(grad, axis=-1, keepdims=True)
        - normed * jnp.mean(grad * normed, axis=-1, keepdims=True)
    )


def as_row(ref):
    return ref[...].astype(F32).reshape(1, -1)


def column_sum(values):
    return jnp.sum(values, axis=0, keepdims=True)


def attend_kernel(n, unit, low, nq, nk, chunk, width, me_ref, flag_ref, *refs):
    pieces, refs = refs[:n], refs[n:]
    count = nk // nq - 1
    others, refs = refs[:count], refs[count:]
    mods_ref, weight_ref, query_bias_ref, value_bias_ref = refs[:4]
    x_out, hint_out, q_out, k_out, v_out, e_out, ot_out, inv_out, mixed_out = refs[4:13]
    k_scr, qt_scr, vt_scr = refs[13:]
    p = pl.program_id(0)

    @pl.when(p == 0)
    def _():
        qt_scr[...] = jnp.zeros_like(qt_scr)
        for h in range(HEADS):
            vt_scr[h, HEAD_DIM:, :] = jnp.ones((ONES, nk * BLOCK), BF16)
        for b in range(nk):
            rows = pl.ds(b * BLOCK, BLOCK)
            if b < nq:
                for s in range(n):
                    at = pl.multiple_of(b * BLOCK + (me_ref[0] ^ s) * chunk, chunk)
                    x_out[pl.ds(at, chunk), :] = pieces[s][low + b]
            else:
                t, inner = b // nq - 1, b % nq
                x_out[rows, :] = others[t][pl.ds(inner * BLOCK, BLOCK), :]
            source = x_out[rows, :].astype(F32)
            normed = layer_norm(source)[0]
            shift = mods_ref[low + b : low + b + 1, 0:width]
            scale = mods_ref[low + b : low + b + 1, width : 2 * width]
            hin = (normed * (1.0 + scale) + shift).astype(BF16)
            hint_out[:, rows] = hin.T
            triple = dot(hin, weight_ref[...])
            keys = triple[:, width : 2 * width].astype(BF16)
            values = (triple[:, 2 * width :] + as_row(value_bias_ref)).astype(BF16)
            values_t = values.T
            for j in range(PAIRS):
                lanes = slice(j * LANES, (j + 1) * LANES)
                k_scr[j, rows, :] = keys[:, lanes]
                k_out[j, rows, :] = keys[:, lanes]
                v_out[j, rows, :] = values[:, lanes]
            for h in range(HEADS):
                vt_scr[h, :HEAD_DIM, rows] = values_t[h * HEAD_DIM : (h + 1) * HEAD_DIM]
            if b < nq:
                query = (triple[:, :width] + as_row(query_bias_ref)) * (HEAD_DIM**-0.5)
                query = query.astype(BF16)
                for j in range(PAIRS):
                    q_out[j, rows, :] = query[:, j * LANES : (j + 1) * LANES]
                query_t = query.T
                for h in range(HEADS):
                    to = (h % 2) * HEAD_DIM
                    qt_scr[h, to : to + HEAD_DIM, rows] = query_t[
                        h * HEAD_DIM : (h + 1) * HEAD_DIM
                    ]

    def tile(columns, krows):
        found = []
        for hh in range(2):
            h = 2 * p + hh
            scores = dot(k_scr[p, krows, :], qt_scr[h, :, columns])
            exps = jnp.exp(scores - jnp.max(scores, axis=0, keepdims=True)).astype(BF16)
            e_out[hh, krows, columns] = exps
            summed = dot(vt_scr[h, :, krows], exps)
            inverse = 1.0 / summed[HEAD_DIM : HEAD_DIM + 1]
            found.append(summed[:HEAD_DIM] * inverse)
            inv_out[0, hh : hh + 1, columns] = inverse
        both = jnp.concatenate(found, axis=0)
        ot_out[0, :, columns] = both
        mixed_out[columns, :] = both.T.astype(BF16)

    @pl.when(flag_ref[unit] == 1)
    def _():
        tile(pl.ds(0, nq * BLOCK), pl.ds(0, nk * BLOCK))

    @pl.when(flag_ref[unit] == 0)
    def _():
        for b in range(nq):
            tile(pl.ds(b * BLOCK, BLOCK), pl.ds(b * BLOCK, BLOCK))


def attend(n, unit, low, nq, nk, chunk, me, flag, pieces, others, mods, weight, query_bias, value_bias):
    width = weight.shape[0]
    qs, ks = nq * BLOCK, nk * BLOCK
    shape = jax.ShapeDtypeStruct
    outs = [
        (shape((ks, width), BF16), None),
        (shape((width, ks), BF16), None),
        (shape((PAIRS, qs, LANES), BF16), None),
        (shape((PAIRS, ks, LANES), BF16), None),
        (shape((PAIRS, ks, LANES), BF16), None),
        (shape((HEADS, ks, qs), BF16), pl.BlockSpec((2, ks, qs), lambda p: (p, 0, 0))),
        (shape((PAIRS, LANES, qs), F32), pl.BlockSpec((1, LANES, qs), lambda p: (p, 0, 0))),
        (shape((PAIRS, 8, qs), F32), pl.BlockSpec((1, 8, qs), lambda p: (p, 0, 0))),
        (shape((qs, width), BF16), pl.BlockSpec((qs, LANES), lambda p: (0, p))),
    ]
    arrays = [*pieces, *others, mods, weight, query_bias, value_bias]
    flops = 2 * ks * width * 3 * width + 4 * HEADS * qs * ks * HEAD_DIM * 4
    return pl.pallas_call(
        partial(attend_kernel, n, unit, low, nq, nk, chunk, width),
        grid=(PAIRS,),
        in_specs=[SMEM, SMEM] + [full(a.shape) for a in arrays],
        out_specs=[spec or full(s.shape) for s, spec in outs],
        out_shape=[s for s, _ in outs],
        scratch_shapes=[
            pltpu.VMEM((PAIRS, ks, LANES), BF16),
            pltpu.VMEM((HEADS, LANES, qs), BF16),
            pltpu.VMEM((HEADS, HEAD_DIM + ONES, ks), BF16),
        ],
        compiler_params=params(),
        cost_estimate=cost(0.1),
        name="attend",
    )(me, flag, *arrays)


def back_tile(qlow, qsize, klow, ksize, e_ref, q_ref, k_ref, v_ref, ot_ref, inv_ref, grad_ref):
    columns, krows = pl.ds(qlow, qsize), pl.ds(klow, ksize)
    lane = lax.broadcasted_iota(jnp.int32, (qsize, LANES), 1)
    grad_t = grad_ref[columns, :].astype(F32).T
    keys_t = k_ref[0, krows, :].T
    query = q_ref[0, columns, :]
    zeros = jnp.zeros((HEAD_DIM, qsize), BF16)
    found, keys_grad, values_grad = [], None, None
    for hh in range(2):
        part = slice(hh * HEAD_DIM, (hh + 1) * HEAD_DIM)
        scaled = (grad_t[part] * inv_ref[0, hh : hh + 1, columns]).astype(BF16)
        delta = column_sum(scaled.astype(F32) * ot_ref[0, part, columns])
        masked = jnp.concatenate([scaled, zeros] if hh == 0 else [zeros, scaled], axis=0)
        exps = e_ref[hh, krows, columns]
        prob_grad = dot(v_ref[0, krows, :], masked)
        score_grad = (exps.astype(F32) * (prob_grad - delta)).astype(BF16)
        own = (lane < HEAD_DIM) if hh == 0 else (lane >= HEAD_DIM)
        values_part = dot_nt(exps, masked)
        keys_part = dot(score_grad, jnp.where(own, query, jnp.zeros_like(query)))
        values_grad = values_part if hh == 0 else values_grad + values_part
        keys_grad = keys_part if hh == 0 else keys_grad + keys_part
        found.append(dot(keys_t[part], score_grad))
    both = jnp.concatenate(found, axis=0) * (HEAD_DIM**-0.5)
    return both.T.astype(BF16), keys_grad.astype(BF16), values_grad.astype(BF16)


def shared_back_kernel(nq, nk, flag_ref, *refs):
    tile_refs, (hint_ref, weight_ref, own_out), refs = refs[:7], refs[7:10], refs[10:]
    others_out, (tw_out, tb_out, tg_scr) = refs[:-3], refs[-3:]
    p = pl.program_id(0)
    qs, rest = nq * BLOCK, (nk - nq) * BLOCK

    def tile(qlow, qsize, klow, ksize):
        query_grad, keys_grad, values_grad = back_tile(qlow, qsize, klow, ksize, *tile_refs)
        tg_scr[p, pl.ds(qlow, qsize), :] = query_grad
        tg_scr[PAIRS + p, pl.ds(klow, ksize), :] = keys_grad
        tg_scr[2 * PAIRS + p, pl.ds(klow, ksize), :] = values_grad

    tg_scr[p, qs:, :] = jnp.zeros((rest, LANES), BF16)

    @pl.when(flag_ref[1] == 1)
    def _():
        tile(0, qs, 0, nk * BLOCK)

    @pl.when(flag_ref[1] == 0)
    def _():
        for j in (1, 2):
            tg_scr[j * PAIRS + p, qs:, :] = jnp.zeros((rest, LANES), BF16)
        for b in range(nq):
            tile(b * BLOCK, BLOCK, b * BLOCK, BLOCK)

    @pl.when(p == PAIRS - 1)
    def _():
        grads = jnp.concatenate([tg_scr[j] for j in range(3 * PAIRS)], axis=1)
        back = dot_nt(grads, weight_ref[...])
        own_out[...] = back[:qs]
        for t, out in enumerate(others_out):
            out[...] = back[(t + 1) * qs : (t + 2) * qs].astype(BF16)
        weight_grad = dot(hint_ref[...], grads)
        sums = column_sum(grads.astype(F32))
        for j in range(PAIRS):
            for m in range(3):
                low = (m * PAIRS + j) * LANES
                tw_out[j, :, m * LANES : (m + 1) * LANES] = weight_grad[:, low : low + LANES]
                tb_out[j, :, m * LANES : (m + 1) * LANES] = jnp.broadcast_to(
                    sums[:, low : low + LANES], (8, LANES)
                )


def whole_back_kernel(size, begun, last, flag_ref, *refs):
    tile_refs, hint_ref, refs = refs[:7], refs[7], refs[8:]
    if begun:
        tw_ref, tb_ref, refs = refs[0], refs[1], refs[2:]
    if last:
        me_ref, mixer_ref, earlier, refs = refs[0], refs[1], refs[2 : 1 + PAIRS], refs[1 + PAIRS :]
    tq_out, tk_out, tv_out, tb_out, refs = *refs[:4], refs[4:]

    def tile(qlow, qsize, klow, ksize):
        query_grad, keys_grad, values_grad = back_tile(qlow, qsize, klow, ksize, *tile_refs)
        tq_out[pl.ds(qlow, qsize), :] = query_grad
        tk_out[pl.ds(klow, ksize), :] = keys_grad
        tv_out[pl.ds(klow, ksize), :] = values_grad

    @pl.when(flag_ref[0] == 1)
    def _():
        tile(0, HALF * BLOCK, 0, HALF * BLOCK)

    @pl.when(flag_ref[0] == 0)
    def _():
        for b in range(HALF):
            tile(b * BLOCK, BLOCK, b * BLOCK, BLOCK)

    grads = jnp.concatenate([tq_out[...], tk_out[...], tv_out[...]], axis=1)
    weight_grad = dot(hint_ref[...], grads)
    sums = column_sum(grads.astype(F32))
    if begun:
        weight_grad, sums = weight_grad + tw_ref[0], sums + tb_ref[0, 0:1]
    tb_out[...] = jnp.broadcast_to(sums, tb_out.shape)
    if not last:
        refs[0][...] = weight_grad
        return
    first_out, second_out, rows_scr = refs
    width = weight_grad.shape[0]
    for m in range(3):
        lanes = slice(m * LANES, (m + 1) * LANES)
        rows = slice(m * width, (m + 1) * width)
        for j, ref in enumerate(earlier):
            rows_scr[rows, j * LANES : (j + 1) * LANES] = ref[:, lanes].astype(BF16)
        rows_scr[rows, (PAIRS - 1) * LANES :] = weight_grad[:, lanes].astype(BF16)
    rows_scr[3 * width : 4 * width, :] = mixer_ref[...].astype(BF16)
    if rows_scr.shape[0] > 4 * width:
        rows_scr[4 * width :, :] = jnp.zeros((rows_scr.shape[0] - 4 * width, width), BF16)
    spread_out(me_ref, rows_scr.shape[0] // size, size, rows_scr, (first_out, second_out))


def back_inputs(nq, nk, first, flag, kept, grad, low):
    hint, q, k, v, e, ot, inv = kept
    qs, ks = nq * BLOCK, nk * BLOCK
    by_pair = lambda *tail: pl.BlockSpec((1,) + tail, lambda p: (first + p, 0, 0))
    in_specs = [
        SMEM,
        pl.BlockSpec((2, ks, qs), lambda p: (first + p, 0, 0)),
        by_pair(qs, LANES),
        by_pair(ks, LANES),
        by_pair(ks, LANES),
        by_pair(LANES, qs),
        by_pair(8, qs),
        pl.BlockSpec((qs, LANES), lambda p: (low * BLOCK // qs, first + p)),
        full(hint.shape),
    ]
    return in_specs, [flag, e, q, k, v, ot, inv, grad, hint]


def back_cost(qs, ks, steps):
    flops = 8 * 2 * steps * qs * ks * HEAD_DIM * 4
    return pl.CostEstimate(flops=flops, bytes_accessed=4 * steps * qs * ks, transcendentals=0)


def shared_back(nq, nk, flag, kept, grad, low, weight):
    width = weight.shape[0]
    qs, ks = nq * BLOCK, nk * BLOCK
    in_specs, arrays = back_inputs(nq, nk, 0, flag, kept, grad, low)
    shape = jax.ShapeDtypeStruct
    outs = [shape((qs, width), F32)] + [shape((qs, width), BF16)] * (nk // nq - 1)
    outs += [shape((PAIRS, width, 3 * LANES), F32), shape((PAIRS, 8, 3 * LANES), F32)]
    return pl.pallas_call(
        partial(shared_back_kernel, nq, nk),
        grid=(PAIRS,),
        in_specs=in_specs + [full(weight.shape)],
        out_specs=[full(o.shape) for o in outs],
        out_shape=outs,
        scratch_shapes=[pltpu.VMEM((3 * PAIRS, ks, LANES), BF16)],
        compiler_params=params(),
        cost_estimate=cost(0.1),
        name="shared_back",
    )(*arrays, weight)


def whole_back(size, me, pair, flag, kept, grad, begun, mixer, earlier):
    width = mixer.shape[0]
    rows = HALF * BLOCK
    in_specs, arrays = back_inputs(HALF, HALF, pair, flag, kept, grad, 0)
    shape = jax.ShapeDtypeStruct
    if begun:
        in_specs += [pl.BlockSpec((1,) + b.shape[1:], lambda p: (pair, 0, 0)) for b in begun]
        arrays += begun
    outs = [shape((rows, LANES), BF16)] * 3 + [shape((8, 3 * LANES), F32)]
    last = pair == PAIRS - 1
    scratch = []
    if last:
        in_specs += [SMEM] + [full(a.shape) for a in (mixer, *earlier)]
        arrays += [me, mixer, *earlier]
        total = padded(4 * width, size)
        outs += [shape((total // 2, width), BF16)] * 2
        scratch = [pltpu.VMEM((total, width), BF16)]
    else:
        outs += [shape((width, 3 * LANES), F32)]
    return pl.pallas_call(
        partial(whole_back_kernel, size, bool(begun), last),
        grid=(1,),
        in_specs=in_specs,
        out_specs=[full(o.shape) for o in outs],
        out_shape=outs,
        scratch_shapes=scratch,
        compiler_params=params(),
        cost_estimate=cost(0.1),
        name="whole_back",
    )(*arrays)


def spread_out(me_ref, chunk, size, source, outs):
    half = size // 2
    for j, out in enumerate(outs):

        @pl.loop(0, half)
        def _(p, j=j, out=out):
            at = pl.multiple_of(((p + j * half) ^ me_ref[0]) * chunk, chunk)
            out[pl.ds(pl.multiple_of(p * chunk, chunk), chunk), :] = source[pl.ds(at, chunk), :]


def padded(rows, size):
    return rows + -rows % (16 * size)


STEP = 6
SPLIT = 1


def feed_kernel(units, n, chunk, width, size, masked, me_ref, *refs):
    total = sum(count for _, count in units)
    u = len(units)
    if masked:
        valid_ref, refs = refs[0], refs[1:]
    xs, mixes, cot_ref, refs = refs[:u], refs[u : 2 * u], refs[2 * u], refs[2 * u + 1 :]
    mods_ref, activity_ref, mixer_w, mixer_b, hidden_w, hidden_b, output_w, output_b = refs[:8]
    out_ref, refs = refs[8], refs[9:]
    middle_out, mixed_grad_out, first_out, second_out, mixer_out, small_out, refs = *refs[:6], refs[6:]
    middle_scr, branch_scr, out_acc, mid_acc, normed_scr, grad_scr, normed_t, grad_t = refs[:8]
    ow_acc, hw_acc, mw_acc, ob_acc, hb_acc, mb_acc, rows_scr, slots_acc = refs[8:]
    f = pl.program_id(0)
    part = ow_acc.shape[1] // SPLIT
    cut = lambda at: slice(at * width, (at + 1) * width)
    lows = [sum(count for _, count in units[:j]) for j in range(u)]

    def cotangent(b):
        cot = jnp.concatenate([cot_ref[s, b] for s in range(n)], axis=0).astype(F32)
        return cot * valid_ref[0] if masked else cot

    @pl.when(f == 0)
    def _():
        for acc in (out_acc, mid_acc, ow_acc, hw_acc, mw_acc, ob_acc, hb_acc, mb_acc, slots_acc):
            acc[...] = jnp.zeros_like(acc)
        for j in range(u):

            for b in range(units[j][1]):
                source = pl.ds(b * BLOCK, BLOCK)
                at = b + lows[j]
                rows = pl.ds(at * BLOCK, BLOCK)
                mods = mods_ref[at : at + 1, :]
                branch = dot(mixes[j][source, :], mixer_w[...]) + as_row(mixer_b)
                middle = xs[j][source, :].astype(F32) + mods[:, cut(2)] * branch
                normed_mid = layer_norm(middle)[0] * (1.0 + mods[:, cut(4)]) + mods[:, cut(3)]
                normed_mid = normed_mid.astype(BF16)
                output_grad = (mods[:, cut(5)] * cotangent(at)).astype(BF16)
                branch_scr[rows, :] = branch
                middle_scr[rows, :] = middle
                normed_scr[rows, :] = normed_mid
                grad_scr[rows, :] = output_grad
                normed_t[:, rows] = normed_mid.T
                grad_t[:, rows] = output_grad.T
                ob_acc[...] += column_sum(output_grad.astype(F32))

    units_of = pl.ds(pl.multiple_of(f * part, part), part)

    @pl.loop(0, total // STEP)
    def _(m):
        rows = pl.ds(pl.multiple_of(m * STEP * BLOCK, STEP * BLOCK), STEP * BLOCK)
        hidden = dot(normed_scr[rows, :], hidden_w[...]) + as_row(hidden_b)
        square = hidden * hidden
        bend = 0.7978845608028654 * 0.044715
        curve = jnp.tanh(hidden * (0.7978845608028654 + bend * square))
        half = 0.5 + 0.5 * curve
        active = (hidden * half).astype(BF16)
        slope = half + (0.5 * hidden) * (1.0 - curve * curve) * (
            0.7978845608028654 + 3.0 * bend * square
        )
        hidden_grad = (dot_nt(grad_scr[rows, :], output_w[...]) * slope).astype(BF16)
        out_acc[rows, :] += dot(active, output_w[...])
        mid_acc[rows, :] += dot_nt(hidden_grad, hidden_w[...])
        ow_acc[:, units_of] += dot(grad_t[:, rows], active)
        hw_acc[:, units_of] += dot(normed_t[:, rows], hidden_grad)
        hb_acc[:, units_of] += column_sum(hidden_grad.astype(F32))

    @pl.when(f == SPLIT - 1)
    def _():
        for j in range(u):

            for b in range(units[j][1]):
                source = pl.ds(b * BLOCK, BLOCK)
                at = b + lows[j]
                rows = pl.ds(at * BLOCK, BLOCK)
                mods = mods_ref[at : at + 1, :]
                gate_one, scale_two, gate_two = mods[:, cut(2)], mods[:, cut(4)], mods[:, cut(5)]
                middle, branch = middle_scr[rows, :], branch_scr[rows, :]
                cot = cotangent(at)
                output = out_acc[rows, :] + as_row(output_b)
                result = (middle + gate_two * output).astype(BF16)
                for s in range(n):
                    out_ref[s, at] = result[s * chunk : (s + 1) * chunk]
                normed, inverse = layer_norm(middle)
                mid_grad = mid_acc[rows, :]
                middle_grad = cot + norm_back(mid_grad * (1.0 + scale_two), normed, inverse)
                middle_out[rows, :] = middle_grad
                branch_grad = (gate_one * middle_grad).astype(BF16)
                mw_acc[...] += dot(mixes[j][source, :].T, branch_grad)
                mb_acc[...] += column_sum(branch_grad.astype(F32))
                mixed_grad_out[rows, :] = dot_nt(branch_grad, mixer_w[...]).astype(BF16)
                found = (
                    column_sum(middle_grad * branch),
                    column_sum(mid_grad),
                    column_sum(mid_grad * normed),
                    column_sum(cot * output),
                )
                for m, row in enumerate(found):
                    slots_acc[m, at : at + 1, :] = row

        ff = ow_acc.shape[1]
        rows_scr[:ff, :] = ow_acc[...].T.astype(BF16)
        for j in range(ff // width):
            lo = ff + j * width
            rows_scr[lo : lo + width, :] = hw_acc[:, j * width : (j + 1) * width].astype(BF16)
        if rows_scr.shape[0] > 2 * ff:
            rows_scr[2 * ff :, :] = jnp.zeros((rows_scr.shape[0] - 2 * ff, width), BF16)
        spread_out(me_ref, rows_scr.shape[0] // size, size, rows_scr, (first_out, second_out))
        mixer_out[...] = mw_acc[...]
        sums = [ob_acc[...]]
        sums += [hb_acc[:, j * width : (j + 1) * width] for j in range(ff // width)]
        sums += [mb_acc[...], jnp.zeros((8 - 2 - ff // width, width), F32)]
        small = [slots_acc[m] for m in range(4)] + [activity_ref[...]] + sums
        small_out[...] = jnp.concatenate(small, axis=0).astype(BF16)


def feed(units, n, chunk, size, me, valid, xs, mixes, cots, mods, activity, weights):
    width, ff = weights[2].shape
    total = sum(count for _, count in units)
    shape = jax.ShapeDtypeStruct
    tokens, part = total * BLOCK, ff // SPLIT
    arrays = [*xs, *mixes, cots, mods, activity, *weights]
    in_specs = [full(a.shape) for a in arrays]
    in_specs[-4] = pl.BlockSpec((width, part), lambda f: (0, f))
    in_specs[-3] = pl.BlockSpec((part,), lambda f: (f,))
    in_specs[-2] = pl.BlockSpec((part, width), lambda f: (f, 0))
    rows = padded(2 * ff, size)
    outs = [shape((n, total, chunk, width), BF16)]
    outs += [shape((tokens, width), F32), shape((tokens, width), BF16)]
    outs += [shape((rows // 2, width), BF16)] * 2
    outs += [shape((width, width), F32), shape((48, width), BF16)]
    in_specs, arrays = [SMEM] + in_specs, [me] + arrays
    if valid is not None:
        in_specs, arrays = [SMEM] + in_specs, [me, valid] + arrays[1:]
    found = pl.pallas_call(
        partial(feed_kernel, units, n, chunk, width, size, valid is not None),
        grid=(SPLIT,),
        in_specs=in_specs,
        out_specs=[full(o.shape) for o in outs],
        out_shape=outs,
        scratch_shapes=[
            pltpu.VMEM((tokens, width), F32),
            pltpu.VMEM((tokens, width), F32),
            pltpu.VMEM((tokens, width), F32),
            pltpu.VMEM((tokens, width), F32),
            pltpu.VMEM((tokens, width), BF16),
            pltpu.VMEM((tokens, width), BF16),
            pltpu.VMEM((width, tokens), BF16),
            pltpu.VMEM((width, tokens), BF16),
            pltpu.VMEM((width, ff), F32),
            pltpu.VMEM((width, ff), F32),
            pltpu.VMEM((width, width), F32),
            pltpu.VMEM((1, width), F32),
            pltpu.VMEM((1, ff), F32),
            pltpu.VMEM((1, width), F32),
            pltpu.VMEM((rows, width), BF16),
            pltpu.VMEM((4, 8, width), F32),
        ],
        compiler_params=params(),
        cost_estimate=cost(0.1),
        name="feed",
    )(*arrays)
    return found[0], found[1:]


def finish_kernel(units, n, chunk, width, count, *refs):
    u = len(units)
    total = sum(c for _, c in units)
    xs, refs = refs[:u], refs[u:]
    parts, weight_ref, refs = refs[: 3 * PAIRS], refs[3 * PAIRS], refs[3 * PAIRS + 1 :]
    if u > 1:
        own_ref, others, refs = refs[0], refs[1 : 1 + count], refs[1 + count :]
    sums, refs = refs[:PAIRS], refs[PAIRS:]
    middle_ref, mods_ref, out_ref, small_out, x_scr, g_scr, slots_acc = refs
    i = pl.program_id(0)

    @pl.when(i == 0)
    def _():
        slots_acc[...] = jnp.zeros_like(slots_acc)

    @pl.when(i < HALF)
    def _():
        x_scr[...] = xs[0][...]
        grads = jnp.concatenate([part[...] for part in parts], axis=1)
        g_scr[...] = dot_nt(grads, weight_ref[...])

    if u > 1:

        @pl.when(i >= HALF)
        def _():
            x_scr[...] = xs[1][...]
            grad = own_ref[...]
            for other in others:
                grad = grad + other[...].astype(F32)
            g_scr[...] = grad

    scale_one = mods_ref[pl.ds(i, 1), width : 2 * width]
    normed, inverse = layer_norm(x_scr[...].astype(F32))
    grad = g_scr[...]
    slots_acc[0, pl.ds(i, 1), :] = column_sum(grad)
    slots_acc[1, pl.ds(i, 1), :] = column_sum(grad * normed)
    result = middle_ref[...] + norm_back(grad * (1.0 + scale_one), normed, inverse)
    result = result.astype(BF16)
    for s in range(n):
        out_ref[s, 0] = result[s * chunk : (s + 1) * chunk]

    @pl.when(i == total - 1)
    def _():
        biases = [
            jnp.concatenate([ref[0:1, m * LANES : (m + 1) * LANES] for ref in sums], axis=1)
            for m in (0, 2)
        ]
        small = [slots_acc[0], slots_acc[1], *biases, jnp.zeros((14, width), F32)]
        small_out[...] = jnp.concatenate(small, axis=0).astype(BF16)


def finish(units, n, chunk, xs, parts, weight, own, others, sums, middle, mods):
    width = middle.shape[1]
    total = sum(count for _, count in units)
    shape = jax.ShapeDtypeStruct
    lows = [sum(count for _, count in units[:j]) for j in range(len(units))]

    def rows_of(j, columns):
        return pl.BlockSpec(
            (BLOCK, columns), lambda i: (jnp.clip(i - lows[j], 0, units[j][1] - 1), 0)
        )

    in_specs = [rows_of(j, width) for j in range(len(units))]
    in_specs += [rows_of(0, LANES)] * (3 * PAIRS) + [full(weight.shape)]
    arrays = [*xs, *parts, weight]
    if len(units) > 1:
        in_specs += [rows_of(1, width)] * (1 + len(others))
        arrays += [own, *others]
    in_specs += [full(s.shape) for s in sums]
    in_specs += [pl.BlockSpec((BLOCK, width), lambda i: (i, 0)), full(mods.shape)]
    arrays += [*sums, middle, mods]
    return pl.pallas_call(
        partial(finish_kernel, units, n, chunk, width, len(others)),
        grid=(total,),
        in_specs=in_specs,
        out_specs=[
            pl.BlockSpec((n, 1, chunk, width), lambda i: (0, i, 0, 0)),
            full((32, width)),
        ],
        out_shape=[shape((n, total, chunk, width), BF16), shape((32, width), BF16)],
        scratch_shapes=[
            pltpu.VMEM((BLOCK, width), BF16),
            pltpu.VMEM((BLOCK, width), F32),
            pltpu.VMEM((2, 8, width), F32),
        ],
        compiler_params=params(),
        cost_estimate=cost(0.1),
        name="finish",
    )(*arrays)


def settle_kernel(size, chunk, places, kept, me_ref, *refs):
    pieces, outs, small_out, rows_scr = refs[:kept], refs[kept:-2], refs[-2], refs[-1]
    held = pieces[0].shape[0] // (size // kept)
    for j, piece in enumerate(pieces):

        @pl.loop(0, size // kept)
        def _(p, j=j, piece=piece):
            at = pl.multiple_of(((p + j * (size // kept)) ^ me_ref[0]) * chunk, chunk)
            low = pl.multiple_of(p * held, 16)
            rows_scr[pl.ds(at, chunk), :] = piece[pl.ds(low, chunk), :].astype(F32)
            small_out[p + j * (size // kept)] = piece[pl.ds(low + chunk, held - chunk), :].astype(F32)

    width = rows_scr.shape[1]
    for out, low in zip(outs, places):
        rows = out.shape[0]
        for c in range(out.shape[1] // width):
            out[:, c * width : (c + 1) * width] = rows_scr[low + c * rows : low + (c + 1) * rows, :]


def settle(size, chunk, me, pieces, shapes):
    width = pieces[0].shape[1]
    held = pieces[0].shape[0] * len(pieces) // size
    places, low = [], 0
    for rows, columns in shapes:
        places.append(low)
        low += rows * (columns // width)
    shapes = [*shapes, (size, held - chunk, width)]
    return pl.pallas_call(
        partial(settle_kernel, size, chunk, places, len(pieces)),
        in_specs=[SMEM] + [full(h.shape) for h in pieces],
        out_specs=[full(s) for s in shapes],
        out_shape=[jax.ShapeDtypeStruct(s, F32) for s in shapes],
        grid=(1,),
        scratch_shapes=[pltpu.VMEM((size * chunk, width), F32)],
        compiler_params=params(40),
        cost_estimate=cost(0.1),
        name="settle",
    )(me, *pieces)


def modulate_kernel(early_ref, late_ref, *refs):
    size, _, width = early_ref.shape
    weight_out, bias_out, early_out, late_out = refs
    flat = lambda ref, m: ref[:, 8 * m : 8 * (m + 1), :].reshape(size * 8, width)
    activity = flat(early_ref, 4).astype(BF16).T
    for m in range(6):
        slots = flat(late_ref, m) if m < 2 else flat(early_ref, m - 2)
        lanes = slice(m * width, (m + 1) * width)
        weight_out[:, lanes] = dot(activity, slots.astype(BF16))
        bias_out[:, lanes] = column_sum(slots)
    early_out[...] = jnp.sum(early_ref[:, 40:48, :], axis=0)
    late_out[...] = jnp.sum(late_ref[:, 16:24, :], axis=0)


def modulate(early, late):
    width = early.shape[2]
    shapes = [(width, 6 * width), (1, 6 * width), (8, width), (8, width)]
    return pl.pallas_call(
        modulate_kernel,
        out_shape=[jax.ShapeDtypeStruct(s, F32) for s in shapes],
        compiler_params=params(40),
        cost_estimate=cost(0.1),
        name="modulate",
    )(early, late)


def xor_permute(value, mask, size):
    return lax.ppermute(value, ("rows", "band"), [(i, i ^ mask) for i in range(size)])


def stages_of(rows, bands):
    band_bits, bits = bands.bit_length() - 1, (rows * bands).bit_length() - 1
    stages = [[band_bits]]
    for low, high in ((band_bits + 1, bits), (0, band_bits)):
        if (high - low) % 2:
            stages.append([low])
            low += 1
        stages += [[b, b + 1] for b in range(low, high, 2)]
    return stages


def digit_of(me, stage):
    return sum(((me >> b) & 1) << i for i, b in enumerate(stage))


def mask_of(t, stage):
    return sum(((t >> i) & 1) << b for i, b in enumerate(stage))


def fold_kernel(count, *refs):
    total = refs[0][...].astype(F32)
    for ref in refs[1:count]:
        total = total + ref[...].astype(F32)
    outs = refs[count:]
    rows = total.shape[0] // len(outs)
    for j, out in enumerate(outs):
        out[...] = total[j * rows : (j + 1) * rows].astype(BF16)


def fold(arrays, parts):
    rows, width = arrays[0].shape
    shape = jax.ShapeDtypeStruct((rows // parts, width), BF16)
    found = pl.pallas_call(
        partial(fold_kernel, len(arrays)),
        out_shape=[shape] * parts,
        compiler_params=params(32),
        cost_estimate=cost(0.1),
        name="fold",
    )(*arrays)
    return list(found)


def after(value, *others):
    return lax.optimization_barrier((value, others))[0]


def join_kernel(count, *refs):
    rows = refs[0].shape[0]
    for j in range(count):
        refs[count][j * rows : (j + 1) * rows, :] = refs[j][...]


def join(arrays):
    rows, width = arrays[0].shape
    return pl.pallas_call(
        partial(join_kernel, len(arrays)),
        out_shape=jax.ShapeDtypeStruct((rows * len(arrays), width), BF16),
        compiler_params=params(32),
        cost_estimate=cost(0.1),
        name="join",
    )(*arrays)


class Sum:
    def __init__(self, stages, size, parts):
        self.stages, self.size, self.at = stages, size, 0
        self.scattered = False
        self.steps = self.left = 2 * len(stages) - 1
        self.send(parts)

    def send(self, parts):
        stage = self.stages[self.at]
        self.held = [parts[0]] + [
            xor_permute(part, mask_of(t, stage), self.size) for t, part in enumerate(parts) if t
        ]

    def step(self, extra=None, done=()):
        held = list(after(self.held, *done)) if done else self.held
        self.left -= 1
        self.at += -1 if self.scattered else 1
        if not self.scattered and self.at < len(self.stages):
            parts = fold(held, 1 << len(self.stages[self.at]))
            self.send(parts)
            return parts
        if not self.scattered:
            self.scattered = True
            self.at -= 1
            value = fold(held, 1)[0]
            if extra is not None:
                value = jnp.concatenate([value, extra], axis=0)
        else:
            value = join(held)
        self.send([value] * (1 << len(self.stages[self.at])))
        return [value]


def body(
    patches,
    condition_table,
    condition_index,
    image_lengths,
    modulate_weight,
    modulate_bias,
    triple_weight,
    query_bias,
    value_bias,
    mixer_weight,
    mixer_bias,
    hidden_weight,
    hidden_bias,
    output_weight,
    output_bias,
    cotangent,
):
    band = lax.axis_index("band")
    n = lax.axis_size("band")
    size = n * lax.axis_size("rows")
    everyone = lax.axis_index(("rows", "band"))
    rows, band_length, width = patches.shape
    ff = hidden_weight.shape[1]
    length = band_length * n
    big = length // 2
    chunk = band_length // (2 * HALF)
    assert length == 2 * HALF * BLOCK
    plan = Plan(rows, n)
    units, total = plan.units(), plan.total
    assert units[0][1] == HALF
    stages = stages_of(size // n, n)
    relative = jnp.int32(0)
    for stage in stages:
        relative = (relative << len(stage)) | digit_of(everyone, stage)
    relative = relative.astype(jnp.int32).reshape(1)

    def deal(pieces):
        return lax.all_to_all(pieces, "band", 0, 0, tiled=True)

    me = band.astype(jnp.int32).reshape(1)
    packed = pack(plan, chunk, big, me, image_lengths, patches, True)
    x_pieces = [p if s == 0 else xor_permute(p, s, size) for s, p in enumerate(packed)]

    mods, activity, flags = prepare(
        plan,
        big,
        me,
        image_lengths,
        condition_index,
        condition_table,
        modulate_weight,
        modulate_bias,
    )
    c_pieces = deal(pack(plan, chunk, big, me, image_lengths, after(cotangent, mods, x_pieces[1:TIE]), False))

    attended, xs, mixes = [], [], []
    others = [[] for _ in units]
    if plan.group > 1:
        own = collect(n, plan.whole * HALF, plan.own, chunk, me, x_pieces)
        others[-1] = [xor_permute(own, t, size) for t in range(1, plan.group)]
    for j, (name, count) in enumerate(units):
        lo = j * HALF
        found = attend(
            n,
            j,
            lo,
            count,
            HALF,
            chunk,
            me,
            flags,
            x_pieces,
            others[j],
            mods,
            triple_weight,
            query_bias,
            value_bias,
        )
        xs.append(found[0])
        attended.append(found[1:8])
        mixes.append(found[8])

    valid = None
    if plan.idle:
        valid = (plan.half_row("shared", band) < plan.halves).astype(F32).reshape(1)

    weights = [
        mixer_weight,
        mixer_bias,
        hidden_weight,
        hidden_bias,
        output_weight,
        output_bias,
    ]
    out_pieces, fed = feed(
        units,
        n,
        chunk,
        size,
        relative,
        valid,
        xs,
        mixes,
        c_pieces,
        mods,
        activity,
        weights,
    )
    middle_grad, mixed_grad, first, second, mixer_grad, feed_small = fed
    out_back = deal(out_pieces)
    feed_sum = Sum(stages, size, [first, second])

    own, others, begun = None, [], []
    token = feed_sum.step()
    mixed_grad = after(mixed_grad, *token)
    if len(units) > 1:
        kept, low = attended[1], HALF
        found = shared_back(units[1][1], HALF, flags, kept, mixed_grad, low, triple_weight)
        own, others = found[0], [xor_permute(o, t + 1, size) for t, o in enumerate(found[1:-2])]
        begun = found[-2:]
        token = feed_sum.step(feed_small, done=(own,))
    grouped, sums, earlier = [], [], []
    for p in range(PAIRS):
        grad = after(mixed_grad, *token, *(others if p == 1 else []))
        found = whole_back(
            size, relative, p, flags, attended[0], grad, begun, mixer_grad, earlier
        )
        grouped.append(found[:3])
        sums.append(found[3])
        if p < PAIRS - 1:
            earlier.append(found[4])
            token = feed_sum.step(feed_small, done=(found[0],))
    last_sum = Sum(stages, size, found[4:6])
    token = feed_sum.step(feed_small, done=(found[3],))
    parts = [grouped[p][m] for m in range(3) for p in range(PAIRS)]
    grad_pieces, last_small = finish(
        units,
        n,
        chunk,
        xs,
        parts,
        triple_weight,
        own,
        others,
        sums,
        after(middle_grad, out_back, *token),
        mods,
    )
    grad_back = deal(grad_pieces)
    feed_chunk, last_chunk = (padded(r, size) // size for r in (2 * ff, 4 * width))
    last_sum.step(last_small, done=(last_small,))
    while feed_sum.left:
        token = feed_sum.step(feed_small, done=token)
    block_out = unpack(plan, chunk, big, image_lengths, out_back, BF16)
    output_w_grad, hidden_w_grad, early = settle(
        size, feed_chunk, relative, feed_sum.held, [(ff, width), (width, ff)]
    )
    patch_grad = unpack(plan, chunk, big, image_lengths, grad_back, F32)
    while last_sum.left:
        token = ()
        if last_sum.left == 2:
            token = (grad_back, block_out, output_w_grad)
        if last_sum.left == 1:
            token = (patch_grad,)
        last_sum.step(last_small, done=token)
    triple_w_grad, mixer_w_grad, late = settle(
        size, last_chunk, relative, last_sum.held, [(width, 3 * width), (width, width)]
    )
    modulate_w_grad, modulate_b_grad, feed_sums, last_sums = modulate(early, late)
    return (
        block_out,
        patch_grad,
        modulate_w_grad,
        modulate_b_grad.reshape(-1),
        triple_w_grad,
        last_sums[0],
        last_sums[1],
        mixer_w_grad,
        feed_sums[1 + ff // width],
        hidden_w_grad,
        feed_sums[1 : 1 + ff // width].reshape(-1),
        output_w_grad,
        feed_sums[0],
    )


def solution(mesh):
    return jax.shard_map(
        body,
        mesh=mesh,
        in_specs=(
            P("rows", None, "band"),
            P(),
            P("rows", None),
            P("rows", None),
            P(),
            P(),
            P(),
            P(),
            P(),
            P(),
            P(),
            P(),
            P(),
            P(),
            P(),
            P("rows", None, "band"),
        ),
        out_specs=(
            P("rows", None, "band"),
            P("rows", None, "band"),
            P(),
            P(),
            P(),
            P(),
            P(),
            P(),
            P(),
            P(),
            P(),
            P(),
            P(),
        ),
        check_vma=False,
    )
```

time: 382 us -> 276 us (0.72)
  starting transfers between devices: 142 us -> 59.7 us
  local copies, waits for them, and re-layouts: 34.1 us -> 13 us
  waiting for transfers between devices: 57.7 us -> 71.1 us
  other arithmetic: 11.6 us -> 0.65 us
  Pallas kernels: 120 us -> 127 us
  matrix products: 5.28 us -> 0 us
    ppermute x93 -> x33, starting transfers between devices: 142 us -> 40.3 us  [xor_permute(): lax.ppermute(value, ('rows', 'band'), [(i, i ^ mask) for i in range(size)])]
    all_to_all x0 -> x3, starting transfers between devices: none -> 19.3 us  [deal(): return lax.all_to_all(pieces, 'band', 0, 0, tiled=True)]
    ppermute x93 -> x33, waiting for transfers between devices: 57.7 us -> 71.1 us  [xor_permute(): lax.ppermute(value, ('rows', 'band'), [(i, i ^ mask) for i in range(size)])]
    slice x13 -> x2, local copies, waits for them, and re-layouts: 9.5 us -> 0.61 us  [the longest x1 0.61 us: body(): feed_sums[0]]
    pallas_call x8 -> x29, Pallas kernels: 115 us -> 123 us  [the longest x2 31.6 us: attend(): pl.pallas_call(partial(attend_kernel, n, unit, low, nq, nk, chunk, width)...]
    reshape x6 -> x1, local copies, waits for them, and re-layouts: 6.86 us -> 0.61 us  [body(): feed_sums[1:1 + ff // width].reshape(-1)]
    dot_general x3 -> x0, matrix products: 5.28 us -> none  [the longest x2 2.81 us: dot(): return jnp.dot(left, right, preferred_element_type=F32)]
    convert_element_type x8 -> x0, other arithmetic: 4.32 us -> none  [the longest x4 1.85 us: reduce_scatter(): value = mine.astype(BF16)]
  transfers between devices with their start and end apart: 93 -> 36, of which waited for: 30 -> 17; matrix products, arithmetic and copies ran while one was open for 9% -> 0% of each run, Pallas kernels for 23% -> 34%
where the time goes in v2:
time: 276 us; the launch traced here: 273 us
  Pallas kernels  127 us (46%)
  waiting for transfers between devices  71.1 us (26%)
  starting transfers between devices  59.7 us (22%)
  local copies, waits for them, and re-layouts  13 us (5%)
    ppermute x33, waiting for transfers between devices, xor_permute(): lax.ppermute(value, ('rows', 'band'), [(i, i ^ mask) for i in range(size)])  71.1 us
    ppermute x33, starting transfers between devices, xor_permute(): lax.ppermute(value, ('rows', 'band'), [(i, i ^ mask) for i in range(size)])  40.3 us
    pallas_call x2, Pallas kernels, attend(): pl.pallas_call(partial(attend_kernel, n, unit, low, nq, nk, chunk, width)...  31.6 us
    pallas_call x3, Pallas kernels, whole_back(): pl.pallas_call(partial(whole_back_kernel, size, bool(begun), last), grid=...  28 us
    pallas_call x1, Pallas kernels, feed(): pl.pallas_call(partial(feed_kernel, units, n, chunk, width, size, valid i...  27 us
    all_to_all x3, starting transfers between devices, deal(): return lax.all_to_all(pieces, 'band', 0, 0, tiled=True)  19.3 us
    pallas_call x1, Pallas kernels, shared_back(): pl.pallas_call(partial(shared_back_kernel, nq, nk), grid=(PAIRS,), in_spe...  13.6 us
    unnamed x58, local copies, waits for them, and re-layouts  11.8 us
  transfers between devices with their start and end apart: 36, of which 17 were waited for; matrix products, arithmetic and copies ran while one was open for 0% of the time, Pallas kernels for 34%

profile of v2, /device:TPU:0, one launch (start us, length us, event | category | flops | bytes accessed | tf_op | source)
XLA Modules:
  0.0 273.1 jit_solution(15038084799313277270)
XLA Ops:
  3.9 3.0 %collective-permute-start = (bf16[6,32,384]{2,1,0:T(8,128)(2,1)S(1)}, bf16[6,32,384]{2,1,0:T(8,128)(2,1)S(1)}, u32[]{:S(2)}, u32[]{:S(2)}) collective-permute-start(bf16[6,32,384]{2,1,0:T(8,128)(2,1)S(1)} %get-tuple-element.127), channel_id=1, source_target_pairs={{0,1},{1,0},{2,3},{3,2},{4,5},{5,4},{6,7},{7,6},{8,9},{9,8},{10,11... | collective-permute-start | bytes 442376 | tf_op jit(solution)/shard_map/ppermute | solution.py:887
  6.9 1.6 collective-permute-start.1
  8.5 3.0 %collective-permute-start.3 = (bf16[6,32,384]{2,1,0:T(8,128)(2,1)S(1)}, bf16[6,32,384]{2,1,0:T(8,128)(2,1)S(1)}, u32[]{:S(2)}, u32[]{:S(2)}) collective-permute-start(bf16[6,32,384]{2,1,0:T(8,128)(2,1)S(1)} %get-tuple-element.130), channel_id=1, source_target_pairs={{0,4},{1,5},{2,6},{3,7},{4,0},{5,1},{6,2},{7,3},{8,12},{9,13},{10,... | collective-permute-start | bytes 442376 | tf_op jit(solution)/shard_map/ppermute | solution.py:887
  12.8 3.6 %collective-permute-start.5 = (bf16[6,32,384]{2,1,0:T(8,128)(2,1)S(1)}, bf16[6,32,384]{2,1,0:T(8,128)(2,1)S(1)}, u32[]{:S(2)}, u32[]{:S(2)}) collective-permute-start(bf16[6,32,384]{2,1,0:T(8,128)(2,1)S(1)} %get-tuple-element.132), channel_id=1, source_target_pairs={{0,6},{1,7},{2,4},{3,5},{4,2},{5,3},{6,0},{7,1},{8,14},{9,15},{10,... | collective-permute-start | bytes 442376 | tf_op jit(solution)/shard_map/ppermute | solution.py:887
  16.4 2.5 collective-permute-done.1.refs_2_
  19.8 1.5 copy-done.2
  23.5 1.4 prepare.1
  26.6 6.3 %collective-permute-done.4.refs_5_ = bf16[6,32,384]{2,1,0:T(8,128)(2,1)S(1)} collective-permute-done((bf16[6,32,384]{2,1,0:T(8,128)(2,1)S(1)}, bf16[6,32,384]{2,1,0:T(8,128)(2,1)S(1)}, u32[]{:S(2)}, u32[]{:S(2)}) %collective-permute-start.4) | collective-permute-done | bytes 147488 | tf_op jit(solution)/shard_map/ppermute | solution.py:887
  33.0 1.9 pack.3
  34.9 8.8 %all-to-all-start = ((bf16[8,6,32,384]{3,2,1,0:T(8,128)(2,1)}), bf16[8,6,32,384]{3,2,1,0:T(8,128)(2,1)S(1)}, u32[]{:S(2)}, u32[]{:S(2)}) async-start(bf16[8,6,32,384]{3,2,1,0:T(8,128)(2,1)} %pack.3), calls=%async_computation | async-start | bytes 2359296 | tf_op jit(solution)/shard_map/all_to_all | solution.py:1024
  43.9 2.1 collective-permute-start.7
  46.0 18.6 %attend.2 = (bf16[1024,384]{1,0:T(8,128)(2,1)}, bf16[384,1024]{1,0:T(8,128)(2,1)}, bf16[3,1024,128]{2,1,0:T(8,128)(2,1)}, bf16[3,1024,128]{2,1,0:T(8,128)(2,1)},...) custom-call(s32[1]{0:T(128)} %bitcast.1.me_ref, ...), custom_call_target="tpu_custom_call" | custom-call | bytes 300000 | tf_op jit(solution)/shard_map/attend/pallas_call | solution.py:341
  66.2 13.0 %attend.3 = (bf16[1024,384]{1,0:T(8,128)(2,1)}, bf16[384,1024]{1,0:T(8,128)(2,1)}, bf16[3,512,128]{2,1,0:T(8,128)(2,1)}, bf16[3,1024,128]{2,1,0:T(8,128)(2,1)}, ...) custom-call(s32[1]{0:T(128)} %bitcast.1.me_ref, ...), custom_call_target="tpu_custom_call" | custom-call | bytes 300000 | tf_op jit(solution)/shard_map/attend/pallas_call | solution.py:341
  80.2 27.0 %feed.1 = (bf16[8,6,32,384]{3,2,1,0:T(8,128)(2,1)}, f32[1536,384]{1,0:T(8,128)}, bf16[1536,384]{1,0:T(8,128)(2,1)}, bf16[1536,384]{1,0:T(8,128)(2,1)}, bf16[1536...) custom-call(s32[1]{0:T(128)} %bitcast.me_ref.refs_10_, ...), custom_call_target="tpu_custom_call" | custom-call | bytes 300000 | tf_op jit(solution)/shard_map/feed/pallas_call | solution.py:698
  107.2 3.1 %collective-permute-done.8.refs_1_ = bf16[1536,384]{1,0:T(8,128)(2,1)S(1)} collective-permute-done((bf16[1536,384]{1,0:T(8,128)(2,1)}, bf16[1536,384]{1,0:T(8,128)(2,1)S(1)}, u32[]{:S(2)}, u32[]{:S(2)}) %collective-permute-start.8) | collective-permute-done | bytes 1179680 | tf_op jit(solution)/shard_map/ppermute | solution.py:887
  111.9 4.7 %all-to-all-start.1 = ((bf16[8,6,32,384]{3,2,1,0:T(8,128)(2,1)}), bf16[8,6,32,384]{3,2,1,0:T(8,128)(2,1)S(1)}, u32[]{:S(2)}, u32[]{:S(2)}) async-start(bf16[8,6,32,384]{3,2,1,0:T(8,128)(2,1)} %get-tuple-element.141), calls=%async_computation.1 | async-start | bytes 2359296 | tf_op jit(solution)/shard_map/all_to_all | solution.py:1024
  116.6 13.6 %shared_back.1 = (f32[512,384]{1,0:T(8,128)}, bf16[512,384]{1,0:T(8,128)(2,1)}, f32[3,384,384]{2,1,0:T(8,128)}, f32[3,8,384]{2,1,0:T(8,128)}) custom-call(s32[2]{0:T(128)} %copy-done.19, bf16[6,1024,512]{2,1,0:T(8,128)(2,1)} %get-tuple-element.154.refs_0_, bf16[3,512,128]{2,1,0:T(8,128)(2,1)} %get-tuple-element.155.refs_1_, ...), custom_call_target="tpu_custom_call" | custom-call | bytes 300000 | tf_op jit(solution)/shard_map/shared_back/pallas_call | solution.py:503
  130.2 2.1 collective-permute-start.11
  132.6 8.7 %whole_back.3 = (bf16[1024,128]{1,0:T(8,128)(2,1)}, bf16[1024,128]{1,0:T(8,128)(2,1)}, bf16[1024,128]{1,0:T(8,128)(2,1)}, f32[8,384]{1,0:T(8,128)}, f32[384,384]{1,0:T(8,128)}) custom-call(s32[2]{0:T(128)} %copy-done.19, bf16[6,1024,1024]{2,1,0:T(8,128)(2,1)} %get-tuple-element.142.refs_0_, bf16[3,1024,128]{2,1,0:T(8,128)(2,1)} %get-tuple-element.143.refs_1_, ...), custom_call_target="tpu_custom_call" | custom-call | bytes 300000 | tf_op jit(solution)/shard_map/whole_back/pallas_call | solution.py:535
  141.3 9.6 %collective-permute-done.10.refs_1_ = bf16[384,384]{1,0:T(8,128)(2,1)S(1)} collective-permute-done((bf16[384,384]{1,0:T(8,128)(2,1)S(1)}, bf16[384,384]{1,0:T(8,128)(2,1)S(1)}, u32[]{:S(2)}, u32[]{:S(2)}) %collective-permute-start.10) | collective-permute-done | bytes 294944 | tf_op jit(solution)/shard_map/ppermute | solution.py:887
  150.9 2.2 collective-permute-start.12
  154.1 1.4 collective-permute-start.14
  155.5 9.1 %whole_back.4 = (bf16[1024,128]{1,0:T(8,128)(2,1)}, bf16[1024,128]{1,0:T(8,128)(2,1)}, bf16[1024,128]{1,0:T(8,128)(2,1)}, f32[8,384]{1,0:T(8,128)}, f32[384,384]{1,0:T(8,128)}) custom-call(s32[2]{0:T(128)} %copy-done.19, bf16[6,1024,1024]{2,1,0:T(8,128)(2,1)} %get-tuple-element.142.refs_0_, bf16[3,1024,128]{2,1,0:T(8,128)(2,1)} %get-tuple-element.143.refs_1_, ...), custom_call_target="tpu_custom_call" | custom-call | bytes 300000 | tf_op jit(solution)/shard_map/whole_back/pallas_call | solution.py:535
  165.9 1.9 collective-permute-start.16
  167.8 1.4 collective-permute-start.17
  169.2 10.1 %whole_back.5 = (bf16[1024,128]{1,0:T(8,128)(2,1)}, bf16[1024,128]{1,0:T(8,128)(2,1)}, bf16[1024,128]{1,0:T(8,128)(2,1)}, f32[8,384]{1,0:T(8,128)}, bf16[768,384]{1,0:T(8,128)(2,1)}, /*index=5*/bf16[768,384]{1,0:T(8,128)(2,1)}) custom-call(s32[2]{0:T(128)} %copy-done.19, bf16[6,1024,1024]{2,1,0:T(8,128)(2,1)} %get-tuple-element.142.refs_0_, ...), custom_call_target="tpu_custom_call" | custom-call | bytes 300000 | tf_op jit(solution)/shard_map/whole_back/pallas_call | solution.py:535
  179.5 9.8 %collective-permute-done.18.refs_1_ = bf16[576,384]{1,0:T(8,128)(2,1)S(1)} collective-permute-done((bf16[576,384]{1,0:T(8,128)(2,1)S(1)}, bf16[576,384]{1,0:T(8,128)(2,1)S(1)}, u32[]{:S(2)}, u32[]{:S(2)}) %collective-permute-start.18) | collective-permute-done | bytes 442400 | tf_op jit(solution)/shard_map/ppermute | solution.py:887
  189.7 8.5 %finish.1 = (bf16[8,6,32,384]{3,2,1,0:T(8,128)(2,1)}, bf16[32,384]{1,0:T(8,128)(2,1)}) custom-call(bf16[1024,384]{1,0:T(8,128)(2,1)} %get-tuple-element.135.refs_0_, bf16[1024,384]{1,0:T(8,128)(2,1)} %get-tuple-element.136.refs_1_, bf16[1024,128]{1,0:T(8,128)(2,1)} %get-tuple-element.170.refs_2_, bf16[1024,128]{1,0:T(8,128)(2,1)} %get-tuple-element.179.refs_3_, ...), custom_call_target="tpu_custom_call" | custom-call | bytes 300000 | tf_op jit(solution)/shard_map/finish/pallas_call | solution.py:800
  198.1 5.7 %all-to-all-start.2 = ((bf16[8,6,32,384]{3,2,1,0:T(8,128)(2,1)}), bf16[8,6,32,384]{3,2,1,0:T(8,128)(2,1)S(1)}, u32[]{:S(2)}, u32[]{:S(2)}) async-start(bf16[8,6,32,384]{3,2,1,0:T(8,128)(2,1)} %get-tuple-element.205), calls=%async_computation.2 | async-start | bytes 2359296 | tf_op jit(solution)/shard_map/all_to_all | solution.py:1024
  203.9 4.1 %collective-permute-done.19.refs_1_ = bf16[1152,384]{1,0:T(8,128)(2,1)} collective-permute-done((bf16[1152,384]{1,0:T(8,128)(2,1)S(1)}, bf16[1152,384]{1,0:T(8,128)(2,1)}, u32[]{:S(2)}, u32[]{:S(2)}) %collective-permute-start.19) | collective-permute-done | bytes 884768 | tf_op jit(solution)/shard_map/ppermute | solution.py:887
  208.0 1.3 join.8.refs_0_
  209.9 4.0 %collective-permute-done.21.refs_1_ = bf16[768,384]{1,0:T(8,128)(2,1)S(1)} collective-permute-done((bf16[768,384]{1,0:T(8,128)(2,1)S(1)}, bf16[768,384]{1,0:T(8,128)(2,1)S(1)}, u32[]{:S(2)}, u32[]{:S(2)}) %collective-permute-start.21) | collective-permute-done | bytes 589856 | tf_op jit(solution)/shard_map/ppermute | solution.py:887
  214.4 8.8 %collective-permute-done.22.refs_1_ = bf16[384,384]{1,0:T(8,128)(2,1)S(1)} collective-permute-done((bf16[384,384]{1,0:T(8,128)(2,1)S(1)}, bf16[384,384]{1,0:T(8,128)(2,1)S(1)}, u32[]{:S(2)}, u32[]{:S(2)}) %collective-permute-start.22) | collective-permute-done | bytes 294944 | tf_op jit(solution)/shard_map/ppermute | solution.py:887
  223.9 4.6 %collective-permute-done.23.refs_1_ = bf16[192,384]{1,0:T(8,128)(2,1)S(1)} collective-permute-done((bf16[192,384]{1,0:T(8,128)(2,1)S(1)}, bf16[192,384]{1,0:T(8,128)(2,1)S(1)}, u32[]{:S(2)}, u32[]{:S(2)}) %collective-permute-start.23) | collective-permute-done | bytes 147488 | tf_op jit(solution)/shard_map/ppermute | solution.py:887
  229.4 3.5 %collective-permute-start.25 = (bf16[48,384]{1,0:T(8,128)(2,1)S(1)}, bf16[48,384]{1,0:T(8,128)(2,1)S(1)}, u32[]{:S(2)}, u32[]{:S(2)}) collective-permute-start(bf16[48,384]{1,0:T(8,128)(2,1)S(1)} %get-tuple-element.222), channel_id=1, source_target_pairs={{0,4},{1,5},{2,6},{3,7},{4,0},{5,1},{6,2},{7,3},{8,12},{9,13},{10,... | collective-permute-start | bytes 110600 | tf_op jit(solution)/shard_map/ppermute | solution.py:887
  233.3 1.5 collective-permute-done.25.refs_2_
  234.9 4.0 %collective-permute-done.26.refs_3_ = bf16[48,384]{1,0:T(8,128)(2,1)S(1)} collective-permute-done((bf16[48,384]{1,0:T(8,128)(2,1)S(1)}, bf16[48,384]{1,0:T(8,128)(2,1)S(1)}, u32[]{:S(2)}, u32[]{:S(2)}) %collective-permute-start.26) | collective-permute-done | bytes 36896 | tf_op jit(solution)/shard_map/ppermute | solution.py:887
  239.9 3.5 %collective-permute-start.29 = (bf16[80,384]{1,0:T(8,128)(2,1)S(1)}, bf16[80,384]{1,0:T(8,128)(2,1)S(1)}, u32[]{:S(2)}, u32[]{:S(2)}) collective-permute-start(bf16[80,384]{1,0:T(8,128)(2,1)S(1)} %pad_maximum_fusion.1.refs_0_), channel_id=1, source_target_pairs={{0,6},{1,7},{2,4},{3,5},{4,2},{5,3},{6,0},{7,1},{8,14},{9,15},{10,... | collective-permute-start | bytes 184328 | tf_op jit(solution)/shard_map/ppermute | solution.py:887
  244.2 2.0 collective-permute-done.29.refs_3_
  246.2 1.7 collective-permute-start.30
  248.0 1.9 unpack.2
  249.8 3.0 %settle.2 = (f32[1536,384]{1,0:T(8,128)}, f32[384,1536]{1,0:T(8,128)}, f32[32,48,384]{2,1,0:T(8,128)S(1)}) custom-call(s32[1]{0:T(128)} %bitcast.me_ref.refs_10_, bf16[2304,384]{1,0:T(8,128)(2,1)S(1)} %join.8.refs_0_, bf16[2304,384]{1,0:T(8,128)(2,1)S(1)} %collective-permute-done.20.refs_1_), custom_call_target="tpu_custom_call" | custom-call | bytes 300000 | tf_op jit(solution)/shard_map/settle/pallas_call | solution.py:847
  252.8 1.4 copy-done
  254.9 2.2 unpack.3
  257.2 6.5 %collective-permute-done.31.refs_1_ = bf16[640,384]{1,0:T(8,128)(2,1)S(1)} collective-permute-done((bf16[640,384]{1,0:T(8,128)(2,1)S(1)}, bf16[640,384]{1,0:T(8,128)(2,1)S(1)}, u32[]{:S(2)}, u32[]{:S(2)}) %collective-permute-start.31) | collective-permute-done | bytes 491552 | tf_op jit(solution)/shard_map/ppermute | solution.py:887
  263.8 2.6 collective-permute-done.32.refs_1_
  266.4 2.0 settle.3
  268.4 2.6 modulate.1
  (119 shorter events, 24.3 us)
Async XLA Ops:
  2.6 30.4 %copy-start.14 = (bf16[6,256,384]{2,1,0:T(8,128)(2,1)S(1)}, bf16[6,256,384]{2,1,0:T(8,128)(2,1)}, u32[]{:S(2)}) copy-start(bf16[6,256,384]{2,1,0:T(8,128)(2,1)} %x_ref.2) | copy-start | bytes 3538948
  3.9 39.8 %copy-start.3 = (bf16[6,32,384]{2,1,0:T(8,128)(2,1)}, bf16[6,32,384]{2,1,0:T(8,128)(2,1)S(1)}, u32[]{:S(2)}) copy-start(bf16[6,32,384]{2,1,0:T(8,128)(2,1)S(1)} %get-tuple-element.126.refs_0_) | copy-start | bytes 442372
  3.9 8.9 %collective-permute-start = (bf16[6,32,384]{2,1,0:T(8,128)(2,1)S(1)}, bf16[6,32,384]{2,1,0:T(8,128)(2,1)S(1)}, u32[]{:S(2)}, u32[]{:S(2)}) collective-permute-start(bf16[6,32,384]{2,1,0:T(8,128)(2,1)S(1)} %get-tuple-element.127), channel_id=1, source_target_pairs={{0,1},{1,0},{2,3},{3,2},{4,5},{5,4},{6,7},{7,6},{8,9},{9,8},{10,11... | collective-permute-start | bytes 442376 | tf_op jit(solution)/shard_map/ppermute | solution.py:887
  6.9 12.0 %collective-permute-start.1 = (bf16[6,32,384]{2,1,0:T(8,128)(2,1)S(1)}, bf16[6,32,384]{2,1,0:T(8,128)(2,1)S(1)}, u32[]{:S(2)}, u32[]{:S(2)}) collective-permute-start(bf16[6,32,384]{2,1,0:T(8,128)(2,1)S(1)} %get-tuple-element.128), channel_id=1, source_target_pairs={{0,2},{1,3},{2,0},{3,1},{4,6},{5,7},{6,4},{7,5},{8,10},{9,11},{10,... | collective-permute-start | bytes 442376 | tf_op jit(solution)/shard_map/ppermute | solution.py:887
  8.5 18.1 %collective-permute-start.2 = (bf16[6,32,384]{2,1,0:T(8,128)(2,1)S(1)}, bf16[6,32,384]{2,1,0:T(8,128)(2,1)S(1)}, u32[]{:S(2)}, u32[]{:S(2)}) collective-permute-start(bf16[6,32,384]{2,1,0:T(8,128)(2,1)S(1)} %get-tuple-element.129), channel_id=1, source_target_pairs={{0,3},{1,2},{2,1},{3,0},{4,7},{5,6},{6,5},{7,4},{8,11},{9,10},{10,... | collective-permute-start | bytes 442376 | tf_op jit(solution)/shard_map/ppermute | solution.py:887
  8.5 18.1 %collective-permute-start.3 = (bf16[6,32,384]{2,1,0:T(8,128)(2,1)S(1)}, bf16[6,32,384]{2,1,0:T(8,128)(2,1)S(1)}, u32[]{:S(2)}, u32[]{:S(2)}) collective-permute-start(bf16[6,32,384]{2,1,0:T(8,128)(2,1)S(1)} %get-tuple-element.130), channel_id=1, source_target_pairs={{0,4},{1,5},{2,6},{3,7},{4,0},{5,1},{6,2},{7,3},{8,12},{9,13},{10,... | collective-permute-start | bytes 442376 | tf_op jit(solution)/shard_map/ppermute | solution.py:887
  11.5 21.5 %collective-permute-start.4 = (bf16[6,32,384]{2,1,0:T(8,128)(2,1)S(1)}, bf16[6,32,384]{2,1,0:T(8,128)(2,1)S(1)}, u32[]{:S(2)}, u32[]{:S(2)}) collective-permute-start(bf16[6,32,384]{2,1,0:T(8,128)(2,1)S(1)} %get-tuple-element.131), channel_id=1, source_target_pairs={{0,5},{1,4},{2,7},{3,6},{4,1},{5,0},{6,3},{7,2},{8,13},{9,12},{10,... | collective-permute-start | bytes 442376 | tf_op jit(solution)/shard_map/ppermute | solution.py:887
  12.8 31.0 %copy-start.4 = (bf16[6,32,384]{2,1,0:T(8,128)(2,1)}, bf16[6,32,384]{2,1,0:T(8,128)(2,1)S(1)}, u32[]{:S(2)}) copy-start(bf16[6,32,384]{2,1,0:T(8,128)(2,1)S(1)} %collective-permute-done.refs_1_) | copy-start | bytes 442372
  12.8 20.2 %collective-permute-start.5 = (bf16[6,32,384]{2,1,0:T(8,128)(2,1)S(1)}, bf16[6,32,384]{2,1,0:T(8,128)(2,1)S(1)}, u32[]{:S(2)}, u32[]{:S(2)}) collective-permute-start(bf16[6,32,384]{2,1,0:T(8,128)(2,1)S(1)} %get-tuple-element.132), channel_id=1, source_target_pairs={{0,6},{1,7},{2,4},{3,5},{4,2},{5,3},{6,0},{7,1},{8,14},{9,15},{10,... | collective-permute-start | bytes 442376 | tf_op jit(solution)/shard_map/ppermute | solution.py:887
  18.9 24.9 %copy-start.5 = (bf16[6,32,384]{2,1,0:T(8,128)(2,1)}, bf16[6,32,384]{2,1,0:T(8,128)(2,1)S(1)}, u32[]{:S(2)}) copy-start(bf16[6,32,384]{2,1,0:T(8,128)(2,1)S(1)} %collective-permute-done.1.refs_2_) | copy-start | bytes 442372
  18.9 14.1 %collective-permute-start.6 = (bf16[6,32,384]{2,1,0:T(8,128)(2,1)S(1)}, bf16[6,32,384]{2,1,0:T(8,128)(2,1)S(1)}, u32[]{:S(2)}, u32[]{:S(2)}) collective-permute-start(bf16[6,32,384]{2,1,0:T(8,128)(2,1)S(1)} %get-tuple-element.133), channel_id=1, source_target_pairs={{0,7},{1,6},{2,5},{3,4},{4,3},{5,2},{6,1},{7,0},{8,15},{9,14},{10,... | collective-permute-start | bytes 442376 | tf_op jit(solution)/shard_map/ppermute | solution.py:887
  26.6 17.2 %copy-start.6 = (bf16[6,32,384]{2,1,0:T(8,128)(2,1)}, bf16[6,32,384]{2,1,0:T(8,128)(2,1)S(1)}, u32[]{:S(2)}) copy-start(bf16[6,32,384]{2,1,0:T(8,128)(2,1)S(1)} %collective-permute-done.2.refs_3_) | copy-start | bytes 442372
  26.6 17.2 %copy-start.7 = (bf16[6,32,384]{2,1,0:T(8,128)(2,1)}, bf16[6,32,384]{2,1,0:T(8,128)(2,1)S(1)}, u32[]{:S(2)}) copy-start(bf16[6,32,384]{2,1,0:T(8,128)(2,1)S(1)} %collective-permute-done.3.refs_4_) | copy-start | bytes 442372
  33.0 10.8 %copy-start.8 = (bf16[6,32,384]{2,1,0:T(8,128)(2,1)}, bf16[6,32,384]{2,1,0:T(8,128)(2,1)S(1)}, u32[]{:S(2)}) copy-start(bf16[6,32,384]{2,1,0:T(8,128)(2,1)S(1)} %collective-permute-done.4.refs_5_) | copy-start | bytes 442372
  33.0 10.8 %copy-start.9 = (bf16[6,32,384]{2,1,0:T(8,128)(2,1)}, bf16[6,32,384]{2,1,0:T(8,128)(2,1)S(1)}, u32[]{:S(2)}) copy-start(bf16[6,32,384]{2,1,0:T(8,128)(2,1)S(1)} %collective-permute-done.5.refs_6_) | copy-start | bytes 442372
  33.0 10.8 %copy-start.10 = (bf16[6,32,384]{2,1,0:T(8,128)(2,1)}, bf16[6,32,384]{2,1,0:T(8,128)(2,1)S(1)}, u32[]{:S(2)}) copy-start(bf16[6,32,384]{2,1,0:T(8,128)(2,1)S(1)} %collective-permute-done.6.refs_7_) | copy-start | bytes 442372
  34.9 44.3 %all-to-all-start = ((bf16[8,6,32,384]{3,2,1,0:T(8,128)(2,1)}), bf16[8,6,32,384]{3,2,1,0:T(8,128)(2,1)S(1)}, u32[]{:S(2)}, u32[]{:S(2)}) async-start(bf16[8,6,32,384]{3,2,1,0:T(8,128)(2,1)} %pack.3), calls=%async_computation | async-start | bytes 2359296 | tf_op jit(solution)/shard_map/all_to_all | solution.py:1024
  43.9 21.5 %collective-permute-start.7 = (bf16[512,384]{1,0:T(8,128)(2,1)S(1)}, bf16[512,384]{1,0:T(8,128)(2,1)S(1)}, u32[]{:S(2)}, u32[]{:S(2)}) collective-permute-start(bf16[512,384]{1,0:T(8,128)(2,1)S(1)} %collect.1), channel_id=1, source_target_pairs={{0,1},{1,0},{2,3},{3,2},{4,5},{5,4},{6,7},{7,6},{8,9},{9,8},{10,11... | collective-permute-start | bytes 1179656 | tf_op jit(solution)/shard_map/ppermute | solution.py:887
  107.2 3.1 %collective-permute-start.8 = (bf16[1536,384]{1,0:T(8,128)(2,1)}, bf16[1536,384]{1,0:T(8,128)(2,1)S(1)}, u32[]{:S(2)}, u32[]{:S(2)}) collective-permute-start(bf16[1536,384]{1,0:T(8,128)(2,1)} %get-tuple-element.150), channel_id=1, source_target_pairs={{0,8},{1,9},{2,10},{3,11},{4,12},{5,13},{6,14},{7,15},{8,0},{9,1},... | collective-permute-start | bytes 3538952 | tf_op jit(solution)/shard_map/ppermute | solution.py:887
  111.8 20.5 %collective-permute-start.9 = (bf16[768,384]{1,0:T(8,128)(2,1)S(1)}, bf16[768,384]{1,0:T(8,128)(2,1)S(1)}, u32[]{:S(2)}, u32[]{:S(2)}) collective-permute-start(bf16[768,384]{1,0:T(8,128)(2,1)S(1)} %get-tuple-element.152), channel_id=1, source_target_pairs={{0,16},{1,17},{2,18},{3,19},{4,20},{5,21},{6,22},{7,23},{8,24},{9,... | collective-permute-start | bytes 1769480 | tf_op jit(solution)/shard_map/ppermute | solution.py:887
  111.9 77.8 %all-to-all-start.1 = ((bf16[8,6,32,384]{3,2,1,0:T(8,128)(2,1)}), bf16[8,6,32,384]{3,2,1,0:T(8,128)(2,1)S(1)}, u32[]{:S(2)}, u32[]{:S(2)}) async-start(bf16[8,6,32,384]{3,2,1,0:T(8,128)(2,1)} %get-tuple-element.141), calls=%async_computation.1 | async-start | bytes 2359296 | tf_op jit(solution)/shard_map/all_to_all | solution.py:1024
  130.2 25.3 %collective-permute-start.11 = (bf16[512,384]{1,0:T(8,128)(2,1)}, bf16[512,384]{1,0:T(8,128)(2,1)S(1)}, u32[]{:S(2)}, u32[]{:S(2)}) collective-permute-start(bf16[512,384]{1,0:T(8,128)(2,1)} %get-tuple-element.177), channel_id=1, source_target_pairs={{0,1},{1,0},{2,3},{3,2},{4,5},{5,4},{6,7},{7,6},{8,9},{9,8},{10,11... | collective-permute-start | bytes 1179656 | tf_op jit(solution)/shard_map/ppermute | solution.py:887
  132.5 18.4 %collective-permute-start.10 = (bf16[384,384]{1,0:T(8,128)(2,1)S(1)}, bf16[384,384]{1,0:T(8,128)(2,1)S(1)}, u32[]{:S(2)}, u32[]{:S(2)}) collective-permute-start(bf16[384,384]{1,0:T(8,128)(2,1)S(1)} %get-tuple-element.165), channel_id=1, source_target_pairs={{0,1},{1,0},{2,3},{3,2},{4,5},{5,4},{6,7},{7,6},{8,9},{9,8},{10,11... | collective-permute-start | bytes 884744 | tf_op jit(solution)/shard_map/ppermute | solution.py:887
  150.9 13.7 %collective-permute-start.12 = (bf16[96,384]{1,0:T(8,128)(2,1)S(1)}, bf16[96,384]{1,0:T(8,128)(2,1)S(1)}, u32[]{:S(2)}, u32[]{:S(2)}) collective-permute-start(bf16[96,384]{1,0:T(8,128)(2,1)S(1)} %get-tuple-element.174), channel_id=1, source_target_pairs={{0,2},{1,3},{2,0},{3,1},{4,6},{5,7},{6,4},{7,5},{8,10},{9,11},{10,... | collective-permute-start | bytes 221192 | tf_op jit(solution)/shard_map/ppermute | solution.py:887
  153.1 11.6 %collective-permute-start.13 = (bf16[96,384]{1,0:T(8,128)(2,1)S(1)}, bf16[96,384]{1,0:T(8,128)(2,1)S(1)}, u32[]{:S(2)}, u32[]{:S(2)}) collective-permute-start(bf16[96,384]{1,0:T(8,128)(2,1)S(1)} %get-tuple-element.175), channel_id=1, source_target_pairs={{0,4},{1,5},{2,6},{3,7},{4,0},{5,1},{6,2},{7,3},{8,12},{9,13},{10,... | collective-permute-start | bytes 221192 | tf_op jit(solution)/shard_map/ppermute | solution.py:887
  154.1 10.6 %collective-permute-start.14 = (bf16[96,384]{1,0:T(8,128)(2,1)S(1)}, bf16[96,384]{1,0:T(8,128)(2,1)S(1)}, u32[]{:S(2)}, u32[]{:S(2)}) collective-permute-start(bf16[96,384]{1,0:T(8,128)(2,1)S(1)} %get-tuple-element.176), channel_id=1, source_target_pairs={{0,6},{1,7},{2,4},{3,5},{4,2},{5,3},{6,0},{7,1},{8,14},{9,15},{10,... | collective-permute-start | bytes 221192 | tf_op jit(solution)/shard_map/ppermute | solution.py:887
  164.7 14.6 %collective-permute-start.15 = (bf16[144,384]{1,0:T(8,128)(2,1)S(1)}, bf16[144,384]{1,0:T(8,128)(2,1)S(1)}, u32[]{:S(2)}, u32[]{:S(2)}) collective-permute-start(bf16[144,384]{1,0:T(8,128)(2,1)S(1)} %pad_maximum_fusion.refs_0_), channel_id=1, source_target_pairs={{0,2},{1,3},{2,0},{3,1},{4,6},{5,7},{6,4},{7,5},{8,10},{9,11},{10,... | collective-permute-start | bytes 331784 | tf_op jit(solution)/shard_map/ppermute | solution.py:887
  165.9 13.5 %collective-permute-start.16 = (bf16[144,384]{1,0:T(8,128)(2,1)S(1)}, bf16[144,384]{1,0:T(8,128)(2,1)S(1)}, u32[]{:S(2)}, u32[]{:S(2)}) collective-permute-start(bf16[144,384]{1,0:T(8,128)(2,1)S(1)} %pad_maximum_fusion.refs_0_), channel_id=1, source_target_pairs={{0,4},{1,5},{2,6},{3,7},{4,0},{5,1},{6,2},{7,3},{8,12},{9,13},{10,... | collective-permute-start | bytes 331784 | tf_op jit(solution)/shard_map/ppermute | solution.py:887
  167.8 11.6 %collective-permute-start.17 = (bf16[144,384]{1,0:T(8,128)(2,1)S(1)}, bf16[144,384]{1,0:T(8,128)(2,1)S(1)}, u32[]{:S(2)}, u32[]{:S(2)}) collective-permute-start(bf16[144,384]{1,0:T(8,128)(2,1)S(1)} %pad_maximum_fusion.refs_0_), channel_id=1, source_target_pairs={{0,6},{1,7},{2,4},{3,5},{4,2},{5,3},{6,0},{7,1},{8,14},{9,15},{10,... | collective-permute-start | bytes 331784 | tf_op jit(solution)/shard_map/ppermute | solution.py:887
  179.4 9.9 %collective-permute-start.18 = (bf16[576,384]{1,0:T(8,128)(2,1)S(1)}, bf16[576,384]{1,0:T(8,128)(2,1)S(1)}, u32[]{:S(2)}, u32[]{:S(2)}) collective-permute-start(bf16[576,384]{1,0:T(8,128)(2,1)S(1)} %join.6.refs_0_), channel_id=1, source_target_pairs={{0,1},{1,0},{2,3},{3,2},{4,5},{5,4},{6,7},{7,6},{8,9},{9,8},{10,11... | collective-permute-start | bytes 1327112 | tf_op jit(solution)/shard_map/ppermute | solution.py:887
  189.4 18.6 %collective-permute-start.19 = (bf16[1152,384]{1,0:T(8,128)(2,1)S(1)}, bf16[1152,384]{1,0:T(8,128)(2,1)}, u32[]{:S(2)}, u32[]{:S(2)}) collective-permute-start(bf16[1152,384]{1,0:T(8,128)(2,1)S(1)} %join.7.refs_0_), channel_id=1, source_target_pairs={{0,16},{1,17},{2,18},{3,19},{4,20},{5,21},{6,22},{7,23},{8,24},{9,... | collective-permute-start | bytes 2654216 | tf_op jit(solution)/shard_map/ppermute | solution.py:887
  198.1 56.1 %all-to-all-start.2 = ((bf16[8,6,32,384]{3,2,1,0:T(8,128)(2,1)}), bf16[8,6,32,384]{3,2,1,0:T(8,128)(2,1)S(1)}, u32[]{:S(2)}, u32[]{:S(2)}) async-start(bf16[8,6,32,384]{3,2,1,0:T(8,128)(2,1)} %get-tuple-element.205), calls=%async_computation.2 | async-start | bytes 2359296 | tf_op jit(solution)/shard_map/all_to_all | solution.py:1024
  209.3 29.6 %copy-start.27 = (bf16[32,384]{1,0:T(8,128)(2,1)S(1)}, bf16[32,384]{1,0:T(8,128)(2,1)}, u32[]{:S(2)}) copy-start(bf16[32,384]{1,0:T(8,128)(2,1)} %get-tuple-element.213) | copy-start | bytes 73732
  209.3 38.7 %copy-start.17 = (s32[6,8]{1,0:T(8,128)S(1)}, s32[6,8]{1,0:T(8,128)}, u32[]{:S(2)}) copy-start(s32[6,8]{1,0:T(8,128)} %lens_ref.9) | copy-start | bytes 580
  209.3 40.5 %collective-permute-start.20 = (bf16[2304,384]{1,0:T(8,128)(2,1)S(1)}, bf16[2304,384]{1,0:T(8,128)(2,1)S(1)}, u32[]{:S(2)}, u32[]{:S(2)}) collective-permute-start(bf16[2304,384]{1,0:T(8,128)(2,1)S(1)} %join.8.refs_0_), channel_id=1, source_target_pairs={{0,8},{1,9},{2,10},{3,11},{4,12},{5,13},{6,14},{7,15},{8,0},{9,1},... | collective-permute-start | bytes 5308424 | tf_op jit(solution)/shard_map/ppermute | solution.py:887
  209.4 4.5 %collective-permute-start.21 = (bf16[768,384]{1,0:T(8,128)(2,1)S(1)}, bf16[768,384]{1,0:T(8,128)(2,1)S(1)}, u32[]{:S(2)}, u32[]{:S(2)}) collective-permute-start(bf16[768,384]{1,0:T(8,128)(2,1)S(1)} %copy-done.28), channel_id=1, source_target_pairs={{0,8},{1,9},{2,10},{3,11},{4,12},{5,13},{6,14},{7,15},{8,0},{9,1},... | collective-permute-start | bytes 1769480 | tf_op jit(solution)/shard_map/ppermute | solution.py:887
  214.1 9.1 %collective-permute-start.22 = (bf16[384,384]{1,0:T(8,128)(2,1)S(1)}, bf16[384,384]{1,0:T(8,128)(2,1)S(1)}, u32[]{:S(2)}, u32[]{:S(2)}) collective-permute-start(bf16[384,384]{1,0:T(8,128)(2,1)S(1)} %get-tuple-element.217), channel_id=1, source_target_pairs={{0,16},{1,17},{2,18},{3,19},{4,20},{5,21},{6,22},{7,23},{8,24},{9,... | collective-permute-start | bytes 884744 | tf_op jit(solution)/shard_map/ppermute | solution.py:887
  223.3 5.2 %collective-permute-start.23 = (bf16[192,384]{1,0:T(8,128)(2,1)S(1)}, bf16[192,384]{1,0:T(8,128)(2,1)S(1)}, u32[]{:S(2)}, u32[]{:S(2)}) collective-permute-start(bf16[192,384]{1,0:T(8,128)(2,1)S(1)} %get-tuple-element.219), channel_id=1, source_target_pairs={{0,1},{1,0},{2,3},{3,2},{4,5},{5,4},{6,7},{7,6},{8,9},{9,8},{10,11... | collective-permute-start | bytes 442376 | tf_op jit(solution)/shard_map/ppermute | solution.py:887
  228.5 4.8 %collective-permute-start.24 = (bf16[48,384]{1,0:T(8,128)(2,1)S(1)}, bf16[48,384]{1,0:T(8,128)(2,1)S(1)}, u32[]{:S(2)}, u32[]{:S(2)}) collective-permute-start(bf16[48,384]{1,0:T(8,128)(2,1)S(1)} %get-tuple-element.221), channel_id=1, source_target_pairs={{0,2},{1,3},{2,0},{3,1},{4,6},{5,7},{6,4},{7,5},{8,10},{9,11},{10,... | collective-permute-start | bytes 110600 | tf_op jit(solution)/shard_map/ppermute | solution.py:887
  229.4 5.4 %collective-permute-start.25 = (bf16[48,384]{1,0:T(8,128)(2,1)S(1)}, bf16[48,384]{1,0:T(8,128)(2,1)S(1)}, u32[]{:S(2)}, u32[]{:S(2)}) collective-permute-start(bf16[48,384]{1,0:T(8,128)(2,1)S(1)} %get-tuple-element.222), channel_id=1, source_target_pairs={{0,4},{1,5},{2,6},{3,7},{4,0},{5,1},{6,2},{7,3},{8,12},{9,13},{10,... | collective-permute-start | bytes 110600 | tf_op jit(solution)/shard_map/ppermute | solution.py:887
  232.9 5.9 %collective-permute-start.26 = (bf16[48,384]{1,0:T(8,128)(2,1)S(1)}, bf16[48,384]{1,0:T(8,128)(2,1)S(1)}, u32[]{:S(2)}, u32[]{:S(2)}) collective-permute-start(bf16[48,384]{1,0:T(8,128)(2,1)S(1)} %get-tuple-element.223), channel_id=1, source_target_pairs={{0,6},{1,7},{2,4},{3,5},{4,2},{5,3},{6,0},{7,1},{8,14},{9,15},{10,... | collective-permute-start | bytes 110600 | tf_op jit(solution)/shard_map/ppermute | solution.py:887
  238.9 4.7 %collective-permute-start.27 = (bf16[80,384]{1,0:T(8,128)(2,1)S(1)}, bf16[80,384]{1,0:T(8,128)(2,1)S(1)}, u32[]{:S(2)}, u32[]{:S(2)}) collective-permute-start(bf16[80,384]{1,0:T(8,128)(2,1)S(1)} %pad_maximum_fusion.1.refs_0_), channel_id=1, source_target_pairs={{0,2},{1,3},{2,0},{3,1},{4,6},{5,7},{6,4},{7,5},{8,10},{9,11},{10,... | collective-permute-start | bytes 184328 | tf_op jit(solution)/shard_map/ppermute | solution.py:887
  239.0 5.2 %collective-permute-start.28 = (bf16[80,384]{1,0:T(8,128)(2,1)S(1)}, bf16[80,384]{1,0:T(8,128)(2,1)S(1)}, u32[]{:S(2)}, u32[]{:S(2)}) collective-permute-start(bf16[80,384]{1,0:T(8,128)(2,1)S(1)} %pad_maximum_fusion.1.refs_0_), channel_id=1, source_target_pairs={{0,4},{1,5},{2,6},{3,7},{4,0},{5,1},{6,2},{7,3},{8,12},{9,13},{10,... | collective-permute-start | bytes 184328 | tf_op jit(solution)/shard_map/ppermute | solution.py:887
  239.9 6.4 %collective-permute-start.29 = (bf16[80,384]{1,0:T(8,128)(2,1)S(1)}, bf16[80,384]{1,0:T(8,128)(2,1)S(1)}, u32[]{:S(2)}, u32[]{:S(2)}) collective-permute-start(bf16[80,384]{1,0:T(8,128)(2,1)S(1)} %pad_maximum_fusion.1.refs_0_), channel_id=1, source_target_pairs={{0,6},{1,7},{2,4},{3,5},{4,2},{5,3},{6,0},{7,1},{8,14},{9,15},{10,... | collective-permute-start | bytes 184328 | tf_op jit(solution)/shard_map/ppermute | solution.py:887
  246.2 8.0 %collective-permute-start.30 = (bf16[320,384]{1,0:T(8,128)(2,1)S(1)}, bf16[320,384]{1,0:T(8,128)(2,1)S(1)}, u32[]{:S(2)}, u32[]{:S(2)}) collective-permute-start(bf16[320,384]{1,0:T(8,128)(2,1)S(1)} %join.9.refs_0_), channel_id=1, source_target_pairs={{0,1},{1,0},{2,3},{3,2},{4,5},{5,4},{6,7},{7,6},{8,9},{9,8},{10,11... | collective-permute-start | bytes 737288 | tf_op jit(solution)/shard_map/ppermute | solution.py:887
  254.3 9.4 %collective-permute-start.31 = (bf16[640,384]{1,0:T(8,128)(2,1)S(1)}, bf16[640,384]{1,0:T(8,128)(2,1)S(1)}, u32[]{:S(2)}, u32[]{:S(2)}) collective-permute-start(bf16[640,384]{1,0:T(8,128)(2,1)S(1)} %join.10.refs_0_), channel_id=1, source_target_pairs={{0,16},{1,17},{2,18},{3,19},{4,20},{5,21},{6,22},{7,23},{8,24},{9,... | collective-permute-start | bytes 1474568 | tf_op jit(solution)/shard_map/ppermute | solution.py:887
  257.2 11.2 %copy-start.1 = (f32[32,48,384]{2,1,0:T(8,128)S(1)}, f32[32,48,384]{2,1,0:T(8,128)}, u32[]{:S(2)}) copy-start(f32[32,48,384]{2,1,0:T(8,128)} %copy-done) | copy-start | bytes 7077892
  263.8 2.6 collective-permute-start.32
  (17 other events, 45.7 us)

commit v3 on v2

--- a/solution.py
+++ b/solution.py
@@ -424,19 +424,18 @@
                 )
 
 
-def whole_back_kernel(size, begun, last, flag_ref, *refs):
+def whole_back_kernel(size, begun, flag_ref, *refs):
     tile_refs, hint_ref, refs = refs[:7], refs[7], refs[8:]
     if begun:
         tw_ref, tb_ref, refs = refs[0], refs[1], refs[2:]
-    if last:
-        me_ref, mixer_ref, earlier, refs = refs[0], refs[1], refs[2 : 1 + PAIRS], refs[1 + PAIRS :]
-    tq_out, tk_out, tv_out, tb_out, refs = *refs[:4], refs[4:]
+    me_ref, mixer_ref, tq_out, tk_out, tv_out, tb_out, first_out, second_out, rows_scr = refs
+    p = pl.program_id(0)
 
     def tile(qlow, qsize, klow, ksize):
         query_grad, keys_grad, values_grad = back_tile(qlow, qsize, klow, ksize, *tile_refs)
-        tq_out[pl.ds(qlow, qsize), :] = query_grad
-        tk_out[pl.ds(klow, ksize), :] = keys_grad
-        tv_out[pl.ds(klow, ksize), :] = values_grad
+        tq_out[0, pl.ds(qlow, qsize), :] = query_grad
+        tk_out[0, pl.ds(klow, ksize), :] = keys_grad
+        tv_out[0, pl.ds(klow, ksize), :] = values_grad
 
     @pl.when(flag_ref[0] == 1)
     def _():
@@ -447,27 +446,25 @@
         for b in range(HALF):
             tile(b * BLOCK, BLOCK, b * BLOCK, BLOCK)
 
-    grads = jnp.concatenate([tq_out[...], tk_out[...], tv_out[...]], axis=1)
+    grads = jnp.concatenate([tq_out[0], tk_out[0], tv_out[0]], axis=1)
     weight_grad = dot(hint_ref[...], grads)
     sums = column_sum(grads.astype(F32))
     if begun:
         weight_grad, sums = weight_grad + tw_ref[0], sums + tb_ref[0, 0:1]
-    tb_out[...] = jnp.broadcast_to(sums, tb_out.shape)
-    if not last:
-        refs[0][...] = weight_grad
-        return
-    first_out, second_out, rows_scr = refs
+    tb_out[0] = jnp.broadcast_to(sums, tb_out.shape[1:])
     width = weight_grad.shape[0]
+    lanes = pl.ds(pl.multiple_of(p * LANES, LANES), LANES)
     for m in range(3):
-        lanes = slice(m * LANES, (m + 1) * LANES)
-        rows = slice(m * width, (m + 1) * width)
-        for j, ref in enumerate(earlier):
-            rows_scr[rows, j * LANES : (j + 1) * LANES] = ref[:, lanes].astype(BF16)
-        rows_scr[rows, (PAIRS - 1) * LANES :] = weight_grad[:, lanes].astype(BF16)
-    rows_scr[3 * width : 4 * width, :] = mixer_ref[...].astype(BF16)
-    if rows_scr.shape[0] > 4 * width:
-        rows_scr[4 * width :, :] = jnp.zeros((rows_scr.shape[0] - 4 * width, width), BF16)
-    spread_out(me_ref, rows_scr.shape[0] // size, size, rows_scr, (first_out, second_out))
+        rows_scr[m * width : (m + 1) * width, lanes] = weight_grad[
+            :, m * LANES : (m + 1) * LANES
+        ].astype(BF16)
+
+    @pl.when(p == PAIRS - 1)
+    def _():
+        rows_scr[3 * width : 4 * width, :] = mixer_ref[...].astype(BF16)
+        if rows_scr.shape[0] > 4 * width:
+            rows_scr[4 * width :, :] = jnp.zeros((rows_scr.shape[0] - 4 * width, width), BF16)
+        spread_out(me_ref, rows_scr.shape[0] // size, size, rows_scr, (first_out, second_out))
 
 
 def back_inputs(nq, nk, first, flag, kept, grad, low):
@@ -513,32 +510,27 @@
     )(*arrays, weight)
 
 
-def whole_back(size, me, pair, flag, kept, grad, begun, mixer, earlier):
+def whole_back(size, me, flag, kept, grad, begun, mixer):
     width = mixer.shape[0]
     rows = HALF * BLOCK
-    in_specs, arrays = back_inputs(HALF, HALF, pair, flag, kept, grad, 0)
+    in_specs, arrays = back_inputs(HALF, HALF, 0, flag, kept, grad, 0)
     shape = jax.ShapeDtypeStruct
     if begun:
-        in_specs += [pl.BlockSpec((1,) + b.shape[1:], lambda p: (pair, 0, 0)) for b in begun]
+        in_specs += [pl.BlockSpec((1,) + b.shape[1:], lambda p: (p, 0, 0)) for b in begun]
         arrays += begun
-    outs = [shape((rows, LANES), BF16)] * 3 + [shape((8, 3 * LANES), F32)]
-    last = pair == PAIRS - 1
-    scratch = []
-    if last:
-        in_specs += [SMEM] + [full(a.shape) for a in (mixer, *earlier)]
-        arrays += [me, mixer, *earlier]
-        total = padded(4 * width, size)
-        outs += [shape((total // 2, width), BF16)] * 2
-        scratch = [pltpu.VMEM((total, width), BF16)]
-    else:
-        outs += [shape((width, 3 * LANES), F32)]
+    in_specs += [SMEM, full(mixer.shape)]
+    arrays += [me, mixer]
+    total = padded(4 * width, size)
+    pairs = [shape((PAIRS, rows, LANES), BF16)] * 3 + [shape((PAIRS, 8, 3 * LANES), F32)]
+    outs = pairs + [shape((total // 2, width), BF16)] * 2
+    out_specs = [pl.BlockSpec((1,) + o.shape[1:], lambda p: (p, 0, 0)) for o in pairs]
     return pl.pallas_call(
-        partial(whole_back_kernel, size, bool(begun), last),
-        grid=(1,),
+        partial(whole_back_kernel, size, bool(begun)),
+        grid=(PAIRS,),
         in_specs=in_specs,
-        out_specs=[full(o.shape) for o in outs],
+        out_specs=out_specs + [full(o.shape) for o in outs[4:]],
         out_shape=outs,
-        scratch_shapes=scratch,
+        scratch_shapes=[pltpu.VMEM((total, width), BF16)],
         compiler_params=params(),
         cost_estimate=cost(0.1),
         name="whole_back",
@@ -733,7 +725,7 @@
     parts, weight_ref, refs = refs[: 3 * PAIRS], refs[3 * PAIRS], refs[3 * PAIRS + 1 :]
     if u > 1:
         own_ref, others, refs = refs[0], refs[1 : 1 + count], refs[1 + count :]
-    sums, refs = refs[:PAIRS], refs[PAIRS:]
+    sums, refs = refs[0], refs[1:]
     middle_ref, mods_ref, out_ref, small_out, x_scr, g_scr, slots_acc = refs
     i = pl.program_id(0)
 
@@ -744,7 +736,7 @@
     @pl.when(i < HALF)
     def _():
         x_scr[...] = xs[0][...]
-        grads = jnp.concatenate([part[...] for part in parts], axis=1)
+        grads = jnp.concatenate([part[0] for part in parts], axis=1)
         g_scr[...] = dot_nt(grads, weight_ref[...])
 
     if u > 1:
@@ -770,7 +762,9 @@
     @pl.when(i == total - 1)
     def _():
         biases = [
-            jnp.concatenate([ref[0:1, m * LANES : (m + 1) * LANES] for ref in sums], axis=1)
+            jnp.concatenate(
+                [sums[j, 0:1, m * LANES : (m + 1) * LANES] for j in range(PAIRS)], axis=1
+            )
             for m in (0, 2)
         ]
         small = [slots_acc[0], slots_acc[1], *biases, jnp.zeros((14, width), F32)]
@@ -789,14 +783,23 @@
         )
 
     in_specs = [rows_of(j, width) for j in range(len(units))]
-    in_specs += [rows_of(0, LANES)] * (3 * PAIRS) + [full(weight.shape)]
-    arrays = [*xs, *parts, weight]
+    arrays = list(xs)
+    for part in parts:
+        for p in range(PAIRS):
+            in_specs.append(
+                pl.BlockSpec(
+                    (1, BLOCK, LANES), lambda i, p=p: (p, jnp.clip(i, 0, HALF - 1), 0)
+                )
+            )
+            arrays.append(part)
+    in_specs.append(full(weight.shape))
+    arrays.append(weight)
     if len(units) > 1:
         in_specs += [rows_of(1, width)] * (1 + len(others))
         arrays += [own, *others]
-    in_specs += [full(s.shape) for s in sums]
+    in_specs += [full(sums.shape)]
     in_specs += [pl.BlockSpec((BLOCK, width), lambda i: (i, 0)), full(mods.shape)]
-    arrays += [*sums, middle, mods]
+    arrays += [sums, middle, mods]
     return pl.pallas_call(
         partial(finish_kernel, units, n, chunk, width, len(others)),
         grid=(total,),
@@ -857,23 +860,30 @@
     )(me, *pieces)
 
 
-def modulate_kernel(early_ref, late_ref, *refs):
+def modulate_kernel(early_ref, late_ref, weight_out, bias_out, query_out, value_out, *outs):
     size, _, width = early_ref.shape
-    weight_out, bias_out, early_out, late_out = refs
+    mixer_out, hidden_out, output_out = outs
     flat = lambda ref, m: ref[:, 8 * m : 8 * (m + 1), :].reshape(size * 8, width)
     activity = flat(early_ref, 4).astype(BF16).T
     for m in range(6):
         slots = flat(late_ref, m) if m < 2 else flat(early_ref, m - 2)
         lanes = slice(m * width, (m + 1) * width)
         weight_out[:, lanes] = dot(activity, slots.astype(BF16))
-        bias_out[:, lanes] = column_sum(slots)
-    early_out[...] = jnp.sum(early_ref[:, 40:48, :], axis=0)
-    late_out[...] = jnp.sum(late_ref[:, 16:24, :], axis=0)
-
-
-def modulate(early, late):
+        bias_out[lanes] = column_sum(slots).reshape(-1)
+    early = jnp.sum(early_ref[:, 40:48, :], axis=0)
+    late = jnp.sum(late_ref[:, 16:24, :], axis=0)
+    query_out[...] = late[0:1].reshape(-1)
+    value_out[...] = late[1:2].reshape(-1)
+    output_out[...] = early[0:1].reshape(-1)
+    parts = hidden_out.shape[0] // width
+    for j in range(parts):
+        hidden_out[j * width : (j + 1) * width] = early[1 + j : 2 + j].reshape(-1)
+    mixer_out[...] = early[1 + parts : 2 + parts].reshape(-1)
+
+
+def modulate(early, late, ff):
     width = early.shape[2]
-    shapes = [(width, 6 * width), (1, 6 * width), (8, width), (8, width)]
+    shapes = [(width, 6 * width), (6 * width,), (width,), (width,), (width,), (ff,), (width,)]
     return pl.pallas_call(
         modulate_kernel,
         out_shape=[jax.ShapeDtypeStruct(s, F32) for s in shapes],
@@ -1037,7 +1047,8 @@
         modulate_weight,
         modulate_bias,
     )
-    c_pieces = deal(pack(plan, chunk, big, me, image_lengths, after(cotangent, mods, x_pieces[1:TIE]), False))
+    c_packed = pack(plan, chunk, big, me, image_lengths, after(cotangent, packed), False)
+    c_pieces = deal(after(c_packed, mods, x_pieces[1:TIE]))
 
     attended, xs, mixes = [], [], []
     others = [[] for _ in units]
@@ -1105,20 +1116,11 @@
         own, others = found[0], [xor_permute(o, t + 1, size) for t, o in enumerate(found[1:-2])]
         begun = found[-2:]
         token = feed_sum.step(feed_small, done=(own,))
-    grouped, sums, earlier = [], [], []
-    for p in range(PAIRS):
-        grad = after(mixed_grad, *token, *(others if p == 1 else []))
-        found = whole_back(
-            size, relative, p, flags, attended[0], grad, begun, mixer_grad, earlier
-        )
-        grouped.append(found[:3])
-        sums.append(found[3])
-        if p < PAIRS - 1:
-            earlier.append(found[4])
-            token = feed_sum.step(feed_small, done=(found[0],))
-    last_sum = Sum(stages, size, found[4:6])
-    token = feed_sum.step(feed_small, done=(found[3],))
-    parts = [grouped[p][m] for m in range(3) for p in range(PAIRS)]
+    grad = after(mixed_grad, *token)
+    *parts, sums, first, second = whole_back(
+        size, relative, flags, attended[0], grad, begun, mixer_grad
+    )
+    token = feed_sum.step(feed_small, done=(sums,))
     grad_pieces, last_small = finish(
         units,
         n,
@@ -1132,11 +1134,18 @@
         after(middle_grad, out_back, *token),
         mods,
     )
-    grad_back = deal(grad_pieces)
     feed_chunk, last_chunk = (padded(r, size) // size for r in (2 * ff, 4 * width))
-    last_sum.step(last_small, done=(last_small,))
+    last_sum = Sum(stages, size, after([first, second], last_small))
+    spreading = feed_sum.step(feed_small, done=(last_small,))
+    grad_back = deal(after(grad_pieces, spreading))
+    last_sum.step(last_small)
+    last_sum.step(last_small)
+    token = last_sum.step(last_small)
+    feed_sum.step(feed_small, done=token)
+    token = last_sum.step(last_small, done=(grad_back,))
     while feed_sum.left:
-        token = feed_sum.step(feed_small, done=token)
+        feed_sum.step(feed_small, done=token)
+        token = last_sum.step(last_small)
     block_out = unpack(plan, chunk, big, image_lengths, out_back, BF16)
     output_w_grad, hidden_w_grad, early = settle(
         size, feed_chunk, relative, feed_sum.held, [(ff, width), (width, ff)]
@@ -1144,29 +1153,29 @@
     patch_grad = unpack(plan, chunk, big, image_lengths, grad_back, F32)
     while last_sum.left:
         token = ()
-        if last_sum.left == 2:
-            token = (grad_back, block_out, output_w_grad)
         if last_sum.left == 1:
-            token = (patch_grad,)
+            token = (patch_grad, block_out, output_w_grad)
         last_sum.step(last_small, done=token)
     triple_w_grad, mixer_w_grad, late = settle(
         size, last_chunk, relative, last_sum.held, [(width, 3 * width), (width, width)]
     )
-    modulate_w_grad, modulate_b_grad, feed_sums, last_sums = modulate(early, late)
+    modulate_w_grad, modulate_b_grad, query_b, value_b, mixer_b, hidden_b, output_b = modulate(
+        early, late, ff
+    )
     return (
         block_out,
         patch_grad,
         modulate_w_grad,
-        modulate_b_grad.reshape(-1),
+        modulate_b_grad,
         triple_w_grad,
-        last_sums[0],
-        last_sums[1],
+        query_b,
+        value_b,
         mixer_w_grad,
-        feed_sums[1 + ff // width],
+        mixer_b,
         hidden_w_grad,
-        feed_sums[1 : 1 + ff // width].reshape(-1),
+        hidden_b,
         output_w_grad,
-        feed_sums[0],
+        output_b,
     )
 
 

time: 276 us -> 265 us (0.960)
  Pallas kernels: 127 us -> 119 us
  local copies, waits for them, and re-layouts: 13 us -> 7.51 us
  starting transfers between devices: 59.7 us -> 64.6 us
  waiting for transfers between devices: 71.1 us -> 67.8 us
    pallas_call x3 -> x1, Pallas kernels: 28 us -> 20 us  [whole_back(): pl.pallas_call(partial(whole_back_kernel, size, bool(begun)), grid=(PAIRS...]
    ppermute x33, starting transfers between devices: 40.3 us -> 46.1 us  [xor_permute(): lax.ppermute(value, ('rows', 'band'), [(i, i ^ mask) for i in range(size)])]
    unnamed x58 -> x52, local copies, waits for them, and re-layouts: 11.8 us -> 7.51 us
    ppermute x33, waiting for transfers between devices: 71.1 us -> 67.8 us  [xor_permute(): lax.ppermute(value, ('rows', 'band'), [(i, i ^ mask) for i in range(size)])]
  transfers between devices with their start and end apart: 36 -> 36, of which waited for: 17 -> 15; matrix products, arithmetic and copies ran while one was open for 0% -> 0% of each run, Pallas kernels for 34% -> 33%
where the time goes in v3:
time: 265 us; the launch traced here: 260 us
  Pallas kernels  119 us (45%)
  waiting for transfers between devices  67.8 us (26%)
  starting transfers between devices  64.6 us (24%)
  local copies, waits for them, and re-layouts  7.51 us (3%)
    ppermute x33, waiting for transfers between devices, xor_permute(): lax.ppermute(value, ('rows', 'band'), [(i, i ^ mask) for i in range(size)])  67.8 us
    ppermute x33, starting transfers between devices, xor_permute(): lax.ppermute(value, ('rows', 'band'), [(i, i ^ mask) for i in range(size)])  46.1 us
    pallas_call x2, Pallas kernels, attend(): pl.pallas_call(partial(attend_kernel, n, unit, low, nq, nk, chunk, width)...  31.6 us
    pallas_call x1, Pallas kernels, feed(): pl.pallas_call(partial(feed_kernel, units, n, chunk, width, size, valid i...  27.2 us
    pallas_call x1, Pallas kernels, whole_back(): pl.pallas_call(partial(whole_back_kernel, size, bool(begun)), grid=(PAIRS...  20 us
    all_to_all x3, starting transfers between devices, deal(): return lax.all_to_all(pieces, 'band', 0, 0, tiled=True)  18.5 us
    pallas_call x1, Pallas kernels, shared_back(): pl.pallas_call(partial(shared_back_kernel, nq, nk), grid=(PAIRS,), in_spe...  13.6 us
    pallas_call x1, Pallas kernels, finish(): pl.pallas_call(partial(finish_kernel, units, n, chunk, width, len(others)...  8.63 us
  transfers between devices with their start and end apart: 36, of which 15 were waited for; matrix products, arithmetic and copies ran while one was open for 0% of the time, Pallas kernels for 33%

profile of v3, /device:TPU:0, one launch (start us, length us, event | category | flops | bytes accessed | tf_op | source)
XLA Modules:
  0.0 259.8 jit_solution(14774805967151952432)
XLA Ops:
  2.6 1.3 pack.2
  3.9 3.0 %collective-permute-start = (bf16[6,32,384]{2,1,0:T(8,128)(2,1)S(1)}, bf16[6,32,384]{2,1,0:T(8,128)(2,1)S(1)}, u32[]{:S(2)}, u32[]{:S(2)}) collective-permute-start(bf16[6,32,384]{2,1,0:T(8,128)(2,1)S(1)} %get-tuple-element.122), channel_id=1, source_target_pairs={{0,1},{1,0},{2,3},{3,2},{4,5},{5,4},{6,7},{7,6},{8,9},{9,8},{10,11... | collective-permute-start | bytes 442376 | tf_op jit(solution)/shard_map/ppermute | solution.py:897
  6.9 1.6 collective-permute-start.1
  8.5 3.0 %collective-permute-start.3 = (bf16[6,32,384]{2,1,0:T(8,128)(2,1)S(1)}, bf16[6,32,384]{2,1,0:T(8,128)(2,1)S(1)}, u32[]{:S(2)}, u32[]{:S(2)}) collective-permute-start(bf16[6,32,384]{2,1,0:T(8,128)(2,1)S(1)} %get-tuple-element.125), channel_id=1, source_target_pairs={{0,4},{1,5},{2,6},{3,7},{4,0},{5,1},{6,2},{7,3},{8,12},{9,13},{10,... | collective-permute-start | bytes 442376 | tf_op jit(solution)/shard_map/ppermute | solution.py:897
  12.8 3.6 %collective-permute-start.5 = (bf16[6,32,384]{2,1,0:T(8,128)(2,1)S(1)}, bf16[6,32,384]{2,1,0:T(8,128)(2,1)S(1)}, u32[]{:S(2)}, u32[]{:S(2)}) collective-permute-start(bf16[6,32,384]{2,1,0:T(8,128)(2,1)S(1)} %get-tuple-element.127), channel_id=1, source_target_pairs={{0,6},{1,7},{2,4},{3,5},{4,2},{5,3},{6,0},{7,1},{8,14},{9,15},{10,... | collective-permute-start | bytes 442376 | tf_op jit(solution)/shard_map/ppermute | solution.py:897
  16.4 2.5 collective-permute-done.1.refs_2_
  21.1 1.9 pack.3
  23.0 1.4 prepare.1
  26.2 6.8 %collective-permute-done.4.refs_5_ = bf16[6,32,384]{2,1,0:T(8,128)(2,1)S(1)} collective-permute-done((bf16[6,32,384]{2,1,0:T(8,128)(2,1)S(1)}, bf16[6,32,384]{2,1,0:T(8,128)(2,1)S(1)}, u32[]{:S(2)}, u32[]{:S(2)}) %collective-permute-start.4) | collective-permute-done | bytes 147488 | tf_op jit(solution)/shard_map/ppermute | solution.py:897
  33.0 8.9 %all-to-all-start = ((bf16[8,6,32,384]{3,2,1,0:T(8,128)(2,1)}), bf16[8,6,32,384]{3,2,1,0:T(8,128)(2,1)S(1)}, u32[]{:S(2)}, u32[]{:S(2)}) async-start(bf16[8,6,32,384]{3,2,1,0:T(8,128)(2,1)} %pack.3), calls=%async_computation | async-start | bytes 2359296 | tf_op jit(solution)/shard_map/all_to_all | solution.py:1034
  42.1 2.1 collective-permute-start.7
  44.2 18.6 %attend.2 = (bf16[1024,384]{1,0:T(8,128)(2,1)}, bf16[384,1024]{1,0:T(8,128)(2,1)}, bf16[3,1024,128]{2,1,0:T(8,128)(2,1)}, bf16[3,1024,128]{2,1,0:T(8,128)(2,1)},...) custom-call(s32[1]{0:T(128)} %bitcast.1.me_ref, ...), custom_call_target="tpu_custom_call" | custom-call | bytes 300000 | tf_op jit(solution)/shard_map/attend/pallas_call | solution.py:341
  64.4 13.0 %attend.3 = (bf16[1024,384]{1,0:T(8,128)(2,1)}, bf16[384,1024]{1,0:T(8,128)(2,1)}, bf16[3,512,128]{2,1,0:T(8,128)(2,1)}, bf16[3,1024,128]{2,1,0:T(8,128)(2,1)}, ...) custom-call(s32[1]{0:T(128)} %bitcast.1.me_ref, ...), custom_call_target="tpu_custom_call" | custom-call | bytes 300000 | tf_op jit(solution)/shard_map/attend/pallas_call | solution.py:341
  78.4 27.2 %feed.1 = (bf16[8,6,32,384]{3,2,1,0:T(8,128)(2,1)}, f32[1536,384]{1,0:T(8,128)}, bf16[1536,384]{1,0:T(8,128)(2,1)}, bf16[1536,384]{1,0:T(8,128)(2,1)}, bf16[1536...) custom-call(s32[1]{0:T(128)} %bitcast.me_ref.refs_10_, ...), custom_call_target="tpu_custom_call" | custom-call | bytes 300000 | tf_op jit(solution)/shard_map/feed/pallas_call | solution.py:690
  105.6 4.9 %all-to-all-start.1 = ((bf16[8,6,32,384]{3,2,1,0:T(8,128)(2,1)}), bf16[8,6,32,384]{3,2,1,0:T(8,128)(2,1)S(1)}, u32[]{:S(2)}, u32[]{:S(2)}) async-start(bf16[8,6,32,384]{3,2,1,0:T(8,128)(2,1)} %get-tuple-element.137), calls=%async_computation.1 | async-start | bytes 2359296 | tf_op jit(solution)/shard_map/all_to_all | solution.py:1034
  111.5 13.6 %shared_back.1 = (f32[512,384]{1,0:T(8,128)}, bf16[512,384]{1,0:T(8,128)(2,1)}, f32[3,384,384]{2,1,0:T(8,128)}, f32[3,8,384]{2,1,0:T(8,128)}) custom-call(s32[2]{0:T(128)} %copy-done.18, bf16[6,1024,512]{2,1,0:T(8,128)(2,1)} %get-tuple-element.150.refs_0_, bf16[3,512,128]{2,1,0:T(8,128)(2,1)} %get-tuple-element.151.refs_1_, ...), custom_call_target="tpu_custom_call" | custom-call | bytes 300000 | tf_op jit(solution)/shard_map/shared_back/pallas_call | solution.py:500
  125.1 2.1 collective-permute-start.10
  128.1 20.0 %whole_back.1 = (bf16[3,1024,128]{2,1,0:T(8,128)(2,1)}, bf16[3,1024,128]{2,1,0:T(8,128)(2,1)}, bf16[3,1024,128]{2,1,0:T(8,128)(2,1)}, f32[3,8,384]{2,1,0:T(8,128...) custom-call(s32[2]{0:T(128)} %copy-done.18, bf16[6,1024,1024]{2,1,0:T(8,128)(2,1)} %get-tuple-element.138.refs_0_, ...), custom_call_target="tpu_custom_call" | custom-call | bytes 300000 | tf_op jit(solution)/shard_map/whole_back/pallas_call | solution.py:527
  148.3 1.5 collective-permute-start.12
  149.8 2.4 collective-permute-start.13
  153.5 8.6 %finish.1 = (bf16[8,6,32,384]{3,2,1,0:T(8,128)(2,1)}, bf16[32,384]{1,0:T(8,128)(2,1)}) custom-call(bf16[1024,384]{1,0:T(8,128)(2,1)} %get-tuple-element.130.refs_0_, bf16[1024,384]{1,0:T(8,128)(2,1)} %get-tuple-element.131.refs_1_, bf16[3,1024,128]{2,1,0:T(8,128)(2,1)} %get-tuple-element.167.refs_2_.refs_3_.refs_4_, ...), custom_call_target="tpu_custom_call" | custom-call | bytes 300000 | tf_op jit(solution)/shard_map/finish/pallas_call | solution.py:803
  162.3 4.7 %all-to-all-start.2 = ((bf16[8,6,32,384]{3,2,1,0:T(8,128)(2,1)}), bf16[8,6,32,384]{3,2,1,0:T(8,128)(2,1)S(1)}, u32[]{:S(2)}, u32[]{:S(2)}) async-start(bf16[8,6,32,384]{3,2,1,0:T(8,128)(2,1)} %get-tuple-element.187), calls=%async_computation.2 | async-start | bytes 2359296 | tf_op jit(solution)/shard_map/all_to_all | solution.py:1034
  167.0 2.2 collective-permute-done.18.refs_1_
  170.1 8.4 %collective-permute-done.19.refs_1_ = bf16[384,384]{1,0:T(8,128)(2,1)S(1)} collective-permute-done((bf16[384,384]{1,0:T(8,128)(2,1)S(1)}, bf16[384,384]{1,0:T(8,128)(2,1)S(1)}, u32[]{:S(2)}, u32[]{:S(2)}) %collective-permute-start.19) | collective-permute-done | bytes 294944 | tf_op jit(solution)/shard_map/ppermute | solution.py:897
  178.6 2.0 collective-permute-start.20
  180.6 1.5 collective-permute-start.15
  182.1 2.4 collective-permute-start.16
  185.0 4.2 %collective-permute-done.15.refs_1_ = bf16[144,384]{1,0:T(8,128)(2,1)S(1)} collective-permute-done((bf16[144,384]{1,0:T(8,128)(2,1)S(1)}, bf16[144,384]{1,0:T(8,128)(2,1)S(1)}, u32[]{:S(2)}, u32[]{:S(2)}) %collective-permute-start.15) | collective-permute-done | bytes 110624 | tf_op jit(solution)/shard_map/ppermute | solution.py:897
  189.2 12.7 %collective-permute-done.16.refs_2_ = bf16[144,384]{1,0:T(8,128)(2,1)S(1)} collective-permute-done((bf16[144,384]{1,0:T(8,128)(2,1)S(1)}, bf16[144,384]{1,0:T(8,128)(2,1)S(1)}, u32[]{:S(2)}, u32[]{:S(2)}) %collective-permute-start.16) | collective-permute-done | bytes 110624 | tf_op jit(solution)/shard_map/ppermute | solution.py:897
  203.3 1.7 collective-permute-start.22
  205.1 2.6 collective-permute-start.24
  207.7 2.3 collective-permute-done.23.refs_2_
  211.1 1.6 collective-permute-start.25
  212.7 2.6 %collective-permute-start.26 = (bf16[80,384]{1,0:T(8,128)(2,1)S(1)}, bf16[80,384]{1,0:T(8,128)(2,1)S(1)}, u32[]{:S(2)}, u32[]{:S(2)}) collective-permute-start(bf16[80,384]{1,0:T(8,128)(2,1)S(1)} %pad_maximum_fusion.1.refs_0_), channel_id=1, source_target_pairs={{0,2},{1,3},{2,0},{3,1},{4,6},{5,7},{6,4},{7,5},{8,10},{9,11},{10,... | collective-permute-start | bytes 184328 | tf_op jit(solution)/shard_map/ppermute | solution.py:897
  215.3 1.6 collective-permute-start.27
  216.9 1.5 collective-permute-start.28
  218.4 2.9 %collective-permute-done.27.refs_2_ = bf16[80,384]{1,0:T(8,128)(2,1)S(1)} collective-permute-done((bf16[80,384]{1,0:T(8,128)(2,1)S(1)}, bf16[80,384]{1,0:T(8,128)(2,1)S(1)}, u32[]{:S(2)}, u32[]{:S(2)}) %collective-permute-start.27) | collective-permute-done | bytes 61472 | tf_op jit(solution)/shard_map/ppermute | solution.py:897
  221.3 1.7 collective-permute-done.28.refs_3_
  223.0 7.7 %collective-permute-done.25.refs_1_ = bf16[1152,384]{1,0:T(8,128)(2,1)S(1)} collective-permute-done((bf16[1152,384]{1,0:T(8,128)(2,1)S(1)}, bf16[1152,384]{1,0:T(8,128)(2,1)S(1)}, u32[]{:S(2)}, u32[]{:S(2)}) %collective-permute-start.25) | collective-permute-done | bytes 884768 | tf_op jit(solution)/shard_map/ppermute | solution.py:897
  231.5 7.9 %collective-permute-done.30.refs_1_ = bf16[320,384]{1,0:T(8,128)(2,1)S(1)} collective-permute-done((bf16[320,384]{1,0:T(8,128)(2,1)S(1)}, bf16[320,384]{1,0:T(8,128)(2,1)S(1)}, u32[]{:S(2)}, u32[]{:S(2)}) %collective-permute-start.30) | collective-permute-done | bytes 245792 | tf_op jit(solution)/shard_map/ppermute | solution.py:897
  239.4 1.7 collective-permute-start.31
  241.1 1.9 unpack.2
  243.0 2.2 unpack.3
  245.2 3.0 %settle.2 = (f32[1536,384]{1,0:T(8,128)}, f32[384,1536]{1,0:T(8,128)}, f32[32,48,384]{2,1,0:T(8,128)S(1)}) custom-call(s32[1]{0:T(128)} %bitcast.me_ref.refs_10_, bf16[2304,384]{1,0:T(8,128)(2,1)S(1)} %join.9.refs_0_, bf16[2304,384]{1,0:T(8,128)(2,1)S(1)} %collective-permute-done.29.refs_1_), custom_call_target="tpu_custom_call" | custom-call | bytes 300000 | tf_op jit(solution)/shard_map/settle/pallas_call | solution.py:850
  248.3 4.0 %collective-permute-done.31.refs_1_ = bf16[640,384]{1,0:T(8,128)(2,1)S(1)} collective-permute-done((bf16[640,384]{1,0:T(8,128)(2,1)S(1)}, bf16[640,384]{1,0:T(8,128)(2,1)S(1)}, u32[]{:S(2)}, u32[]{:S(2)}) %collective-permute-start.31) | collective-permute-done | bytes 491552 | tf_op jit(solution)/shard_map/ppermute | solution.py:897
  252.5 2.6 collective-permute-done.32.refs_1_
  255.0 2.0 settle.3
  257.0 2.6 %modulate.1 = (f32[384,2304]{1,0:T(8,128)}, f32[2304]{0:T(1024)}, f32[384]{0:T(512)}, f32[384]{0:T(512)}, f32[384]{0:T(512)}, /*index=5*/f32[1536]{0:T(1024)}, f32[384]{0:T(512)}) custom-call(f32[32,48,384]{2,1,0:T(8,128)S(1)} %get-tuple-element.212.early_ref, f32[32,32,384]{2,1,0:T(8,128)S(1)} %get-tuple-element.216.late_ref), custom_call_target="tpu_custom_call" | custom-call | bytes 300000 | tf_op jit(solution)/shard_map/modulate/pallas_call | solution.py:887
  (107 shorter events, 18.3 us)
Async XLA Ops:
  0.6 22.4 %copy-start.19 = (bf16[2304]{0:T(1024)(128)(2,1)S(1)}, bf16[2304]{0:T(1024)(128)(2,1)}, u32[]{:S(2)}) copy-start(bf16[2304]{0:T(1024)(128)(2,1)} %bias_ref.1) | copy-start | bytes 13828
  2.6 20.4 %copy-start = (bf16[384,2304]{1,0:T(8,128)(2,1)S(1)}, bf16[384,2304]{1,0:T(8,128)(2,1)}, u32[]{:S(2)}) copy-start(bf16[384,2304]{1,0:T(8,128)(2,1)} %weight_ref.1) | copy-start | bytes 5308420
  3.9 38.0 %copy-start.1 = (bf16[6,32,384]{2,1,0:T(8,128)(2,1)}, bf16[6,32,384]{2,1,0:T(8,128)(2,1)S(1)}, u32[]{:S(2)}) copy-start(bf16[6,32,384]{2,1,0:T(8,128)(2,1)S(1)} %get-tuple-element.121.refs_0_) | copy-start | bytes 442372
  3.9 8.9 %collective-permute-start = (bf16[6,32,384]{2,1,0:T(8,128)(2,1)S(1)}, bf16[6,32,384]{2,1,0:T(8,128)(2,1)S(1)}, u32[]{:S(2)}, u32[]{:S(2)}) collective-permute-start(bf16[6,32,384]{2,1,0:T(8,128)(2,1)S(1)} %get-tuple-element.122), channel_id=1, source_target_pairs={{0,1},{1,0},{2,3},{3,2},{4,5},{5,4},{6,7},{7,6},{8,9},{9,8},{10,11... | collective-permute-start | bytes 442376 | tf_op jit(solution)/shard_map/ppermute | solution.py:897
  6.9 12.0 %collective-permute-start.1 = (bf16[6,32,384]{2,1,0:T(8,128)(2,1)S(1)}, bf16[6,32,384]{2,1,0:T(8,128)(2,1)S(1)}, u32[]{:S(2)}, u32[]{:S(2)}) collective-permute-start(bf16[6,32,384]{2,1,0:T(8,128)(2,1)S(1)} %get-tuple-element.123), channel_id=1, source_target_pairs={{0,2},{1,3},{2,0},{3,1},{4,6},{5,7},{6,4},{7,5},{8,10},{9,11},{10,... | collective-permute-start | bytes 442376 | tf_op jit(solution)/shard_map/ppermute | solution.py:897
  8.5 17.6 %collective-permute-start.2 = (bf16[6,32,384]{2,1,0:T(8,128)(2,1)S(1)}, bf16[6,32,384]{2,1,0:T(8,128)(2,1)S(1)}, u32[]{:S(2)}, u32[]{:S(2)}) collective-permute-start(bf16[6,32,384]{2,1,0:T(8,128)(2,1)S(1)} %get-tuple-element.124), channel_id=1, source_target_pairs={{0,3},{1,2},{2,1},{3,0},{4,7},{5,6},{6,5},{7,4},{8,11},{9,10},{10,... | collective-permute-start | bytes 442376 | tf_op jit(solution)/shard_map/ppermute | solution.py:897
  8.5 17.6 %collective-permute-start.3 = (bf16[6,32,384]{2,1,0:T(8,128)(2,1)S(1)}, bf16[6,32,384]{2,1,0:T(8,128)(2,1)S(1)}, u32[]{:S(2)}, u32[]{:S(2)}) collective-permute-start(bf16[6,32,384]{2,1,0:T(8,128)(2,1)S(1)} %get-tuple-element.125), channel_id=1, source_target_pairs={{0,4},{1,5},{2,6},{3,7},{4,0},{5,1},{6,2},{7,3},{8,12},{9,13},{10,... | collective-permute-start | bytes 442376 | tf_op jit(solution)/shard_map/ppermute | solution.py:897
  11.5 21.5 %collective-permute-start.4 = (bf16[6,32,384]{2,1,0:T(8,128)(2,1)S(1)}, bf16[6,32,384]{2,1,0:T(8,128)(2,1)S(1)}, u32[]{:S(2)}, u32[]{:S(2)}) collective-permute-start(bf16[6,32,384]{2,1,0:T(8,128)(2,1)S(1)} %get-tuple-element.126), channel_id=1, source_target_pairs={{0,5},{1,4},{2,7},{3,6},{4,1},{5,0},{6,3},{7,2},{8,13},{9,12},{10,... | collective-permute-start | bytes 442376 | tf_op jit(solution)/shard_map/ppermute | solution.py:897
  12.8 29.2 %copy-start.2 = (bf16[6,32,384]{2,1,0:T(8,128)(2,1)}, bf16[6,32,384]{2,1,0:T(8,128)(2,1)S(1)}, u32[]{:S(2)}) copy-start(bf16[6,32,384]{2,1,0:T(8,128)(2,1)S(1)} %collective-permute-done.refs_1_) | copy-start | bytes 442372
  12.8 20.2 %collective-permute-start.5 = (bf16[6,32,384]{2,1,0:T(8,128)(2,1)S(1)}, bf16[6,32,384]{2,1,0:T(8,128)(2,1)S(1)}, u32[]{:S(2)}, u32[]{:S(2)}) collective-permute-start(bf16[6,32,384]{2,1,0:T(8,128)(2,1)S(1)} %get-tuple-element.127), channel_id=1, source_target_pairs={{0,6},{1,7},{2,4},{3,5},{4,2},{5,3},{6,0},{7,1},{8,14},{9,15},{10,... | collective-permute-start | bytes 442376 | tf_op jit(solution)/shard_map/ppermute | solution.py:897
  18.9 23.1 %copy-start.3 = (bf16[6,32,384]{2,1,0:T(8,128)(2,1)}, bf16[6,32,384]{2,1,0:T(8,128)(2,1)S(1)}, u32[]{:S(2)}) copy-start(bf16[6,32,384]{2,1,0:T(8,128)(2,1)S(1)} %collective-permute-done.1.refs_2_) | copy-start | bytes 442372
  18.9 14.1 %collective-permute-start.6 = (bf16[6,32,384]{2,1,0:T(8,128)(2,1)S(1)}, bf16[6,32,384]{2,1,0:T(8,128)(2,1)S(1)}, u32[]{:S(2)}, u32[]{:S(2)}) collective-permute-start(bf16[6,32,384]{2,1,0:T(8,128)(2,1)S(1)} %get-tuple-element.128), channel_id=1, source_target_pairs={{0,7},{1,6},{2,5},{3,4},{4,3},{5,2},{6,1},{7,0},{8,15},{9,14},{10,... | collective-permute-start | bytes 442376 | tf_op jit(solution)/shard_map/ppermute | solution.py:897
  26.2 15.9 %copy-start.4 = (bf16[6,32,384]{2,1,0:T(8,128)(2,1)}, bf16[6,32,384]{2,1,0:T(8,128)(2,1)S(1)}, u32[]{:S(2)}) copy-start(bf16[6,32,384]{2,1,0:T(8,128)(2,1)S(1)} %collective-permute-done.2.refs_3_) | copy-start | bytes 442372
  26.2 15.9 %copy-start.5 = (bf16[6,32,384]{2,1,0:T(8,128)(2,1)}, bf16[6,32,384]{2,1,0:T(8,128)(2,1)S(1)}, u32[]{:S(2)}) copy-start(bf16[6,32,384]{2,1,0:T(8,128)(2,1)S(1)} %collective-permute-done.3.refs_4_) | copy-start | bytes 442372
  33.0 9.1 %copy-start.6 = (bf16[6,32,384]{2,1,0:T(8,128)(2,1)}, bf16[6,32,384]{2,1,0:T(8,128)(2,1)S(1)}, u32[]{:S(2)}) copy-start(bf16[6,32,384]{2,1,0:T(8,128)(2,1)S(1)} %collective-permute-done.4.refs_5_) | copy-start | bytes 442372
  33.0 9.1 %copy-start.7 = (bf16[6,32,384]{2,1,0:T(8,128)(2,1)}, bf16[6,32,384]{2,1,0:T(8,128)(2,1)S(1)}, u32[]{:S(2)}) copy-start(bf16[6,32,384]{2,1,0:T(8,128)(2,1)S(1)} %collective-permute-done.5.refs_6_) | copy-start | bytes 442372
  33.0 9.1 %copy-start.8 = (bf16[6,32,384]{2,1,0:T(8,128)(2,1)}, bf16[6,32,384]{2,1,0:T(8,128)(2,1)S(1)}, u32[]{:S(2)}) copy-start(bf16[6,32,384]{2,1,0:T(8,128)(2,1)S(1)} %collective-permute-done.6.refs_7_) | copy-start | bytes 442372
  33.0 44.4 %all-to-all-start = ((bf16[8,6,32,384]{3,2,1,0:T(8,128)(2,1)}), bf16[8,6,32,384]{3,2,1,0:T(8,128)(2,1)S(1)}, u32[]{:S(2)}, u32[]{:S(2)}) async-start(bf16[8,6,32,384]{3,2,1,0:T(8,128)(2,1)} %pack.3), calls=%async_computation | async-start | bytes 2359296 | tf_op jit(solution)/shard_map/all_to_all | solution.py:1034
  42.1 21.5 %collective-permute-start.7 = (bf16[512,384]{1,0:T(8,128)(2,1)S(1)}, bf16[512,384]{1,0:T(8,128)(2,1)S(1)}, u32[]{:S(2)}, u32[]{:S(2)}) collective-permute-start(bf16[512,384]{1,0:T(8,128)(2,1)S(1)} %collect.1), channel_id=1, source_target_pairs={{0,1},{1,0},{2,3},{3,2},{4,5},{5,4},{6,7},{7,6},{8,9},{9,8},{10,11... | collective-permute-start | bytes 1179656 | tf_op jit(solution)/shard_map/ppermute | solution.py:897
  105.6 4.9 %collective-permute-start.8 = (bf16[1536,384]{1,0:T(8,128)(2,1)}, bf16[1536,384]{1,0:T(8,128)(2,1)S(1)}, u32[]{:S(2)}, u32[]{:S(2)}) collective-permute-start(bf16[1536,384]{1,0:T(8,128)(2,1)} %get-tuple-element.146), channel_id=1, source_target_pairs={{0,8},{1,9},{2,10},{3,11},{4,12},{5,13},{6,14},{7,15},{8,0},{9,1},... | collective-permute-start | bytes 3538952 | tf_op jit(solution)/shard_map/ppermute | solution.py:897
  105.6 47.1 %all-to-all-start.1 = ((bf16[8,6,32,384]{3,2,1,0:T(8,128)(2,1)}), bf16[8,6,32,384]{3,2,1,0:T(8,128)(2,1)S(1)}, u32[]{:S(2)}, u32[]{:S(2)}) async-start(bf16[8,6,32,384]{3,2,1,0:T(8,128)(2,1)} %get-tuple-element.137), calls=%async_computation.1 | async-start | bytes 2359296 | tf_op jit(solution)/shard_map/all_to_all | solution.py:1034
  110.8 16.4 %collective-permute-start.9 = (bf16[768,384]{1,0:T(8,128)(2,1)S(1)}, bf16[768,384]{1,0:T(8,128)(2,1)S(1)}, u32[]{:S(2)}, u32[]{:S(2)}) collective-permute-start(bf16[768,384]{1,0:T(8,128)(2,1)S(1)} %get-tuple-element.148), channel_id=1, source_target_pairs={{0,16},{1,17},{2,18},{3,19},{4,20},{5,21},{6,22},{7,23},{8,24},{9,... | collective-permute-start | bytes 1769480 | tf_op jit(solution)/shard_map/ppermute | solution.py:897
  125.1 27.6 %collective-permute-start.10 = (bf16[512,384]{1,0:T(8,128)(2,1)}, bf16[512,384]{1,0:T(8,128)(2,1)S(1)}, u32[]{:S(2)}, u32[]{:S(2)}) collective-permute-start(bf16[512,384]{1,0:T(8,128)(2,1)} %get-tuple-element.170), channel_id=1, source_target_pairs={{0,1},{1,0},{2,3},{3,2},{4,5},{5,4},{6,7},{7,6},{8,9},{9,8},{10,11... | collective-permute-start | bytes 1179656 | tf_op jit(solution)/shard_map/ppermute | solution.py:897
  127.3 20.9 %collective-permute-start.11 = (bf16[384,384]{1,0:T(8,128)(2,1)S(1)}, bf16[384,384]{1,0:T(8,128)(2,1)S(1)}, u32[]{:S(2)}, u32[]{:S(2)}) collective-permute-start(bf16[384,384]{1,0:T(8,128)(2,1)S(1)} %get-tuple-element.161), channel_id=1, source_target_pairs={{0,1},{1,0},{2,3},{3,2},{4,5},{5,4},{6,7},{7,6},{8,9},{9,8},{10,11... | collective-permute-start | bytes 884744 | tf_op jit(solution)/shard_map/ppermute | solution.py:897
  148.3 13.9 %collective-permute-start.12 = (bf16[96,384]{1,0:T(8,128)(2,1)S(1)}, bf16[96,384]{1,0:T(8,128)(2,1)S(1)}, u32[]{:S(2)}, u32[]{:S(2)}) collective-permute-start(bf16[96,384]{1,0:T(8,128)(2,1)S(1)} %get-tuple-element.176), channel_id=1, source_target_pairs={{0,2},{1,3},{2,0},{3,1},{4,6},{5,7},{6,4},{7,5},{8,10},{9,11},{10,... | collective-permute-start | bytes 221192 | tf_op jit(solution)/shard_map/ppermute | solution.py:897
  149.8 12.3 %collective-permute-start.13 = (bf16[96,384]{1,0:T(8,128)(2,1)S(1)}, bf16[96,384]{1,0:T(8,128)(2,1)S(1)}, u32[]{:S(2)}, u32[]{:S(2)}) collective-permute-start(bf16[96,384]{1,0:T(8,128)(2,1)S(1)} %get-tuple-element.177), channel_id=1, source_target_pairs={{0,4},{1,5},{2,6},{3,7},{4,0},{5,1},{6,2},{7,3},{8,12},{9,13},{10,... | collective-permute-start | bytes 221192 | tf_op jit(solution)/shard_map/ppermute | solution.py:897
  152.2 10.0 %collective-permute-start.14 = (bf16[96,384]{1,0:T(8,128)(2,1)S(1)}, bf16[96,384]{1,0:T(8,128)(2,1)S(1)}, u32[]{:S(2)}, u32[]{:S(2)}) collective-permute-start(bf16[96,384]{1,0:T(8,128)(2,1)S(1)} %get-tuple-element.178), channel_id=1, source_target_pairs={{0,6},{1,7},{2,4},{3,5},{4,2},{5,3},{6,0},{7,1},{8,14},{9,15},{10,... | collective-permute-start | bytes 221192 | tf_op jit(solution)/shard_map/ppermute | solution.py:897
  162.3 48.7 %all-to-all-start.2 = ((bf16[8,6,32,384]{3,2,1,0:T(8,128)(2,1)}), bf16[8,6,32,384]{3,2,1,0:T(8,128)(2,1)S(1)}, u32[]{:S(2)}, u32[]{:S(2)}) async-start(bf16[8,6,32,384]{3,2,1,0:T(8,128)(2,1)} %get-tuple-element.187), calls=%async_computation.2 | async-start | bytes 2359296 | tf_op jit(solution)/shard_map/all_to_all | solution.py:1034
  166.9 44.0 %copy-start.25 = (bf16[32,384]{1,0:T(8,128)(2,1)S(1)}, bf16[32,384]{1,0:T(8,128)(2,1)}, u32[]{:S(2)}) copy-start(bf16[32,384]{1,0:T(8,128)(2,1)} %get-tuple-element.181) | copy-start | bytes 73732
  166.9 2.3 collective-permute-start.18
  169.4 9.1 %collective-permute-start.19 = (bf16[384,384]{1,0:T(8,128)(2,1)S(1)}, bf16[384,384]{1,0:T(8,128)(2,1)S(1)}, u32[]{:S(2)}, u32[]{:S(2)}) collective-permute-start(bf16[384,384]{1,0:T(8,128)(2,1)S(1)} %get-tuple-element.193), channel_id=1, source_target_pairs={{0,16},{1,17},{2,18},{3,19},{4,20},{5,21},{6,22},{7,23},{8,24},{9,... | collective-permute-start | bytes 884744 | tf_op jit(solution)/shard_map/ppermute | solution.py:897
  178.6 6.4 %collective-permute-start.20 = (bf16[192,384]{1,0:T(8,128)(2,1)S(1)}, bf16[192,384]{1,0:T(8,128)(2,1)S(1)}, u32[]{:S(2)}, u32[]{:S(2)}) collective-permute-start(bf16[192,384]{1,0:T(8,128)(2,1)S(1)} %get-tuple-element.195), channel_id=1, source_target_pairs={{0,1},{1,0},{2,3},{3,2},{4,5},{5,4},{6,7},{7,6},{8,9},{9,8},{10,11... | collective-permute-start | bytes 442376 | tf_op jit(solution)/shard_map/ppermute | solution.py:897
  180.6 8.7 %collective-permute-start.15 = (bf16[144,384]{1,0:T(8,128)(2,1)S(1)}, bf16[144,384]{1,0:T(8,128)(2,1)S(1)}, u32[]{:S(2)}, u32[]{:S(2)}) collective-permute-start(bf16[144,384]{1,0:T(8,128)(2,1)S(1)} %pad_maximum_fusion.refs_0_), channel_id=1, source_target_pairs={{0,2},{1,3},{2,0},{3,1},{4,6},{5,7},{6,4},{7,5},{8,10},{9,11},{10,... | collective-permute-start | bytes 331784 | tf_op jit(solution)/shard_map/ppermute | solution.py:897
  182.1 19.9 %collective-permute-start.16 = (bf16[144,384]{1,0:T(8,128)(2,1)S(1)}, bf16[144,384]{1,0:T(8,128)(2,1)S(1)}, u32[]{:S(2)}, u32[]{:S(2)}) collective-permute-start(bf16[144,384]{1,0:T(8,128)(2,1)S(1)} %pad_maximum_fusion.refs_0_), channel_id=1, source_target_pairs={{0,4},{1,5},{2,6},{3,7},{4,0},{5,1},{6,2},{7,3},{8,12},{9,13},{10,... | collective-permute-start | bytes 331784 | tf_op jit(solution)/shard_map/ppermute | solution.py:897
  184.4 17.6 %collective-permute-start.17 = (bf16[144,384]{1,0:T(8,128)(2,1)S(1)}, bf16[144,384]{1,0:T(8,128)(2,1)S(1)}, u32[]{:S(2)}, u32[]{:S(2)}) collective-permute-start(bf16[144,384]{1,0:T(8,128)(2,1)S(1)} %pad_maximum_fusion.refs_0_), channel_id=1, source_target_pairs={{0,6},{1,7},{2,4},{3,5},{4,2},{5,3},{6,0},{7,1},{8,14},{9,15},{10,... | collective-permute-start | bytes 331784 | tf_op jit(solution)/shard_map/ppermute | solution.py:897
  202.0 8.9 %collective-permute-start.21 = (bf16[576,384]{1,0:T(8,128)(2,1)S(1)}, bf16[576,384]{1,0:T(8,128)(2,1)S(1)}, u32[]{:S(2)}, u32[]{:S(2)}) collective-permute-start(bf16[576,384]{1,0:T(8,128)(2,1)S(1)} %join.6.refs_0_), channel_id=1, source_target_pairs={{0,1},{1,0},{2,3},{3,2},{4,5},{5,4},{6,7},{7,6},{8,9},{9,8},{10,11... | collective-permute-start | bytes 1327112 | tf_op jit(solution)/shard_map/ppermute | solution.py:897
  203.3 4.4 %collective-permute-start.22 = (bf16[48,384]{1,0:T(8,128)(2,1)S(1)}, bf16[48,384]{1,0:T(8,128)(2,1)S(1)}, u32[]{:S(2)}, u32[]{:S(2)}) collective-permute-start(bf16[48,384]{1,0:T(8,128)(2,1)S(1)} %get-tuple-element.197), channel_id=1, source_target_pairs={{0,2},{1,3},{2,0},{3,1},{4,6},{5,7},{6,4},{7,5},{8,10},{9,11},{10,... | collective-permute-start | bytes 110600 | tf_op jit(solution)/shard_map/ppermute | solution.py:897
  205.0 5.0 %collective-permute-start.23 = (bf16[48,384]{1,0:T(8,128)(2,1)S(1)}, bf16[48,384]{1,0:T(8,128)(2,1)S(1)}, u32[]{:S(2)}, u32[]{:S(2)}) collective-permute-start(bf16[48,384]{1,0:T(8,128)(2,1)S(1)} %get-tuple-element.198), channel_id=1, source_target_pairs={{0,4},{1,5},{2,6},{3,7},{4,0},{5,1},{6,2},{7,3},{8,12},{9,13},{10,... | collective-permute-start | bytes 110600 | tf_op jit(solution)/shard_map/ppermute | solution.py:897
  205.1 5.8 %collective-permute-start.24 = (bf16[48,384]{1,0:T(8,128)(2,1)S(1)}, bf16[48,384]{1,0:T(8,128)(2,1)S(1)}, u32[]{:S(2)}, u32[]{:S(2)}) collective-permute-start(bf16[48,384]{1,0:T(8,128)(2,1)S(1)} %get-tuple-element.199), channel_id=1, source_target_pairs={{0,6},{1,7},{2,4},{3,5},{4,2},{5,3},{6,0},{7,1},{8,14},{9,15},{10,... | collective-permute-start | bytes 110600 | tf_op jit(solution)/shard_map/ppermute | solution.py:897
  211.1 19.7 %collective-permute-start.25 = (bf16[1152,384]{1,0:T(8,128)(2,1)S(1)}, bf16[1152,384]{1,0:T(8,128)(2,1)S(1)}, u32[]{:S(2)}, u32[]{:S(2)}) collective-permute-start(bf16[1152,384]{1,0:T(8,128)(2,1)S(1)} %join.7.refs_0_), channel_id=1, source_target_pairs={{0,16},{1,17},{2,18},{3,19},{4,20},{5,21},{6,22},{7,23},{8,24},{9,... | collective-permute-start | bytes 2654216 | tf_op jit(solution)/shard_map/ppermute | solution.py:897
  212.7 5.7 %collective-permute-start.26 = (bf16[80,384]{1,0:T(8,128)(2,1)S(1)}, bf16[80,384]{1,0:T(8,128)(2,1)S(1)}, u32[]{:S(2)}, u32[]{:S(2)}) collective-permute-start(bf16[80,384]{1,0:T(8,128)(2,1)S(1)} %pad_maximum_fusion.1.refs_0_), channel_id=1, source_target_pairs={{0,2},{1,3},{2,0},{3,1},{4,6},{5,7},{6,4},{7,5},{8,10},{9,11},{10,... | collective-permute-start | bytes 184328 | tf_op jit(solution)/shard_map/ppermute | solution.py:897
  215.3 6.0 %collective-permute-start.27 = (bf16[80,384]{1,0:T(8,128)(2,1)S(1)}, bf16[80,384]{1,0:T(8,128)(2,1)S(1)}, u32[]{:S(2)}, u32[]{:S(2)}) collective-permute-start(bf16[80,384]{1,0:T(8,128)(2,1)S(1)} %pad_maximum_fusion.1.refs_0_), channel_id=1, source_target_pairs={{0,4},{1,5},{2,6},{3,7},{4,0},{5,1},{6,2},{7,3},{8,12},{9,13},{10,... | collective-permute-start | bytes 184328 | tf_op jit(solution)/shard_map/ppermute | solution.py:897
  216.9 6.1 %collective-permute-start.28 = (bf16[80,384]{1,0:T(8,128)(2,1)S(1)}, bf16[80,384]{1,0:T(8,128)(2,1)S(1)}, u32[]{:S(2)}, u32[]{:S(2)}) collective-permute-start(bf16[80,384]{1,0:T(8,128)(2,1)S(1)} %pad_maximum_fusion.1.refs_0_), channel_id=1, source_target_pairs={{0,6},{1,7},{2,4},{3,5},{4,2},{5,3},{6,0},{7,1},{8,14},{9,15},{10,... | collective-permute-start | bytes 184328 | tf_op jit(solution)/shard_map/ppermute | solution.py:897
  223.0 18.1 %copy-start.15 = (s32[6,8]{1,0:T(8,128)S(1)}, s32[6,8]{1,0:T(8,128)}, u32[]{:S(2)}) copy-start(s32[6,8]{1,0:T(8,128)} %lens_ref.9) | copy-start | bytes 580
  230.9 14.3 %collective-permute-start.29 = (bf16[2304,384]{1,0:T(8,128)(2,1)S(1)}, bf16[2304,384]{1,0:T(8,128)(2,1)S(1)}, u32[]{:S(2)}, u32[]{:S(2)}) collective-permute-start(bf16[2304,384]{1,0:T(8,128)(2,1)S(1)} %join.9.refs_0_), channel_id=1, source_target_pairs={{0,8},{1,9},{2,10},{3,11},{4,12},{5,13},{6,14},{7,15},{8,0},{9,1},... | collective-permute-start | bytes 5308424 | tf_op jit(solution)/shard_map/ppermute | solution.py:897
  231.0 8.4 %collective-permute-start.30 = (bf16[320,384]{1,0:T(8,128)(2,1)S(1)}, bf16[320,384]{1,0:T(8,128)(2,1)S(1)}, u32[]{:S(2)}, u32[]{:S(2)}) collective-permute-start(bf16[320,384]{1,0:T(8,128)(2,1)S(1)} %join.8.refs_0_), channel_id=1, source_target_pairs={{0,1},{1,0},{2,3},{3,2},{4,5},{5,4},{6,7},{7,6},{8,9},{9,8},{10,11... | collective-permute-start | bytes 737288 | tf_op jit(solution)/shard_map/ppermute | solution.py:897
  239.4 12.9 %collective-permute-start.31 = (bf16[640,384]{1,0:T(8,128)(2,1)S(1)}, bf16[640,384]{1,0:T(8,128)(2,1)S(1)}, u32[]{:S(2)}, u32[]{:S(2)}) collective-permute-start(bf16[640,384]{1,0:T(8,128)(2,1)S(1)} %join.10.refs_0_), channel_id=1, source_target_pairs={{0,16},{1,17},{2,18},{3,19},{4,20},{5,21},{6,22},{7,23},{8,24},{9,... | collective-permute-start | bytes 1474568 | tf_op jit(solution)/shard_map/ppermute | solution.py:897
  252.4 2.6 %collective-permute-start.32 = (bf16[1280,384]{1,0:T(8,128)(2,1)S(1)}, bf16[1280,384]{1,0:T(8,128)(2,1)S(1)}, u32[]{:S(2)}, u32[]{:S(2)}) collective-permute-start(bf16[1280,384]{1,0:T(8,128)(2,1)S(1)} %join.11.refs_0_), channel_id=1, source_target_pairs={{0,8},{1,9},{2,10},{3,11},{4,12},{5,13},{6,14},{7,15},{8,0},{9,1},... | collective-permute-start | bytes 2949128 | tf_op jit(solution)/shard_map/ppermute | solution.py:897
  (14 other events, 32.1 us)

commit v4 on v3

--- a/solution.py
+++ b/solution.py
@@ -1138,14 +1138,13 @@
     last_sum = Sum(stages, size, after([first, second], last_small))
     spreading = feed_sum.step(feed_small, done=(last_small,))
     grad_back = deal(after(grad_pieces, spreading))
-    last_sum.step(last_small)
-    last_sum.step(last_small)
-    token = last_sum.step(last_small)
-    feed_sum.step(feed_small, done=token)
+    for _ in range(3):
+        last_sum.step(last_small)
     token = last_sum.step(last_small, done=(grad_back,))
     while feed_sum.left:
         feed_sum.step(feed_small, done=token)
-        token = last_sum.step(last_small)
+        if last_sum.left > 1:
+            token = last_sum.step(last_small)
     block_out = unpack(plan, chunk, big, image_lengths, out_back, BF16)
     output_w_grad, hidden_w_grad, early = settle(
         size, feed_chunk, relative, feed_sum.held, [(ff, width), (width, ff)]
@@ -1154,7 +1153,7 @@
     while last_sum.left:
         token = ()
         if last_sum.left == 1:
-            token = (patch_grad, block_out, output_w_grad)
+            token = (patch_grad, block_out)
         last_sum.step(last_small, done=token)
     triple_w_grad, mixer_w_grad, late = settle(
         size, last_chunk, relative, last_sum.held, [(width, 3 * width), (width, width)]

time: 265 us -> 264 us (level)
  transfers between devices with their start and end apart: 36 -> 36, of which waited for: 15 -> 14; matrix products, arithmetic and copies ran while one was open for 0% -> 0% of each run, Pallas kernels for 33% -> 32%
where the time goes in v4:
time: 264 us; the launch traced here: 260 us
  Pallas kernels  119 us (45%)
  waiting for transfers between devices  67.8 us (26%)
  starting transfers between devices  64.9 us (25%)
  local copies, waits for them, and re-layouts  7.51 us (3%)
    ppermute x33, waiting for transfers between devices, xor_permute(): lax.ppermute(value, ('rows', 'band'), [(i, i ^ mask) for i in range(size)])  67.8 us
    ppermute x33, starting transfers between devices, xor_permute(): lax.ppermute(value, ('rows', 'band'), [(i, i ^ mask) for i in range(size)])  48.2 us
    pallas_call x2, Pallas kernels, attend(): pl.pallas_call(partial(attend_kernel, n, unit, low, nq, nk, chunk, width)...  31.6 us
    pallas_call x1, Pallas kernels, feed(): pl.pallas_call(partial(feed_kernel, units, n, chunk, width, size, valid i...  27.2 us
    pallas_call x1, Pallas kernels, whole_back(): pl.pallas_call(partial(whole_back_kernel, size, bool(begun)), grid=(PAIRS...  20.1 us
    all_to_all x3, starting transfers between devices, deal(): return lax.all_to_all(pieces, 'band', 0, 0, tiled=True)  16.8 us
    pallas_call x1, Pallas kernels, shared_back(): pl.pallas_call(partial(shared_back_kernel, nq, nk), grid=(PAIRS,), in_spe...  13.6 us
    pallas_call x1, Pallas kernels, finish(): pl.pallas_call(partial(finish_kernel, units, n, chunk, width, len(others)...  8.63 us
  transfers between devices with their start and end apart: 36, of which 14 were waited for; matrix products, arithmetic and copies ran while one was open for 0% of the time, Pallas kernels for 32%

profile of v4, /device:TPU:0, one launch (start us, length us, event | category | flops | bytes accessed | tf_op | source)
XLA Modules:
  0.0 260.2 jit_solution(12343158919821752513)
XLA Ops:
  2.6 1.3 pack.2
  3.9 3.0 %collective-permute-start = (bf16[6,32,384]{2,1,0:T(8,128)(2,1)S(1)}, bf16[6,32,384]{2,1,0:T(8,128)(2,1)S(1)}, u32[]{:S(2)}, u32[]{:S(2)}) collective-permute-start(bf16[6,32,384]{2,1,0:T(8,128)(2,1)S(1)} %get-tuple-element.122), channel_id=1, source_target_pairs={{0,1},{1,0},{2,3},{3,2},{4,5},{5,4},{6,7},{7,6},{8,9},{9,8},{10,11... | collective-permute-start | bytes 442376 | tf_op jit(solution)/shard_map/ppermute | solution.py:897
  6.9 1.6 collective-permute-start.1
  8.5 3.0 %collective-permute-start.3 = (bf16[6,32,384]{2,1,0:T(8,128)(2,1)S(1)}, bf16[6,32,384]{2,1,0:T(8,128)(2,1)S(1)}, u32[]{:S(2)}, u32[]{:S(2)}) collective-permute-start(bf16[6,32,384]{2,1,0:T(8,128)(2,1)S(1)} %get-tuple-element.125), channel_id=1, source_target_pairs={{0,4},{1,5},{2,6},{3,7},{4,0},{5,1},{6,2},{7,3},{8,12},{9,13},{10,... | collective-permute-start | bytes 442376 | tf_op jit(solution)/shard_map/ppermute | solution.py:897
  12.8 3.6 %collective-permute-start.5 = (bf16[6,32,384]{2,1,0:T(8,128)(2,1)S(1)}, bf16[6,32,384]{2,1,0:T(8,128)(2,1)S(1)}, u32[]{:S(2)}, u32[]{:S(2)}) collective-permute-start(bf16[6,32,384]{2,1,0:T(8,128)(2,1)S(1)} %get-tuple-element.127), channel_id=1, source_target_pairs={{0,6},{1,7},{2,4},{3,5},{4,2},{5,3},{6,0},{7,1},{8,14},{9,15},{10,... | collective-permute-start | bytes 442376 | tf_op jit(solution)/shard_map/ppermute | solution.py:897
  16.4 2.5 collective-permute-done.1.refs_2_
  19.8 1.3 copy-done.11
  21.1 1.9 pack.3
  23.0 1.4 prepare.1
  26.2 6.8 %collective-permute-done.4.refs_5_ = bf16[6,32,384]{2,1,0:T(8,128)(2,1)S(1)} collective-permute-done((bf16[6,32,384]{2,1,0:T(8,128)(2,1)S(1)}, bf16[6,32,384]{2,1,0:T(8,128)(2,1)S(1)}, u32[]{:S(2)}, u32[]{:S(2)}) %collective-permute-start.4) | collective-permute-done | bytes 147488 | tf_op jit(solution)/shard_map/ppermute | solution.py:897
  33.0 8.9 %all-to-all-start = ((bf16[8,6,32,384]{3,2,1,0:T(8,128)(2,1)}), bf16[8,6,32,384]{3,2,1,0:T(8,128)(2,1)S(1)}, u32[]{:S(2)}, u32[]{:S(2)}) async-start(bf16[8,6,32,384]{3,2,1,0:T(8,128)(2,1)} %pack.3), calls=%async_computation | async-start | bytes 2359296 | tf_op jit(solution)/shard_map/all_to_all | solution.py:1034
  42.1 2.1 collective-permute-start.7
  44.2 18.6 %attend.2 = (bf16[1024,384]{1,0:T(8,128)(2,1)}, bf16[384,1024]{1,0:T(8,128)(2,1)}, bf16[3,1024,128]{2,1,0:T(8,128)(2,1)}, bf16[3,1024,128]{2,1,0:T(8,128)(2,1)},...) custom-call(s32[1]{0:T(128)} %bitcast.1.me_ref, ...), custom_call_target="tpu_custom_call" | custom-call | bytes 300000 | tf_op jit(solution)/shard_map/attend/pallas_call | solution.py:341
  64.4 13.0 %attend.3 = (bf16[1024,384]{1,0:T(8,128)(2,1)}, bf16[384,1024]{1,0:T(8,128)(2,1)}, bf16[3,512,128]{2,1,0:T(8,128)(2,1)}, bf16[3,1024,128]{2,1,0:T(8,128)(2,1)}, ...) custom-call(s32[1]{0:T(128)} %bitcast.1.me_ref, ...), custom_call_target="tpu_custom_call" | custom-call | bytes 300000 | tf_op jit(solution)/shard_map/attend/pallas_call | solution.py:341
  78.4 27.2 %feed.1 = (bf16[8,6,32,384]{3,2,1,0:T(8,128)(2,1)}, f32[1536,384]{1,0:T(8,128)}, bf16[1536,384]{1,0:T(8,128)(2,1)}, bf16[1536,384]{1,0:T(8,128)(2,1)}, bf16[1536...) custom-call(s32[1]{0:T(128)} %bitcast.me_ref.refs_10_, ...), custom_call_target="tpu_custom_call" | custom-call | bytes 300000 | tf_op jit(solution)/shard_map/feed/pallas_call | solution.py:690
  105.6 4.0 %all-to-all-start.1 = ((bf16[8,6,32,384]{3,2,1,0:T(8,128)(2,1)}), bf16[8,6,32,384]{3,2,1,0:T(8,128)(2,1)S(1)}, u32[]{:S(2)}, u32[]{:S(2)}) async-start(bf16[8,6,32,384]{3,2,1,0:T(8,128)(2,1)} %get-tuple-element.137), calls=%async_computation.1 | async-start | bytes 2359296 | tf_op jit(solution)/shard_map/all_to_all | solution.py:1034
  109.9 2.4 collective-permute-start.9
  112.4 13.6 %shared_back.1 = (f32[512,384]{1,0:T(8,128)}, bf16[512,384]{1,0:T(8,128)(2,1)}, f32[3,384,384]{2,1,0:T(8,128)}, f32[3,8,384]{2,1,0:T(8,128)}) custom-call(s32[2]{0:T(128)} %copy-done.18, bf16[6,1024,512]{2,1,0:T(8,128)(2,1)} %get-tuple-element.150.refs_0_, bf16[3,512,128]{2,1,0:T(8,128)(2,1)} %get-tuple-element.151.refs_1_, ...), custom_call_target="tpu_custom_call" | custom-call | bytes 300000 | tf_op jit(solution)/shard_map/shared_back/pallas_call | solution.py:500
  125.9 2.1 collective-permute-start.10
  128.3 20.1 %whole_back.1 = (bf16[3,1024,128]{2,1,0:T(8,128)(2,1)}, bf16[3,1024,128]{2,1,0:T(8,128)(2,1)}, bf16[3,1024,128]{2,1,0:T(8,128)(2,1)}, f32[3,8,384]{2,1,0:T(8,128...) custom-call(s32[2]{0:T(128)} %copy-done.18, bf16[6,1024,1024]{2,1,0:T(8,128)(2,1)} %get-tuple-element.138.refs_0_, ...), custom_call_target="tpu_custom_call" | custom-call | bytes 300000 | tf_op jit(solution)/shard_map/whole_back/pallas_call | solution.py:527
  148.4 2.1 collective-permute-start.12
  151.5 1.4 collective-permute-start.14
  153.7 8.6 %finish.1 = (bf16[8,6,32,384]{3,2,1,0:T(8,128)(2,1)}, bf16[32,384]{1,0:T(8,128)(2,1)}) custom-call(bf16[1024,384]{1,0:T(8,128)(2,1)} %get-tuple-element.130.refs_0_, bf16[1024,384]{1,0:T(8,128)(2,1)} %get-tuple-element.131.refs_1_, bf16[3,1024,128]{2,1,0:T(8,128)(2,1)} %get-tuple-element.167.refs_2_.refs_3_.refs_4_, ...), custom_call_target="tpu_custom_call" | custom-call | bytes 300000 | tf_op jit(solution)/shard_map/finish/pallas_call | solution.py:803
  162.4 3.8 %all-to-all-start.2 = ((bf16[8,6,32,384]{3,2,1,0:T(8,128)(2,1)}), bf16[8,6,32,384]{3,2,1,0:T(8,128)(2,1)S(1)}, u32[]{:S(2)}, u32[]{:S(2)}) async-start(bf16[8,6,32,384]{3,2,1,0:T(8,128)(2,1)} %get-tuple-element.187), calls=%async_computation.2 | async-start | bytes 2359296 | tf_op jit(solution)/shard_map/all_to_all | solution.py:1034
  166.3 2.2 collective-permute-done.18.refs_1_
  168.7 2.4 collective-permute-start.19
  171.1 7.3 %collective-permute-done.19.refs_1_ = bf16[384,384]{1,0:T(8,128)(2,1)S(1)} collective-permute-done((bf16[384,384]{1,0:T(8,128)(2,1)S(1)}, bf16[384,384]{1,0:T(8,128)(2,1)S(1)}, u32[]{:S(2)}, u32[]{:S(2)}) %collective-permute-start.19) | collective-permute-done | bytes 294944 | tf_op jit(solution)/shard_map/ppermute | solution.py:897
  178.5 2.0 collective-permute-start.20
  180.5 5.8 %collective-permute-done.20.refs_1_ = bf16[192,384]{1,0:T(8,128)(2,1)S(1)} collective-permute-done((bf16[192,384]{1,0:T(8,128)(2,1)S(1)}, bf16[192,384]{1,0:T(8,128)(2,1)S(1)}, u32[]{:S(2)}, u32[]{:S(2)}) %collective-permute-start.20) | collective-permute-done | bytes 147488 | tf_op jit(solution)/shard_map/ppermute | solution.py:897
  186.4 2.5 collective-permute-start.21
  188.8 2.0 collective-permute-start.22
  192.3 2.9 %collective-permute-start.16 = (bf16[144,384]{1,0:T(8,128)(2,1)S(1)}, bf16[144,384]{1,0:T(8,128)(2,1)S(1)}, u32[]{:S(2)}, u32[]{:S(2)}) collective-permute-start(bf16[144,384]{1,0:T(8,128)(2,1)S(1)} %pad_maximum_fusion.refs_0_), channel_id=1, source_target_pairs={{0,4},{1,5},{2,6},{3,7},{4,0},{5,1},{6,2},{7,3},{8,12},{9,13},{10,... | collective-permute-start | bytes 331784 | tf_op jit(solution)/shard_map/ppermute | solution.py:897
  195.2 2.4 collective-permute-start.17
  197.6 5.8 %collective-permute-done.22.refs_2_ = bf16[48,384]{1,0:T(8,128)(2,1)S(1)} collective-permute-done((bf16[48,384]{1,0:T(8,128)(2,1)S(1)}, bf16[48,384]{1,0:T(8,128)(2,1)S(1)}, u32[]{:S(2)}, u32[]{:S(2)}) %collective-permute-start.22) | collective-permute-done | bytes 36896 | tf_op jit(solution)/shard_map/ppermute | solution.py:897
  203.4 2.6 collective-permute-done.16.refs_2_
  207.3 1.9 collective-permute-start.25
  209.2 2.5 collective-permute-start.27
  212.1 3.7 %collective-permute-done.26.refs_2_ = bf16[80,384]{1,0:T(8,128)(2,1)S(1)} collective-permute-done((bf16[80,384]{1,0:T(8,128)(2,1)S(1)}, bf16[80,384]{1,0:T(8,128)(2,1)S(1)}, u32[]{:S(2)}, u32[]{:S(2)}) %collective-permute-start.26) | collective-permute-done | bytes 61472 | tf_op jit(solution)/shard_map/ppermute | solution.py:897
  216.0 1.7 collective-permute-start.29
  217.7 4.6 %collective-permute-done.29.refs_1_ = bf16[320,384]{1,0:T(8,128)(2,1)S(1)} collective-permute-done((bf16[320,384]{1,0:T(8,128)(2,1)S(1)}, bf16[320,384]{1,0:T(8,128)(2,1)S(1)}, u32[]{:S(2)}, u32[]{:S(2)}) %collective-permute-start.29) | collective-permute-done | bytes 245792 | tf_op jit(solution)/shard_map/ppermute | solution.py:897
  222.3 13.5 %collective-permute-done.28.refs_1_ = bf16[1152,384]{1,0:T(8,128)(2,1)S(1)} collective-permute-done((bf16[1152,384]{1,0:T(8,128)(2,1)S(1)}, bf16[1152,384]{1,0:T(8,128)(2,1)S(1)}, u32[]{:S(2)}, u32[]{:S(2)}) %collective-permute-start.28) | collective-permute-done | bytes 884768 | tf_op jit(solution)/shard_map/ppermute | solution.py:897
  236.4 1.9 unpack.2
  238.2 2.2 unpack.3
  240.5 9.2 %collective-permute-done.31.refs_1_ = bf16[640,384]{1,0:T(8,128)(2,1)S(1)} collective-permute-done((bf16[640,384]{1,0:T(8,128)(2,1)S(1)}, bf16[640,384]{1,0:T(8,128)(2,1)S(1)}, u32[]{:S(2)}, u32[]{:S(2)}) %collective-permute-start.31) | collective-permute-done | bytes 491552 | tf_op jit(solution)/shard_map/ppermute | solution.py:897
  249.8 2.6 collective-permute-done.32.refs_1_
  252.4 2.0 settle.3
  254.4 3.0 %settle.2 = (f32[1536,384]{1,0:T(8,128)}, f32[384,1536]{1,0:T(8,128)}, f32[32,48,384]{2,1,0:T(8,128)S(1)}) custom-call(s32[1]{0:T(128)} %bitcast.me_ref.refs_10_, bf16[2304,384]{1,0:T(8,128)(2,1)S(1)} %join.10.refs_0_, bf16[2304,384]{1,0:T(8,128)(2,1)S(1)} %collective-permute-done.30.refs_1_), custom_call_target="tpu_custom_call" | custom-call | bytes 300000 | tf_op jit(solution)/shard_map/settle/pallas_call | solution.py:850
  257.4 2.6 modulate.1
  (107 shorter events, 15.6 us)
Async XLA Ops:
  0.6 22.4 %copy-start.19 = (bf16[2304]{0:T(1024)(128)(2,1)S(1)}, bf16[2304]{0:T(1024)(128)(2,1)}, u32[]{:S(2)}) copy-start(bf16[2304]{0:T(1024)(128)(2,1)} %bias_ref.1) | copy-start | bytes 13828
  2.6 20.4 %copy-start = (bf16[384,2304]{1,0:T(8,128)(2,1)S(1)}, bf16[384,2304]{1,0:T(8,128)(2,1)}, u32[]{:S(2)}) copy-start(bf16[384,2304]{1,0:T(8,128)(2,1)} %weight_ref.1) | copy-start | bytes 5308420
  3.9 38.0 %copy-start.1 = (bf16[6,32,384]{2,1,0:T(8,128)(2,1)}, bf16[6,32,384]{2,1,0:T(8,128)(2,1)S(1)}, u32[]{:S(2)}) copy-start(bf16[6,32,384]{2,1,0:T(8,128)(2,1)S(1)} %get-tuple-element.121.refs_0_) | copy-start | bytes 442372
  3.9 8.9 %collective-permute-start = (bf16[6,32,384]{2,1,0:T(8,128)(2,1)S(1)}, bf16[6,32,384]{2,1,0:T(8,128)(2,1)S(1)}, u32[]{:S(2)}, u32[]{:S(2)}) collective-permute-start(bf16[6,32,384]{2,1,0:T(8,128)(2,1)S(1)} %get-tuple-element.122), channel_id=1, source_target_pairs={{0,1},{1,0},{2,3},{3,2},{4,5},{5,4},{6,7},{7,6},{8,9},{9,8},{10,11... | collective-permute-start | bytes 442376 | tf_op jit(solution)/shard_map/ppermute | solution.py:897
  6.9 12.0 %collective-permute-start.1 = (bf16[6,32,384]{2,1,0:T(8,128)(2,1)S(1)}, bf16[6,32,384]{2,1,0:T(8,128)(2,1)S(1)}, u32[]{:S(2)}, u32[]{:S(2)}) collective-permute-start(bf16[6,32,384]{2,1,0:T(8,128)(2,1)S(1)} %get-tuple-element.123), channel_id=1, source_target_pairs={{0,2},{1,3},{2,0},{3,1},{4,6},{5,7},{6,4},{7,5},{8,10},{9,11},{10,... | collective-permute-start | bytes 442376 | tf_op jit(solution)/shard_map/ppermute | solution.py:897
  8.5 17.6 %collective-permute-start.2 = (bf16[6,32,384]{2,1,0:T(8,128)(2,1)S(1)}, bf16[6,32,384]{2,1,0:T(8,128)(2,1)S(1)}, u32[]{:S(2)}, u32[]{:S(2)}) collective-permute-start(bf16[6,32,384]{2,1,0:T(8,128)(2,1)S(1)} %get-tuple-element.124), channel_id=1, source_target_pairs={{0,3},{1,2},{2,1},{3,0},{4,7},{5,6},{6,5},{7,4},{8,11},{9,10},{10,... | collective-permute-start | bytes 442376 | tf_op jit(solution)/shard_map/ppermute | solution.py:897
  8.5 17.6 %collective-permute-start.3 = (bf16[6,32,384]{2,1,0:T(8,128)(2,1)S(1)}, bf16[6,32,384]{2,1,0:T(8,128)(2,1)S(1)}, u32[]{:S(2)}, u32[]{:S(2)}) collective-permute-start(bf16[6,32,384]{2,1,0:T(8,128)(2,1)S(1)} %get-tuple-element.125), channel_id=1, source_target_pairs={{0,4},{1,5},{2,6},{3,7},{4,0},{5,1},{6,2},{7,3},{8,12},{9,13},{10,... | collective-permute-start | bytes 442376 | tf_op jit(solution)/shard_map/ppermute | solution.py:897
  11.5 21.5 %collective-permute-start.4 = (bf16[6,32,384]{2,1,0:T(8,128)(2,1)S(1)}, bf16[6,32,384]{2,1,0:T(8,128)(2,1)S(1)}, u32[]{:S(2)}, u32[]{:S(2)}) collective-permute-start(bf16[6,32,384]{2,1,0:T(8,128)(2,1)S(1)} %get-tuple-element.126), channel_id=1, source_target_pairs={{0,5},{1,4},{2,7},{3,6},{4,1},{5,0},{6,3},{7,2},{8,13},{9,12},{10,... | collective-permute-start | bytes 442376 | tf_op jit(solution)/shard_map/ppermute | solution.py:897
  12.8 29.2 %copy-start.2 = (bf16[6,32,384]{2,1,0:T(8,128)(2,1)}, bf16[6,32,384]{2,1,0:T(8,128)(2,1)S(1)}, u32[]{:S(2)}) copy-start(bf16[6,32,384]{2,1,0:T(8,128)(2,1)S(1)} %collective-permute-done.refs_1_) | copy-start | bytes 442372
  12.8 20.2 %collective-permute-start.5 = (bf16[6,32,384]{2,1,0:T(8,128)(2,1)S(1)}, bf16[6,32,384]{2,1,0:T(8,128)(2,1)S(1)}, u32[]{:S(2)}, u32[]{:S(2)}) collective-permute-start(bf16[6,32,384]{2,1,0:T(8,128)(2,1)S(1)} %get-tuple-element.127), channel_id=1, source_target_pairs={{0,6},{1,7},{2,4},{3,5},{4,2},{5,3},{6,0},{7,1},{8,14},{9,15},{10,... | collective-permute-start | bytes 442376 | tf_op jit(solution)/shard_map/ppermute | solution.py:897
  18.9 23.1 %copy-start.3 = (bf16[6,32,384]{2,1,0:T(8,128)(2,1)}, bf16[6,32,384]{2,1,0:T(8,128)(2,1)S(1)}, u32[]{:S(2)}) copy-start(bf16[6,32,384]{2,1,0:T(8,128)(2,1)S(1)} %collective-permute-done.1.refs_2_) | copy-start | bytes 442372
  18.9 14.1 %collective-permute-start.6 = (bf16[6,32,384]{2,1,0:T(8,128)(2,1)S(1)}, bf16[6,32,384]{2,1,0:T(8,128)(2,1)S(1)}, u32[]{:S(2)}, u32[]{:S(2)}) collective-permute-start(bf16[6,32,384]{2,1,0:T(8,128)(2,1)S(1)} %get-tuple-element.128), channel_id=1, source_target_pairs={{0,7},{1,6},{2,5},{3,4},{4,3},{5,2},{6,1},{7,0},{8,15},{9,14},{10,... | collective-permute-start | bytes 442376 | tf_op jit(solution)/shard_map/ppermute | solution.py:897
  26.2 15.9 %copy-start.4 = (bf16[6,32,384]{2,1,0:T(8,128)(2,1)}, bf16[6,32,384]{2,1,0:T(8,128)(2,1)S(1)}, u32[]{:S(2)}) copy-start(bf16[6,32,384]{2,1,0:T(8,128)(2,1)S(1)} %collective-permute-done.2.refs_3_) | copy-start | bytes 442372
  26.2 15.9 %copy-start.5 = (bf16[6,32,384]{2,1,0:T(8,128)(2,1)}, bf16[6,32,384]{2,1,0:T(8,128)(2,1)S(1)}, u32[]{:S(2)}) copy-start(bf16[6,32,384]{2,1,0:T(8,128)(2,1)S(1)} %collective-permute-done.3.refs_4_) | copy-start | bytes 442372
  33.0 9.1 %copy-start.6 = (bf16[6,32,384]{2,1,0:T(8,128)(2,1)}, bf16[6,32,384]{2,1,0:T(8,128)(2,1)S(1)}, u32[]{:S(2)}) copy-start(bf16[6,32,384]{2,1,0:T(8,128)(2,1)S(1)} %collective-permute-done.4.refs_5_) | copy-start | bytes 442372
  33.0 9.1 %copy-start.7 = (bf16[6,32,384]{2,1,0:T(8,128)(2,1)}, bf16[6,32,384]{2,1,0:T(8,128)(2,1)S(1)}, u32[]{:S(2)}) copy-start(bf16[6,32,384]{2,1,0:T(8,128)(2,1)S(1)} %collective-permute-done.5.refs_6_) | copy-start | bytes 442372
  33.0 9.1 %copy-start.8 = (bf16[6,32,384]{2,1,0:T(8,128)(2,1)}, bf16[6,32,384]{2,1,0:T(8,128)(2,1)S(1)}, u32[]{:S(2)}) copy-start(bf16[6,32,384]{2,1,0:T(8,128)(2,1)S(1)} %collective-permute-done.6.refs_7_) | copy-start | bytes 442372
  33.0 44.4 %all-to-all-start = ((bf16[8,6,32,384]{3,2,1,0:T(8,128)(2,1)}), bf16[8,6,32,384]{3,2,1,0:T(8,128)(2,1)S(1)}, u32[]{:S(2)}, u32[]{:S(2)}) async-start(bf16[8,6,32,384]{3,2,1,0:T(8,128)(2,1)} %pack.3), calls=%async_computation | async-start | bytes 2359296 | tf_op jit(solution)/shard_map/all_to_all | solution.py:1034
  42.1 21.5 %collective-permute-start.7 = (bf16[512,384]{1,0:T(8,128)(2,1)S(1)}, bf16[512,384]{1,0:T(8,128)(2,1)S(1)}, u32[]{:S(2)}, u32[]{:S(2)}) collective-permute-start(bf16[512,384]{1,0:T(8,128)(2,1)S(1)} %collect.1), channel_id=1, source_target_pairs={{0,1},{1,0},{2,3},{3,2},{4,5},{5,4},{6,7},{7,6},{8,9},{9,8},{10,11... | collective-permute-start | bytes 1179656 | tf_op jit(solution)/shard_map/ppermute | solution.py:897
  105.6 4.1 %collective-permute-start.8 = (bf16[1536,384]{1,0:T(8,128)(2,1)}, bf16[1536,384]{1,0:T(8,128)(2,1)S(1)}, u32[]{:S(2)}, u32[]{:S(2)}) collective-permute-start(bf16[1536,384]{1,0:T(8,128)(2,1)} %get-tuple-element.146), channel_id=1, source_target_pairs={{0,8},{1,9},{2,10},{3,11},{4,12},{5,13},{6,14},{7,15},{8,0},{9,1},... | collective-permute-start | bytes 3538952 | tf_op jit(solution)/shard_map/ppermute | solution.py:897
  105.6 47.3 %all-to-all-start.1 = ((bf16[8,6,32,384]{3,2,1,0:T(8,128)(2,1)}), bf16[8,6,32,384]{3,2,1,0:T(8,128)(2,1)S(1)}, u32[]{:S(2)}, u32[]{:S(2)}) async-start(bf16[8,6,32,384]{3,2,1,0:T(8,128)(2,1)} %get-tuple-element.137), calls=%async_computation.1 | async-start | bytes 2359296 | tf_op jit(solution)/shard_map/all_to_all | solution.py:1034
  109.9 18.1 %collective-permute-start.9 = (bf16[768,384]{1,0:T(8,128)(2,1)S(1)}, bf16[768,384]{1,0:T(8,128)(2,1)S(1)}, u32[]{:S(2)}, u32[]{:S(2)}) collective-permute-start(bf16[768,384]{1,0:T(8,128)(2,1)S(1)} %get-tuple-element.148), channel_id=1, source_target_pairs={{0,16},{1,17},{2,18},{3,19},{4,20},{5,21},{6,22},{7,23},{8,24},{9,... | collective-permute-start | bytes 1769480 | tf_op jit(solution)/shard_map/ppermute | solution.py:897
  125.9 27.0 %collective-permute-start.10 = (bf16[512,384]{1,0:T(8,128)(2,1)}, bf16[512,384]{1,0:T(8,128)(2,1)S(1)}, u32[]{:S(2)}, u32[]{:S(2)}) collective-permute-start(bf16[512,384]{1,0:T(8,128)(2,1)} %get-tuple-element.170), channel_id=1, source_target_pairs={{0,1},{1,0},{2,3},{3,2},{4,5},{5,4},{6,7},{7,6},{8,9},{9,8},{10,11... | collective-permute-start | bytes 1179656 | tf_op jit(solution)/shard_map/ppermute | solution.py:897
  128.2 20.2 %collective-permute-start.11 = (bf16[384,384]{1,0:T(8,128)(2,1)S(1)}, bf16[384,384]{1,0:T(8,128)(2,1)S(1)}, u32[]{:S(2)}, u32[]{:S(2)}) collective-permute-start(bf16[384,384]{1,0:T(8,128)(2,1)S(1)} %get-tuple-element.161), channel_id=1, source_target_pairs={{0,1},{1,0},{2,3},{3,2},{4,5},{5,4},{6,7},{7,6},{8,9},{9,8},{10,11... | collective-permute-start | bytes 884744 | tf_op jit(solution)/shard_map/ppermute | solution.py:897
  148.4 13.9 %collective-permute-start.12 = (bf16[96,384]{1,0:T(8,128)(2,1)S(1)}, bf16[96,384]{1,0:T(8,128)(2,1)S(1)}, u32[]{:S(2)}, u32[]{:S(2)}) collective-permute-start(bf16[96,384]{1,0:T(8,128)(2,1)S(1)} %get-tuple-element.176), channel_id=1, source_target_pairs={{0,2},{1,3},{2,0},{3,1},{4,6},{5,7},{6,4},{7,5},{8,10},{9,11},{10,... | collective-permute-start | bytes 221192 | tf_op jit(solution)/shard_map/ppermute | solution.py:897
  150.5 11.9 %collective-permute-start.13 = (bf16[96,384]{1,0:T(8,128)(2,1)S(1)}, bf16[96,384]{1,0:T(8,128)(2,1)S(1)}, u32[]{:S(2)}, u32[]{:S(2)}) collective-permute-start(bf16[96,384]{1,0:T(8,128)(2,1)S(1)} %get-tuple-element.177), channel_id=1, source_target_pairs={{0,4},{1,5},{2,6},{3,7},{4,0},{5,1},{6,2},{7,3},{8,12},{9,13},{10,... | collective-permute-start | bytes 221192 | tf_op jit(solution)/shard_map/ppermute | solution.py:897
  151.5 10.9 %collective-permute-start.14 = (bf16[96,384]{1,0:T(8,128)(2,1)S(1)}, bf16[96,384]{1,0:T(8,128)(2,1)S(1)}, u32[]{:S(2)}, u32[]{:S(2)}) collective-permute-start(bf16[96,384]{1,0:T(8,128)(2,1)S(1)} %get-tuple-element.178), channel_id=1, source_target_pairs={{0,6},{1,7},{2,4},{3,5},{4,2},{5,3},{6,0},{7,1},{8,14},{9,15},{10,... | collective-permute-start | bytes 221192 | tf_op jit(solution)/shard_map/ppermute | solution.py:897
  162.4 40.9 %all-to-all-start.2 = ((bf16[8,6,32,384]{3,2,1,0:T(8,128)(2,1)}), bf16[8,6,32,384]{3,2,1,0:T(8,128)(2,1)S(1)}, u32[]{:S(2)}, u32[]{:S(2)}) async-start(bf16[8,6,32,384]{3,2,1,0:T(8,128)(2,1)} %get-tuple-element.187), calls=%async_computation.2 | async-start | bytes 2359296 | tf_op jit(solution)/shard_map/all_to_all | solution.py:1034
  166.2 37.2 %copy-start.25 = (bf16[32,384]{1,0:T(8,128)(2,1)S(1)}, bf16[32,384]{1,0:T(8,128)(2,1)}, u32[]{:S(2)}) copy-start(bf16[32,384]{1,0:T(8,128)(2,1)} %get-tuple-element.181) | copy-start | bytes 73732
  166.2 2.3 collective-permute-start.18
  168.7 9.7 %collective-permute-start.19 = (bf16[384,384]{1,0:T(8,128)(2,1)S(1)}, bf16[384,384]{1,0:T(8,128)(2,1)S(1)}, u32[]{:S(2)}, u32[]{:S(2)}) collective-permute-start(bf16[384,384]{1,0:T(8,128)(2,1)S(1)} %get-tuple-element.193), channel_id=1, source_target_pairs={{0,16},{1,17},{2,18},{3,19},{4,20},{5,21},{6,22},{7,23},{8,24},{9,... | collective-permute-start | bytes 884744 | tf_op jit(solution)/shard_map/ppermute | solution.py:897
  178.5 7.9 %collective-permute-start.20 = (bf16[192,384]{1,0:T(8,128)(2,1)S(1)}, bf16[192,384]{1,0:T(8,128)(2,1)S(1)}, u32[]{:S(2)}, u32[]{:S(2)}) collective-permute-start(bf16[192,384]{1,0:T(8,128)(2,1)S(1)} %get-tuple-element.195), channel_id=1, source_target_pairs={{0,1},{1,0},{2,3},{3,2},{4,5},{5,4},{6,7},{7,6},{8,9},{9,8},{10,11... | collective-permute-start | bytes 442376 | tf_op jit(solution)/shard_map/ppermute | solution.py:897
  186.4 8.8 %collective-permute-start.21 = (bf16[48,384]{1,0:T(8,128)(2,1)S(1)}, bf16[48,384]{1,0:T(8,128)(2,1)S(1)}, u32[]{:S(2)}, u32[]{:S(2)}) collective-permute-start(bf16[48,384]{1,0:T(8,128)(2,1)S(1)} %get-tuple-element.197), channel_id=1, source_target_pairs={{0,2},{1,3},{2,0},{3,1},{4,6},{5,7},{6,4},{7,5},{8,10},{9,11},{10,... | collective-permute-start | bytes 110600 | tf_op jit(solution)/shard_map/ppermute | solution.py:897
  188.8 14.5 %collective-permute-start.22 = (bf16[48,384]{1,0:T(8,128)(2,1)S(1)}, bf16[48,384]{1,0:T(8,128)(2,1)S(1)}, u32[]{:S(2)}, u32[]{:S(2)}) collective-permute-start(bf16[48,384]{1,0:T(8,128)(2,1)S(1)} %get-tuple-element.198), channel_id=1, source_target_pairs={{0,4},{1,5},{2,6},{3,7},{4,0},{5,1},{6,2},{7,3},{8,12},{9,13},{10,... | collective-permute-start | bytes 110600 | tf_op jit(solution)/shard_map/ppermute | solution.py:897
  190.8 12.6 %collective-permute-start.23 = (bf16[48,384]{1,0:T(8,128)(2,1)S(1)}, bf16[48,384]{1,0:T(8,128)(2,1)S(1)}, u32[]{:S(2)}, u32[]{:S(2)}) collective-permute-start(bf16[48,384]{1,0:T(8,128)(2,1)S(1)} %get-tuple-element.199), channel_id=1, source_target_pairs={{0,6},{1,7},{2,4},{3,5},{4,2},{5,3},{6,0},{7,1},{8,14},{9,15},{10,... | collective-permute-start | bytes 110600 | tf_op jit(solution)/shard_map/ppermute | solution.py:897
  191.3 12.1 %collective-permute-start.15 = (bf16[144,384]{1,0:T(8,128)(2,1)S(1)}, bf16[144,384]{1,0:T(8,128)(2,1)S(1)}, u32[]{:S(2)}, u32[]{:S(2)}) collective-permute-start(bf16[144,384]{1,0:T(8,128)(2,1)S(1)} %pad_maximum_fusion.refs_0_), channel_id=1, source_target_pairs={{0,2},{1,3},{2,0},{3,1},{4,6},{5,7},{6,4},{7,5},{8,10},{9,11},{10,... | collective-permute-start | bytes 331784 | tf_op jit(solution)/shard_map/ppermute | solution.py:897
  192.3 13.7 %collective-permute-start.16 = (bf16[144,384]{1,0:T(8,128)(2,1)S(1)}, bf16[144,384]{1,0:T(8,128)(2,1)S(1)}, u32[]{:S(2)}, u32[]{:S(2)}) collective-permute-start(bf16[144,384]{1,0:T(8,128)(2,1)S(1)} %pad_maximum_fusion.refs_0_), channel_id=1, source_target_pairs={{0,4},{1,5},{2,6},{3,7},{4,0},{5,1},{6,2},{7,3},{8,12},{9,13},{10,... | collective-permute-start | bytes 331784 | tf_op jit(solution)/shard_map/ppermute | solution.py:897
  195.2 10.8 %collective-permute-start.17 = (bf16[144,384]{1,0:T(8,128)(2,1)S(1)}, bf16[144,384]{1,0:T(8,128)(2,1)S(1)}, u32[]{:S(2)}, u32[]{:S(2)}) collective-permute-start(bf16[144,384]{1,0:T(8,128)(2,1)S(1)} %pad_maximum_fusion.refs_0_), channel_id=1, source_target_pairs={{0,6},{1,7},{2,4},{3,5},{4,2},{5,3},{6,0},{7,1},{8,14},{9,15},{10,... | collective-permute-start | bytes 331784 | tf_op jit(solution)/shard_map/ppermute | solution.py:897
  206.1 9.7 %collective-permute-start.24 = (bf16[576,384]{1,0:T(8,128)(2,1)S(1)}, bf16[576,384]{1,0:T(8,128)(2,1)S(1)}, u32[]{:S(2)}, u32[]{:S(2)}) collective-permute-start(bf16[576,384]{1,0:T(8,128)(2,1)S(1)} %join.6.refs_0_), channel_id=1, source_target_pairs={{0,1},{1,0},{2,3},{3,2},{4,5},{5,4},{6,7},{7,6},{8,9},{9,8},{10,11... | collective-permute-start | bytes 1327112 | tf_op jit(solution)/shard_map/ppermute | solution.py:897
  207.3 4.8 %collective-permute-start.25 = (bf16[80,384]{1,0:T(8,128)(2,1)S(1)}, bf16[80,384]{1,0:T(8,128)(2,1)S(1)}, u32[]{:S(2)}, u32[]{:S(2)}) collective-permute-start(bf16[80,384]{1,0:T(8,128)(2,1)S(1)} %pad_maximum_fusion.1.refs_0_), channel_id=1, source_target_pairs={{0,2},{1,3},{2,0},{3,1},{4,6},{5,7},{6,4},{7,5},{8,10},{9,11},{10,... | collective-permute-start | bytes 184328 | tf_op jit(solution)/shard_map/ppermute | solution.py:897
  209.2 6.6 %collective-permute-start.26 = (bf16[80,384]{1,0:T(8,128)(2,1)S(1)}, bf16[80,384]{1,0:T(8,128)(2,1)S(1)}, u32[]{:S(2)}, u32[]{:S(2)}) collective-permute-start(bf16[80,384]{1,0:T(8,128)(2,1)S(1)} %pad_maximum_fusion.1.refs_0_), channel_id=1, source_target_pairs={{0,4},{1,5},{2,6},{3,7},{4,0},{5,1},{6,2},{7,3},{8,12},{9,13},{10,... | collective-permute-start | bytes 184328 | tf_op jit(solution)/shard_map/ppermute | solution.py:897
  209.2 6.6 %collective-permute-start.27 = (bf16[80,384]{1,0:T(8,128)(2,1)S(1)}, bf16[80,384]{1,0:T(8,128)(2,1)S(1)}, u32[]{:S(2)}, u32[]{:S(2)}) collective-permute-start(bf16[80,384]{1,0:T(8,128)(2,1)S(1)} %pad_maximum_fusion.1.refs_0_), channel_id=1, source_target_pairs={{0,6},{1,7},{2,4},{3,5},{4,2},{5,3},{6,0},{7,1},{8,14},{9,15},{10,... | collective-permute-start | bytes 184328 | tf_op jit(solution)/shard_map/ppermute | solution.py:897
  215.9 19.9 %collective-permute-start.28 = (bf16[1152,384]{1,0:T(8,128)(2,1)S(1)}, bf16[1152,384]{1,0:T(8,128)(2,1)S(1)}, u32[]{:S(2)}, u32[]{:S(2)}) collective-permute-start(bf16[1152,384]{1,0:T(8,128)(2,1)S(1)} %join.8.refs_0_), channel_id=1, source_target_pairs={{0,16},{1,17},{2,18},{3,19},{4,20},{5,21},{6,22},{7,23},{8,24},{9,... | collective-permute-start | bytes 2654216 | tf_op jit(solution)/shard_map/ppermute | solution.py:897
  216.0 6.3 %collective-permute-start.29 = (bf16[320,384]{1,0:T(8,128)(2,1)S(1)}, bf16[320,384]{1,0:T(8,128)(2,1)S(1)}, u32[]{:S(2)}, u32[]{:S(2)}) collective-permute-start(bf16[320,384]{1,0:T(8,128)(2,1)S(1)} %join.7.refs_0_), channel_id=1, source_target_pairs={{0,1},{1,0},{2,3},{3,2},{4,5},{5,4},{6,7},{7,6},{8,9},{9,8},{10,11... | collective-permute-start | bytes 737288 | tf_op jit(solution)/shard_map/ppermute | solution.py:897
  222.3 14.1 %copy-start.15 = (s32[6,8]{1,0:T(8,128)S(1)}, s32[6,8]{1,0:T(8,128)}, u32[]{:S(2)}) copy-start(s32[6,8]{1,0:T(8,128)} %lens_ref.9) | copy-start | bytes 580
  236.0 18.4 %collective-permute-start.30 = (bf16[2304,384]{1,0:T(8,128)(2,1)S(1)}, bf16[2304,384]{1,0:T(8,128)(2,1)S(1)}, u32[]{:S(2)}, u32[]{:S(2)}) collective-permute-start(bf16[2304,384]{1,0:T(8,128)(2,1)S(1)} %join.10.refs_0_), channel_id=1, source_target_pairs={{0,8},{1,9},{2,10},{3,11},{4,12},{5,13},{6,14},{7,15},{8,0},{9,1},... | collective-permute-start | bytes 5308424 | tf_op jit(solution)/shard_map/ppermute | solution.py:897
  236.0 13.6 %collective-permute-start.31 = (bf16[640,384]{1,0:T(8,128)(2,1)S(1)}, bf16[640,384]{1,0:T(8,128)(2,1)S(1)}, u32[]{:S(2)}, u32[]{:S(2)}) collective-permute-start(bf16[640,384]{1,0:T(8,128)(2,1)S(1)} %join.9.refs_0_), channel_id=1, source_target_pairs={{0,16},{1,17},{2,18},{3,19},{4,20},{5,21},{6,22},{7,23},{8,24},{9,... | collective-permute-start | bytes 1474568 | tf_op jit(solution)/shard_map/ppermute | solution.py:897
  249.8 2.6 %collective-permute-start.32 = (bf16[1280,384]{1,0:T(8,128)(2,1)S(1)}, bf16[1280,384]{1,0:T(8,128)(2,1)S(1)}, u32[]{:S(2)}, u32[]{:S(2)}) collective-permute-start(bf16[1280,384]{1,0:T(8,128)(2,1)S(1)} %join.11.refs_0_), channel_id=1, source_target_pairs={{0,8},{1,9},{2,10},{3,11},{4,12},{5,13},{6,14},{7,15},{8,0},{9,1},... | collective-permute-start | bytes 2949128 | tf_op jit(solution)/shard_map/ppermute | solution.py:897
  (14 other events, 30.3 us)
